TPU v7x, 512 devices: a whole 4x8x8 slice. The times are simulated.
512 devices in a mesh: blk: 128 (over x, y_lo, z), head: 4 (over y_hi, core).
Axes of the slice: x: 4, y: 8 (y_hi: 2, y_lo: 4; y = y_hi * 4 + y_lo), z: 8, core: 2. Of those that a mesh axis runs over, the one named last changes fastest.
Arguments:
- queries: bfloat16 [65536, 2048], P(('blk', 'head')), may hold values from -32 to 32
- keys: bfloat16 [65536, 512], P(('blk', 'head')), may hold values from -32 to 32
- values: bfloat16 [65536, 512], P(('blk', 'head')), may hold values from -6 to 6
- frame_of: int32 [512], replicated, may hold values from 0 to 511, each once
- counts: int32 [512], replicated, may hold values from 64 to 128
Outputs:
- attended: bfloat16 [65536, 2048], P(('blk', 'head'))
Inputs may be any that keep to these rules, and one draw needn't show every extreme that they name: `frame_of`: every value from 0 to 511 appears once.
All inputs are finite; a program needn't handle non-finite values.
Results may differ from a plain program's by a relative error of at most 0.006.
Values may be sent and summed in bfloat16 or wider, within the bound.
No kernel may reach another device: no remote copies, remote signals or barrier semaphores. Data moves between devices by JAX's collectives and lax.ppermute only.
A program may use at most 64 MiB of HBM per device.

v0:
```python
import jax
import jax.numpy as jnp
from jax import lax
from jax.sharding import PartitionSpec as P

HEAD_DIM = 128
FRAME_TOK = 128
CYCLE = 4


NEGATIVE = -1e30


def passed_along(value, axis, steps):
    count = lax.axis_size(axis)
    pairs = [(source, (source + steps) % count) for source in range(count)]
    return lax.ppermute(value, axis, pairs)


def visible(query_pos, query_tok, key_pos, key_tok, key_count):
    earlier = key_pos[None, :] < query_pos[:, None]
    same_frame = (key_pos[None, :] == query_pos[:, None]) & (key_tok[None, :] <= query_tok[:, None])
    return (earlier | same_frame) & (key_tok < key_count)[None, :]


def frame_rows(table, start, number):
    return jnp.repeat(lax.dynamic_slice_in_dim(table, start, number), FRAME_TOK)


def absorb(carry_state, queries, keys, values, allowed):
    running_max, running_sum, weighted = carry_state
    scores = jnp.einsum(
        "rcge,kce->cgrk", queries, keys, preferred_element_type=jnp.float32
    ) * HEAD_DIM ** (-0.5)
    masked = jnp.where(allowed[None, None], scores, NEGATIVE)
    new_max = jnp.maximum(running_max, jnp.max(masked, axis=-1))
    weights = jnp.where(allowed[None, None], jnp.exp(masked - new_max[..., None]), 0.0)
    shrink = jnp.exp(running_max - new_max)
    running_sum = running_sum * shrink + jnp.sum(weights, axis=-1)
    rounded = weights.astype(jnp.bfloat16)
    weighted = weighted * shrink[..., None] + jnp.einsum(
        "cgrk,kce->cgre", rounded, values, preferred_element_type=jnp.float32
    )
    return (new_max, running_sum, weighted)


def circulate(first, second):
    blocks = [(first, second)]
    for offset in range(1, CYCLE):
        prior = blocks[-1]
        blocks.append(passed_along((prior[0], prior[1]), "blk", 1))
    return blocks


def attend_window(
    local_queries, blocks, query_pos, frame_of, counts, group_index, group_frames, group_count
):
    row_count, kv_heads, group_size = (
        local_queries.shape[0],
        local_queries.shape[1],
        local_queries.shape[2],
    )
    key_rows = blocks[0][0].shape[0]
    query_tok = jnp.arange(row_count, dtype=jnp.int32) % FRAME_TOK
    key_tok = jnp.arange(key_rows, dtype=jnp.int32) % FRAME_TOK
    carry_state = (
        jnp.full((kv_heads, group_size, row_count), NEGATIVE, jnp.float32),
        jnp.zeros((kv_heads, group_size, row_count), jnp.float32),
        jnp.zeros((kv_heads, group_size, row_count, HEAD_DIM), jnp.float32),
    )
    for offset in range(CYCLE):
        source = (group_index - offset) % group_count
        key_pos = frame_rows(frame_of, source * group_frames, group_frames)
        key_count = frame_rows(counts, source * group_frames, group_frames)
        block_keys = blocks[offset][0].reshape(key_rows, kv_heads, HEAD_DIM)
        block_values = blocks[offset][1].reshape(key_rows, kv_heads, HEAD_DIM)
        allowed = visible(query_pos, query_tok, key_pos, key_tok, key_count)
        carry_state = absorb(carry_state, local_queries, block_keys, block_values, allowed)
    running_max, running_sum, weighted = carry_state
    attended = weighted / running_sum[..., None]
    return (
        attended.transpose(2, 0, 1, 3)
        .reshape(row_count, kv_heads * group_size * HEAD_DIM)
        .astype(jnp.bfloat16)
    )


def on_device(queries, keys, values, frame_of, counts):
    head_count = lax.axis_size("head")
    group_count = lax.axis_size("blk")
    frames_dev = queries.shape[0] // FRAME_TOK
    group_frames = frames_dev * head_count
    kv_heads = keys.shape[1] // HEAD_DIM
    group_size = queries.shape[1] // HEAD_DIM // kv_heads
    group_index = lax.axis_index("blk")
    spread_q, spread_k, spread_v = (
        lax.all_to_all(queries, "head", split_axis=1, concat_axis=0, tiled=True),
        lax.all_to_all(keys, "head", split_axis=1, concat_axis=0, tiled=True),
        lax.all_to_all(values, "head", split_axis=1, concat_axis=0, tiled=True),
    )
    row_count = spread_q.shape[0]
    local_kv = spread_k.shape[1] // HEAD_DIM
    local_queries = spread_q.reshape(row_count, local_kv, group_size, HEAD_DIM)
    blocks = circulate(spread_k, spread_v)
    query_pos = frame_rows(frame_of, group_index * group_frames, group_frames)
    result = attend_window(
        local_queries, blocks, query_pos, frame_of, counts, group_index, group_frames, group_count
    )
    return lax.all_to_all(result, "head", split_axis=0, concat_axis=1, tiled=True)


def solution(mesh):
    in_specs = (
        P(("blk", "head"), None),
        P(("blk", "head"), None),
        P(("blk", "head"), None),
        P(),
        P(),
    )
    out_specs = P(("blk", "head"), None)
    return jax.shard_map(
        on_device, mesh=mesh, in_specs=in_specs, out_specs=out_specs, check_vma=False
    )
```

profile of v0, /device:TPU:1, one launch (start us, length us, event | category | flops | bytes accessed | tf_op | source)
XLA Modules:
  0.0 117.4 jit_solution(1782881195675065086)
XLA Ops:
  0.0 0.9 copy-done
  0.9 0.7 copy_bitcast_fusion.2
  1.6 10.2 %all-to-all-start = ((bf16[128,4,128]{2,0,1:T(8,128)(2,1)}), bf16[128,4,128]{2,0,1:T(8,128)(2,1)S(1)}, u32[]{:S(2)}, u32[]{:S(2)}) async-start(bf16[128,4,128]{2,0,1:T(8,128)(2,1)} %copy_bitcast_fusion.2), calls=%async_computation | async-start | bytes 262144 | tf_op jit(solution)/shard_map/all_to_all | solution.py:98
  11.7 0.9 fusion.94
  12.7 0.1 broadcast_bitcast_fusion
  12.8 0.1 broadcast_bitcast_fusion.1
  12.8 0.1 broadcast_bitcast_fusion.2
  12.9 0.1 broadcast_bitcast_fusion.3
  13.0 1.9 %copy.64 = bf16[16,4,8,512]{3,2,0,1:T(8,128)(2,1)} copy(bf16[16,4,8,512]{3,2,1,0:T(8,128)(2,1)} %bitcast.190) | data formatting | bytes 1048576 | tf_op jit(solution)/shard_map/all_to_all | solution.py:97
  14.9 1.6 %copy_bitcast_fusion.1 = bf16[128,4,128]{2,0,1:T(8,128)(2,1)} fusion(bf16[128,512]{1,0:T(8,128)(2,1)} %param.7), kind=kLoop, calls=%fused_computation.62 | loop fusion | bytes 262144 | tf_op jit(solution)/shard_map/all_to_all | solution.py:99
  16.5 0.1 bitcast_compare_fusion
  16.6 2.7 %all-to-all-done = bf16[128,4,128]{2,0,1:T(8,128)(2,1)S(1)} async-done(((bf16[128,4,128]{2,0,1:T(8,128)(2,1)}), bf16[128,4,128]{2,0,1:T(8,128)(2,1)S(1)}, u32[]{:S(2)}, u32[]{:S(2)}) %all-to-all-start) | async-done | bytes 131104 | tf_op jit(solution)/shard_map/all_to_all | solution.py:98
  19.3 4.5 %all-to-all-start.2 = ((bf16[128,4,128]{2,0,1:T(8,128)(2,1)}), bf16[128,4,128]{2,0,1:T(8,128)(2,1)S(1)}, u32[]{:S(2)}, u32[]{:S(2)}) async-start(bf16[128,4,128]{2,0,1:T(8,128)(2,1)} %copy_bitcast_fusion.1), calls=%async_computation.2 | async-start | bytes 262144 | tf_op jit(solution)/shard_map/all_to_all | solution.py:99
  23.8 0.1 bitcast_compare_fusion.1
  23.8 7.4 %all-to-all-done.2 = bf16[128,4,128]{2,0,1:T(8,128)(2,1)S(1)} async-done(((bf16[128,4,128]{2,0,1:T(8,128)(2,1)}), bf16[128,4,128]{2,0,1:T(8,128)(2,1)S(1)}, u32[]{:S(2)}, u32[]{:S(2)}) %all-to-all-start.2) | async-done | bytes 131104 | tf_op jit(solution)/shard_map/all_to_all | solution.py:99
  31.3 4.5 %all-to-all-start.1 = ((bf16[128,4,512]{2,0,1:T(8,128)(2,1)}), bf16[128,4,512]{2,0,1:T(8,128)(2,1)S(1)}, u32[]{:S(2)}, u32[]{:S(2)}) async-start(bf16[128,4,512]{2,0,1:T(8,128)(2,1)} %bitcast.184), calls=%async_computation.1 | async-start | bytes 1048576 | tf_op jit(solution)/shard_map/all_to_all | solution.py:97
  35.8 0.1 bitcast_compare_fusion.2
  35.8 2.4 %collective-permute-start = (bf16[512,128]{1,0:T(8,128)(2,1)S(1)}, bf16[512,128]{1,0:T(8,128)(2,1)S(1)}, u32[]{:S(2)}, u32[]{:S(2)}) collective-permute-start(bf16[512,128]{1,0:T(8,128)(2,1)S(1)} %bitcast.188), channel_id=1, source_target_pairs={{0,4},{4,8},{8,12},{12,16},{16,20},{20,24},{24,28},{28,32},{32,36}... | collective-permute-start | bytes 393224 | tf_op jit(solution)/shard_map/ppermute | solution.py:17
  38.3 4.0 %collective-permute-start.1 = (bf16[512,128]{1,0:T(8,128)(2,1)S(1)}, bf16[512,128]{1,0:T(8,128)(2,1)S(1)}, u32[]{:S(2)}, u32[]{:S(2)}) collective-permute-start(bf16[512,128]{1,0:T(8,128)(2,1)S(1)} %bitcast.191), channel_id=1, source_target_pairs={{0,4},{4,8},{8,12},{12,16},{16,20},{20,24},{24,28},{28,32},{32,36}... | collective-permute-start | bytes 393224 | tf_op jit(solution)/shard_map/ppermute | solution.py:17
  42.3 0.1 bitcast_compare_fusion.3
  42.3 14.4 %collective-permute-done = bf16[512,128]{1,0:T(8,128)(2,1)S(1)} collective-permute-done((bf16[512,128]{1,0:T(8,128)(2,1)S(1)}, bf16[512,128]{1,0:T(8,128)(2,1)S(1)}, u32[]{:S(2)}, u32[]{:S(2)}) %collective-permute-start) | collective-permute-done | bytes 131104 | tf_op jit(solution)/shard_map/ppermute | solution.py:17
  56.8 1.9 %collective-permute-start.2 = (bf16[512,128]{1,0:T(8,128)(2,1)S(1)}, bf16[512,128]{1,0:T(8,128)(2,1)S(1)}, u32[]{:S(2)}, u32[]{:S(2)}) collective-permute-start(bf16[512,128]{1,0:T(8,128)(2,1)S(1)} %collective-permute-done), channel_id=1, source_target_pairs={{0,4},{4,8},{8,12},{12,16},{16,20},{20,24},{24,28},{28,32},{32,36}... | collective-permute-start | bytes 393224 | tf_op jit(solution)/shard_map/ppermute | solution.py:17
  58.7 1.0 collective-permute-done.1
  59.7 1.9 %collective-permute-start.3 = (bf16[512,128]{1,0:T(8,128)(2,1)S(1)}, bf16[512,128]{1,0:T(8,128)(2,1)S(1)}, u32[]{:S(2)}, u32[]{:S(2)}) collective-permute-start(bf16[512,128]{1,0:T(8,128)(2,1)S(1)} %collective-permute-done.1), channel_id=1, source_target_pairs={{0,4},{4,8},{8,12},{12,16},{16,20},{20,24},{24,28},{28,32},{32,36}... | collective-permute-start | bytes 393224 | tf_op jit(solution)/shard_map/ppermute | solution.py:17
  61.6 1.7 %fusion.52 = (pred[512,512]{0,1:T(8,128)(4,1)S(1)}, pred[512,512]{0,1:T(8,128)(4,1)S(1)}, pred[512,512]{0,1:T(8,128)(4,1)S(1)}, pred[512,512]{0,1:T(8,128)(4,1)S(1)}) fusion(s32[512]{0:T(512)S(1)} %add_select_fusion, s32[512]{0:T(512)S(1)} %broadcast_bitcast_fusion.3, s32[512]{0:T(512)S(1)} %broadcast_bitcast_fusion.2, ...), kind=kLoop, calls=%fused_computation.47 | loop fusion | flops 5505024 | bytes 1062912 | tf_op jit(solution)/shard_map/and | solution.py:23
  63.3 9.5 %collective-permute-done.2 = bf16[512,128]{1,0:T(8,128)(2,1)S(1)} collective-permute-done((bf16[512,128]{1,0:T(8,128)(2,1)S(1)}, bf16[512,128]{1,0:T(8,128)(2,1)S(1)}, u32[]{:S(2)}, u32[]{:S(2)}) %collective-permute-start.2) | collective-permute-done | bytes 131104 | tf_op jit(solution)/shard_map/ppermute | solution.py:17
  72.8 1.9 %collective-permute-start.4 = (bf16[512,128]{1,0:T(8,128)(2,1)S(1)}, bf16[512,128]{1,0:T(8,128)(2,1)S(1)}, u32[]{:S(2)}, u32[]{:S(2)}) collective-permute-start(bf16[512,128]{1,0:T(8,128)(2,1)S(1)} %collective-permute-done.2), channel_id=1, source_target_pairs={{0,4},{4,8},{8,12},{12,16},{16,20},{20,24},{24,28},{28,32},{32,36}... | collective-permute-start | bytes 393224 | tf_op jit(solution)/shard_map/ppermute | solution.py:17
  74.8 0.9 collective-permute-done.3
  75.6 1.9 %collective-permute-start.5 = (bf16[512,128]{1,0:T(8,128)(2,1)S(1)}, bf16[512,128]{1,0:T(8,128)(2,1)S(1)}, u32[]{:S(2)}, u32[]{:S(2)}) collective-permute-start(bf16[512,128]{1,0:T(8,128)(2,1)S(1)} %collective-permute-done.3), channel_id=1, source_target_pairs={{0,4},{4,8},{8,12},{12,16},{16,20},{20,24},{24,28},{28,32},{32,36}... | collective-permute-start | bytes 393224 | tf_op jit(solution)/shard_map/ppermute | solution.py:17
  77.6 0.1 reshape.749
  77.7 0.9 fusion
  78.6 0.9 fusion.2
  79.5 0.9 fusion.1
  80.4 4.8 %collective-permute-done.4 = bf16[512,128]{1,0:T(8,128)(2,1)S(1)} collective-permute-done((bf16[512,128]{1,0:T(8,128)(2,1)S(1)}, bf16[512,128]{1,0:T(8,128)(2,1)S(1)}, u32[]{:S(2)}, u32[]{:S(2)}) %collective-permute-start.4) | collective-permute-done | bytes 131104 | tf_op jit(solution)/shard_map/ppermute | solution.py:17
  85.2 0.9 fusion.3
  86.1 1.1 fusion.4
  87.2 1.0 fusion.6
  88.2 1.1 fusion.8
  89.3 1.0 fusion.10
  90.4 2.1 %fusion.46 = f32[4,512,128]{2,1,0:T(8,128)S(1)} fusion(bf16[512,128,1]{1,0,2:T(8,128)(2,1)S(1)} %bitcast.192, f32[512,512,4]{1,0,2:T(8,128)S(1)} %get-tuple-element.34, f32[4,512]{1,0:T(4,128)S(1)} %get-tuple-element.13, pred[512,512]{0,1:T(8,128)(4,1)S(1)} %get-tuple-element.16, f32[4,512]{1,0:T(4,128)S(1)} %get-tuple-element.8, ...), kind=kOutput, calls=%fused_computation.42 | convolution fusion | flops 274202624 | bytes 5660672 | tf_op jit(solution)/shard_map/cgrk,kce->cgre/dot_general | solution.py:41
  92.4 1.6 %fusion.40 = f32[4,512,128]{2,1,0:T(8,128)S(1)} fusion(f32[4,512,128]{2,1,0:T(8,128)S(1)} %fusion.46, f32[512,512,4]{1,0,2:T(8,128)S(1)} %get-tuple-element.32, f32[4,512]{1,0:T(4,128)S(1)} %get-tuple-element.11, pred[512,512]{0,1:T(8,128)(4,1)S(1)} %get-tuple-element.14, f32[4,512]{1,0:T(4,128)S(1)} %get-tuple-element.7, ...), kind=kOutput, calls=%fused_computation.40 | convolution fusion | flops 274202624 | bytes 6701056 | tf_op jit(solution)/shard_map/cgrk,kce->cgre/dot_general | solution.py:41
  94.1 1.7 %fusion.34 = f32[4,512,128]{2,1,0:T(8,128)S(1)} fusion(f32[4,512,128]{2,1,0:T(8,128)S(1)} %fusion.40, f32[512,512,4]{1,0,2:T(8,128)S(1)} %get-tuple-element.30, f32[4,512]{1,0:T(4,128)S(1)} %get-tuple-element.10, pred[512,512]{0,1:T(8,128)(4,1)S(1)} %get-tuple-element.15, f32[4,512]{1,0:T(4,128)S(1)} %get-tuple-element.6, ...), kind=kOutput, calls=%fused_computation.38 | convolution fusion | flops 274202624 | bytes 6701056 | tf_op jit(solution)/shard_map/cgrk,kce->cgre/dot_general | solution.py:41
  95.8 1.7 %fusion.59 = bf16[512,1,4,128]{3,0,2,1:T(8,128)(2,1)S(1)} fusion(f32[4,512,128]{2,1,0:T(8,128)S(1)} %fusion.34, f32[512,512,4]{1,0,2:T(8,128)S(1)} %get-tuple-element.28, f32[4,512]{1,0:T(4,128)S(1)} %get-tuple-element.9, pred[512,512]{0,1:T(8,128)(4,1)S(1)} %get-tuple-element.17, f32[4,512]{1,0:T(4,128)S(1)} %get-tuple-element.5, ...), kind=kOutput, calls=%fused_computation.52 | convolution fusion | flops 274464768 | bytes 6176768 | tf_op jit(solution)/shard_map/cgrk,kce->cgre/dot_general | solution.py:41
  97.4 0.4 copy.35
  97.8 0.2 convert_element_type.32
  98.0 18.0 %all_to_all.64 = bf16[4,128,512]{2,1,0:T(8,128)(2,1)S(1)} all-to-all(bf16[4,128,512]{2,1,0:T(8,128)(2,1)S(1)} %convert_element_type.32), channel_id=1, replica_groups=mesh['blk'=128,'head'=4] {'head'}, dimensions={0} | all-to-all | bytes 1048576 | tf_op jit(solution)/shard_map/all_to_all | solution.py:109
  116.1 0.3 copy.36
  116.4 1.0 copy.37
  (7 shorter events, 0.1 us)
Async XLA Ops:
  0.0 0.9 copy-start
  1.6 17.7 %all-to-all-start = ((bf16[128,4,128]{2,0,1:T(8,128)(2,1)}), bf16[128,4,128]{2,0,1:T(8,128)(2,1)S(1)}, u32[]{:S(2)}, u32[]{:S(2)}) async-start(bf16[128,4,128]{2,0,1:T(8,128)(2,1)} %copy_bitcast_fusion.2), calls=%async_computation | async-start | bytes 262144 | tf_op jit(solution)/shard_map/all_to_all | solution.py:98
  19.3 12.0 %all-to-all-start.2 = ((bf16[128,4,128]{2,0,1:T(8,128)(2,1)}), bf16[128,4,128]{2,0,1:T(8,128)(2,1)S(1)}, u32[]{:S(2)}, u32[]{:S(2)}) async-start(bf16[128,4,128]{2,0,1:T(8,128)(2,1)} %copy_bitcast_fusion.1), calls=%async_computation.2 | async-start | bytes 262144 | tf_op jit(solution)/shard_map/all_to_all | solution.py:99
  31.3 46.3 %all-to-all-start.1 = ((bf16[128,4,512]{2,0,1:T(8,128)(2,1)}), bf16[128,4,512]{2,0,1:T(8,128)(2,1)S(1)}, u32[]{:S(2)}, u32[]{:S(2)}) async-start(bf16[128,4,512]{2,0,1:T(8,128)(2,1)} %bitcast.184), calls=%async_computation.1 | async-start | bytes 1048576 | tf_op jit(solution)/shard_map/all_to_all | solution.py:97
  35.8 20.9 %collective-permute-start = (bf16[512,128]{1,0:T(8,128)(2,1)S(1)}, bf16[512,128]{1,0:T(8,128)(2,1)S(1)}, u32[]{:S(2)}, u32[]{:S(2)}) collective-permute-start(bf16[512,128]{1,0:T(8,128)(2,1)S(1)} %bitcast.188), channel_id=1, source_target_pairs={{0,4},{4,8},{8,12},{12,16},{16,20},{20,24},{24,28},{28,32},{32,36}... | collective-permute-start | bytes 393224 | tf_op jit(solution)/shard_map/ppermute | solution.py:17
  38.3 21.4 %collective-permute-start.1 = (bf16[512,128]{1,0:T(8,128)(2,1)S(1)}, bf16[512,128]{1,0:T(8,128)(2,1)S(1)}, u32[]{:S(2)}, u32[]{:S(2)}) collective-permute-start(bf16[512,128]{1,0:T(8,128)(2,1)S(1)} %bitcast.191), channel_id=1, source_target_pairs={{0,4},{4,8},{8,12},{12,16},{16,20},{20,24},{24,28},{28,32},{32,36}... | collective-permute-start | bytes 393224 | tf_op jit(solution)/shard_map/ppermute | solution.py:17
  56.8 16.1 %collective-permute-start.2 = (bf16[512,128]{1,0:T(8,128)(2,1)S(1)}, bf16[512,128]{1,0:T(8,128)(2,1)S(1)}, u32[]{:S(2)}, u32[]{:S(2)}) collective-permute-start(bf16[512,128]{1,0:T(8,128)(2,1)S(1)} %collective-permute-done), channel_id=1, source_target_pairs={{0,4},{4,8},{8,12},{12,16},{16,20},{20,24},{24,28},{28,32},{32,36}... | collective-permute-start | bytes 393224 | tf_op jit(solution)/shard_map/ppermute | solution.py:17
  59.7 16.0 %collective-permute-start.3 = (bf16[512,128]{1,0:T(8,128)(2,1)S(1)}, bf16[512,128]{1,0:T(8,128)(2,1)S(1)}, u32[]{:S(2)}, u32[]{:S(2)}) collective-permute-start(bf16[512,128]{1,0:T(8,128)(2,1)S(1)} %collective-permute-done.1), channel_id=1, source_target_pairs={{0,4},{4,8},{8,12},{12,16},{16,20},{20,24},{24,28},{28,32},{32,36}... | collective-permute-start | bytes 393224 | tf_op jit(solution)/shard_map/ppermute | solution.py:17
  72.8 12.4 %collective-permute-start.4 = (bf16[512,128]{1,0:T(8,128)(2,1)S(1)}, bf16[512,128]{1,0:T(8,128)(2,1)S(1)}, u32[]{:S(2)}, u32[]{:S(2)}) collective-permute-start(bf16[512,128]{1,0:T(8,128)(2,1)S(1)} %collective-permute-done.2), channel_id=1, source_target_pairs={{0,4},{4,8},{8,12},{12,16},{16,20},{20,24},{24,28},{28,32},{32,36}... | collective-permute-start | bytes 393224 | tf_op jit(solution)/shard_map/ppermute | solution.py:17
  75.6 20.1 %collective-permute-start.5 = (bf16[512,128]{1,0:T(8,128)(2,1)S(1)}, bf16[512,128]{1,0:T(8,128)(2,1)S(1)}, u32[]{:S(2)}, u32[]{:S(2)}) collective-permute-start(bf16[512,128]{1,0:T(8,128)(2,1)S(1)} %collective-permute-done.3), channel_id=1, source_target_pairs={{0,4},{4,8},{8,12},{12,16},{16,20},{20,24},{24,28},{28,32},{32,36}... | collective-permute-start | bytes 393224 | tf_op jit(solution)/shard_map/ppermute | solution.py:17
where the time goes:
time: 118 us; the launch traced here: 117 us
  waiting for transfers between devices  40.8 us (35%)
  starting transfers between devices  33.2 us (28%)
  blocking collectives  18 us (15%)
  matrix products  10.6 us (9%)
  local copies, waits for them, and re-layouts  8.33 us (7%)
  other arithmetic  6.27 us (5%)
    ppermute x6, waiting for transfers between devices, passed_along(): return lax.ppermute(value, axis, pairs)  30.6 us
    all_to_all x1, blocking collectives, on_device(): lax.all_to_all(result, 'head', split_axis=0, concat_axis=1, tiled=True)  18 us
    ppermute x6, starting transfers between devices, passed_along(): return lax.ppermute(value, axis, pairs)  14.1 us
    all_to_all x1, starting transfers between devices, on_device(): lax.all_to_all(keys, 'head', split_axis=1, concat_axis=0, tiled=True)  10.2 us
    all_to_all x1, waiting for transfers between devices, on_device(): lax.all_to_all(values, 'head', split_axis=1, concat_axis=0, tiled=True)  7.43 us
    dot_general x4, matrix products, absorb(): jnp.einsum('cgrk,kce->cgre', rounded, values, preferred_element_type=jnp....  7.02 us
    all_to_all x1, starting transfers between devices, on_device(): lax.all_to_all(values, 'head', split_axis=1, concat_axis=0, tiled=True)  4.52 us
    all_to_all x1, starting transfers between devices, on_device(): lax.all_to_all(queries, 'head', split_axis=1, concat_axis=0, tiled=True)  4.48 us
  transfers between devices with their start and end apart: 9, of which 7 were waited for; matrix products, arithmetic and copies ran while one was open for 17% of the time, Pallas kernels for 0%

commit v1 on v0

v1 whole, which is shorter than its diff:
```python
import functools
import math

import jax
import jax.numpy as jnp
from jax import lax
from jax.experimental import pallas as pl
from jax.experimental.pallas import tpu as pltpu
from jax.sharding import PartitionSpec as P

HEAD_DIM = 128
FRAME_TOK = 128
CYCLE = 4
NEGATIVE = -1e30
SCALE = math.log2(math.e) * HEAD_DIM ** (-0.5)

NX, NYLO, NYHI, NZ, NC = 4, 4, 2, 8, 2
AXES = ("blk", "head")


def flat(place):
    x, y, z, c = place
    return ((x * NYLO + y % NYLO) * NZ + z) * (NYHI * NC) + (y // NYLO) * NC + c


def places():
    for x in range(NX):
        for y in range(NYLO * NYHI):
            for z in range(NZ):
                for c in range(NC):
                    yield (x, y, z, c)


def next_group(place):
    x, y, z, c = place
    z += 1
    if z == NZ:
        z = 0
        if y % NYLO == NYLO - 1:
            x = (x + 1) % NX
        y = (y + 1) % (NYLO * NYHI)
    return (x, y, z, c)


def other_column(place):
    x, y, z, c = place
    return (x, (y + NYLO) % (NYLO * NYHI), z, c)


def other_core(place):
    x, y, z, c = place
    return (x, y, z, 1 - c)


def moved(value, target):
    return lax.ppermute(value, AXES, [(flat(p), flat(target(p))) for p in places()])


def attend_kernel(tags, first, last, where_ref, frame_ref, count_ref, query_ref, *refs):
    pieces, refs = refs[: len(tags)], refs[len(tags):]
    if not first:
        (acc_in, stat_in), refs = refs[:2], refs[2:]
    blk, head = where_ref[0], where_ref[1]
    group_dev = NYHI * NC
    blocks = NX * NYLO * NZ
    query_pos = frame_ref[blk * group_dev + head]
    key_tok = lax.broadcasted_iota(jnp.int32, (FRAME_TOK, FRAME_TOK), 0)
    query_tok = lax.broadcasted_iota(jnp.int32, (FRAME_TOK, FRAME_TOK), 1)
    allowed = []
    for offset, column, mate in tags:
        source = lax.rem(blk - offset + blocks, blocks)
        crossed = jnp.where(source // (NYLO * NZ) != blk // (NYLO * NZ), 1, 0)
        side = lax.rem(head // NC + crossed + column, NYHI)
        core = lax.rem(head + mate, NC)
        frame = source * group_dev + side * NC + core
        limit = jnp.where(frame_ref[frame] < query_pos, count_ref[frame], 0)
        if (offset, column, mate) == (0, 0, 0):
            seen = (key_tok <= query_tok) & (key_tok < count_ref[frame])
        else:
            seen = key_tok < limit
        allowed.append(jnp.concatenate([seen] * 4, axis=1))
    allowed = jnp.concatenate(allowed, axis=0) if len(allowed) > 1 else allowed[0]
    kv_heads = pieces[0].shape[1] // (2 * HEAD_DIM)
    for c in range(kv_heads):
        queries = jnp.concatenate(
            [query_ref[:, (4 * c + r) * HEAD_DIM:(4 * c + r + 1) * HEAD_DIM] for r in range(4)], axis=0
        )
        keys = jnp.concatenate([p[:, c * HEAD_DIM:(c + 1) * HEAD_DIM] for p in pieces], axis=0)
        values = jnp.concatenate(
            [p[:, (kv_heads + c) * HEAD_DIM:(kv_heads + c + 1) * HEAD_DIM] for p in pieces], axis=0
        )
        scores = lax.dot_general(
            keys, queries, (((1,), (1,)), ((), ())), preferred_element_type=jnp.float32
        )
        scores = jnp.where(allowed, scores, NEGATIVE)
        top = jnp.max(scores, axis=0, keepdims=True)
        if not first:
            old = stat_in[c:c + 1, :]
            top = jnp.maximum(top, old)
        weights = jnp.exp2((scores - top) * SCALE)
        total = jnp.sum(weights, axis=0, keepdims=True)
        weighted = lax.dot_general(
            values, weights.astype(jnp.bfloat16), (((0,), (0,)), ((), ())),
            preferred_element_type=jnp.float32,
        )
        if not first:
            shrink = jnp.exp2((old - top) * SCALE)
            total = total + stat_in[kv_heads + c:kv_heads + c + 1, :] * shrink
            weighted = weighted + acc_in[c] * shrink
        if last:
            (out_ref,) = refs
            result = weighted / total
            for r in range(4):
                out_ref[:, (4 * c + r) * HEAD_DIM:(4 * c + r + 1) * HEAD_DIM] = (
                    result[:, r * FRAME_TOK:(r + 1) * FRAME_TOK].T.astype(jnp.bfloat16)
                )
        else:
            acc_ref, stat_ref = refs
            acc_ref[c] = weighted
            stat_ref[c:c + 1, :] = top
            stat_ref[kv_heads + c:kv_heads + c + 1, :] = total


def attend(tags, state, last, where, frame_of, counts, queries, pieces):
    rows, width = queries.shape
    kv_heads = pieces[0].shape[1] // (2 * HEAD_DIM)
    in_smem = pl.BlockSpec(memory_space=pltpu.SMEM)
    in_vmem = pl.BlockSpec(memory_space=pltpu.VMEM)
    if last:
        out_shape = jax.ShapeDtypeStruct((rows, width), jnp.bfloat16)
        out_specs = in_vmem
    else:
        out_shape = (
            jax.ShapeDtypeStruct((kv_heads, HEAD_DIM, 4 * FRAME_TOK), jnp.float32),
            jax.ShapeDtypeStruct((2 * kv_heads, 4 * FRAME_TOK), jnp.float32),
        )
        out_specs = (in_vmem, in_vmem)
    keys = len(pieces) * FRAME_TOK
    per_head = 4 * FRAME_TOK * keys
    return pl.pallas_call(
        functools.partial(attend_kernel, tags, state is None, last),
        out_shape=out_shape,
        in_specs=[in_smem] * 3 + [in_vmem] * (1 + len(pieces) + (0 if state is None else 2)),
        out_specs=out_specs,
        compiler_params=pltpu.CompilerParams(vmem_limit_bytes=40 * 1024 * 1024),
        cost_estimate=pl.CostEstimate(
            flops=4 * HEAD_DIM * per_head * kv_heads,
            bytes_accessed=(len(pieces) + 4) * 256 * 1024,
            transcendentals=per_head * kv_heads,
        ),
    )(where, frame_of, counts, queries, *pieces, *(() if state is None else state))


def on_device(queries, keys, values, frame_of, counts):
    where = jnp.stack([lax.axis_index("blk"), lax.axis_index("head")]).astype(jnp.int32)
    own = jnp.concatenate([keys, values], axis=1)
    cross = [moved(own, other_column)]
    near = [own]
    for offset in range(1, CYCLE):
        near.append(moved(near[-1], next_group))
        cross.append(moved(cross[-1], next_group))
    run = functools.partial(attend, where=where, frame_of=frame_of, counts=counts, queries=queries)

    def stage(entries, state, last):
        tags, pieces = [], []
        for offset, column in entries:
            piece = (near, cross)[column][offset]
            tags += [(offset, column, 0), (offset, column, 1)]
            pieces += [piece, moved(piece, other_core)]
        return run(tuple(tags), state, last, pieces=pieces)

    state = stage([(0, 0)], None, False)
    state = stage([(1, 0), (0, 1)], state, False)
    state = stage([(2, 0), (1, 1)], state, False)
    state = stage([(3, 0), (2, 1)], state, False)
    return stage([(3, 1)], state, True)


def solution(mesh):
    in_specs = (
        P(("blk", "head"), None),
        P(("blk", "head"), None),
        P(("blk", "head"), None),
        P(),
        P(),
    )
    out_specs = P(("blk", "head"), None)
    return jax.shard_map(
        on_device, mesh=mesh, in_specs=in_specs, out_specs=out_specs, check_vma=False
    )
```

time: 118 us -> 94.3 us (0.80)
  blocking collectives: 18 us -> 0 us
  Pallas kernels: 0 us -> 14.8 us
  starting transfers between devices: 33.2 us -> 44.8 us
  waiting for transfers between devices: 40.8 us -> 29.6 us
  matrix products: 10.6 us -> 0 us
  other arithmetic: 6.27 us -> 0.08 us
  local copies, waits for them, and re-layouts: 8.33 us -> 4.14 us
    ppermute x6 -> x15, starting transfers between devices: 14.1 us -> 44.8 us  [moved(): lax.ppermute(value, AXES, [(flat(p), flat(target(p))) for p in places()])]
    all_to_all x3 -> x0, starting transfers between devices: 19.2 us -> none  [the longest x1 10.2 us: on_device(): lax.all_to_all(keys, 'head', split_axis=1, concat_axis=0, tiled=True)]
    all_to_all x1 -> x0, blocking collectives: 18 us -> none  [on_device(): lax.all_to_all(result, 'head', split_axis=0, concat_axis=1, tiled=True)]
    pallas_call x0 -> x5, Pallas kernels: none -> 14.8 us  [attend(): pl.pallas_call(functools.partial(attend_kernel, tags, state is None, last...]
    dot_general x8 -> x0, matrix products: 10.6 us -> none  [the longest x4 7.02 us: absorb(): jnp.einsum('cgrk,kce->cgre', rounded, values, preferred_element_type=jnp....]
    all_to_all x3 -> x0, waiting for transfers between devices: 10.1 us -> none  [the longest x1 7.43 us: on_device(): lax.all_to_all(values, 'head', split_axis=1, concat_axis=0, tiled=True)]
    all_to_all x5 -> x0, local copies, waits for them, and re-layouts: 5.4 us -> none  [the longest x1 1.88 us: on_device(): lax.all_to_all(queries, 'head', split_axis=1, concat_axis=0, tiled=True)]
    reduce_sum x4 -> x0, other arithmetic: 4.21 us -> none  [absorb(): running_sum = running_sum * shrink + jnp.sum(weights, axis=-1)]
  transfers between devices with their start and end apart: 9 -> 15, of which waited for: 7 -> 6; matrix products, arithmetic and copies ran while one was open for 17% -> 0% of each run, Pallas kernels for 0% -> 13%
where the time goes in v1:
time: 94.3 us; the launch traced here: 93.7 us
  starting transfers between devices  44.8 us (48%)
  waiting for transfers between devices  29.6 us (31%)
  Pallas kernels  14.8 us (16%)
  local copies, waits for them, and re-layouts  4.14 us (4%)
    ppermute x15, starting transfers between devices, moved(): lax.ppermute(value, AXES, [(flat(p), flat(target(p))) for p in places()])  44.8 us
    ppermute x15, waiting for transfers between devices, moved(): lax.ppermute(value, AXES, [(flat(p), flat(target(p))) for p in places()])  29.6 us
    pallas_call x5, Pallas kernels, attend(): pl.pallas_call(functools.partial(attend_kernel, tags, state is None, last...  14.8 us
    unnamed x11, local copies, waits for them, and re-layouts  3.23 us
  transfers between devices with their start and end apart: 15, of which 6 were waited for; matrix products, arithmetic and copies ran while one was open for 0% of the time, Pallas kernels for 13%

profile of v1, /device:TPU:1, one launch (start us, length us, event | category | flops | bytes accessed | tf_op | source)
XLA Modules:
  0.0 93.7 jit_solution(9866501980580360883)
XLA Ops:
  0.0 0.0 copy-start
  0.0 1.0 %constant_dynamic-update-slice_fusion.1 = bf16[128,1024]{1,0:T(8,128)(2,1)S(1)} fusion(bf16[128,512]{1,0:T(8,128)(2,1)} %param.6), kind=kLoop, calls=%fused_computation.1 | loop fusion | bytes 262144
  1.0 0.9 constant_dynamic-update-slice_fusion.refs_0_
  1.9 8.3 %collective-permute-start = (bf16[128,1024]{1,0:T(8,128)(2,1)S(1)}, bf16[128,1024]{1,0:T(8,128)(2,1)S(1)}, u32[]{:S(2)}, u32[]{:S(2)}) collective-permute-start(bf16[128,1024]{1,0:T(8,128)(2,1)S(1)} %constant_dynamic-update-slice_fusion.refs_0_), channel_id=1, source_target_pairs={{0,2},{1,3},{4,6},{5,7},{8,10},{9,11},{12,14},{13,15},{16,18},{17,... | collective-permute-start | bytes 786440 | tf_op jit(solution)/shard_map/ppermute | solution.py:56
  10.2 4.0 %collective-permute-start.5 = (bf16[128,1024]{1,0:T(8,128)(2,1)S(1)}, bf16[128,1024]{1,0:T(8,128)(2,1)S(1)}, u32[]{:S(2)}, u32[]{:S(2)}) collective-permute-start(bf16[128,1024]{1,0:T(8,128)(2,1)S(1)} %constant_dynamic-update-slice_fusion.refs_0_), channel_id=1, source_target_pairs={{0,4},{1,5},{4,8},{5,9},{8,12},{9,13},{12,16},{13,17},{16,20},{17,... | collective-permute-start | bytes 786440 | tf_op jit(solution)/shard_map/ppermute | solution.py:56
  14.2 4.5 %collective-permute-done.refs_2_ = bf16[128,1024]{1,0:T(8,128)(2,1)S(1)} collective-permute-done((bf16[128,1024]{1,0:T(8,128)(2,1)S(1)}, bf16[128,1024]{1,0:T(8,128)(2,1)S(1)}, u32[]{:S(2)}, u32[]{:S(2)}) %collective-permute-start) | collective-permute-done | bytes 262176 | tf_op jit(solution)/shard_map/ppermute | solution.py:56
  18.7 3.1 %collective-permute-start.1 = (bf16[128,1024]{1,0:T(8,128)(2,1)S(1)}, bf16[128,1024]{1,0:T(8,128)(2,1)S(1)}, u32[]{:S(2)}, u32[]{:S(2)}) collective-permute-start(bf16[128,1024]{1,0:T(8,128)(2,1)S(1)} %collective-permute-done.refs_2_), channel_id=1, source_target_pairs={{0,4},{1,5},{4,8},{5,9},{8,12},{9,13},{12,16},{13,17},{16,20},{17,... | collective-permute-start | bytes 786440 | tf_op jit(solution)/shard_map/ppermute | solution.py:56
  21.8 17.1 %collective-permute-done.5.refs_0_ = bf16[128,1024]{1,0:T(8,128)(2,1)S(1)} collective-permute-done((bf16[128,1024]{1,0:T(8,128)(2,1)S(1)}, bf16[128,1024]{1,0:T(8,128)(2,1)S(1)}, u32[]{:S(2)}, u32[]{:S(2)}) %collective-permute-start.5) | collective-permute-done | bytes 262176 | tf_op jit(solution)/shard_map/ppermute | solution.py:56
  38.8 1.9 %collective-permute-start.6 = (bf16[128,1024]{1,0:T(8,128)(2,1)S(1)}, bf16[128,1024]{1,0:T(8,128)(2,1)S(1)}, u32[]{:S(2)}, u32[]{:S(2)}) collective-permute-start(bf16[128,1024]{1,0:T(8,128)(2,1)S(1)} %collective-permute-done.5.refs_0_), channel_id=1, source_target_pairs={{0,4},{1,5},{4,8},{5,9},{8,12},{9,13},{12,16},{13,17},{16,20},{17,... | collective-permute-start | bytes 786440 | tf_op jit(solution)/shard_map/ppermute | solution.py:56
  40.8 2.6 %collective-permute-done.1.refs_2_ = bf16[128,1024]{1,0:T(8,128)(2,1)S(1)} collective-permute-done((bf16[128,1024]{1,0:T(8,128)(2,1)S(1)}, bf16[128,1024]{1,0:T(8,128)(2,1)S(1)}, u32[]{:S(2)}, u32[]{:S(2)}) %collective-permute-start.1) | collective-permute-done | bytes 262176 | tf_op jit(solution)/shard_map/ppermute | solution.py:56
  43.3 1.9 %collective-permute-start.2 = (bf16[128,1024]{1,0:T(8,128)(2,1)S(1)}, bf16[128,1024]{1,0:T(8,128)(2,1)S(1)}, u32[]{:S(2)}, u32[]{:S(2)}) collective-permute-start(bf16[128,1024]{1,0:T(8,128)(2,1)S(1)} %collective-permute-done.1.refs_2_), channel_id=1, source_target_pairs={{0,4},{1,5},{4,8},{5,9},{8,12},{9,13},{12,16},{13,17},{16,20},{17,... | collective-permute-start | bytes 786440 | tf_op jit(solution)/shard_map/ppermute | solution.py:56
  45.3 3.5 %collective-permute-start.14 = (bf16[128,1024]{1,0:T(8,128)(2,1)S(1)}, bf16[128,1024]{1,0:T(8,128)(2,1)S(1)}, u32[]{:S(2)}, u32[]{:S(2)}) collective-permute-start(bf16[128,1024]{1,0:T(8,128)(2,1)S(1)} %constant_dynamic-update-slice_fusion.refs_0_), channel_id=1, source_target_pairs={{0,1},{1,0},{4,5},{5,4},{8,9},{9,8},{12,13},{13,12},{16,17},{17,16... | collective-permute-start | bytes 786440 | tf_op jit(solution)/shard_map/ppermute | solution.py:56
  48.8 1.9 %collective-permute-start.12 = (bf16[128,1024]{1,0:T(8,128)(2,1)S(1)}, bf16[128,1024]{1,0:T(8,128)(2,1)S(1)}, u32[]{:S(2)}, u32[]{:S(2)}) collective-permute-start(bf16[128,1024]{1,0:T(8,128)(2,1)S(1)} %collective-permute-done.5.refs_0_), channel_id=1, source_target_pairs={{0,1},{1,0},{4,5},{5,4},{8,9},{9,8},{12,13},{13,12},{16,17},{17,16... | collective-permute-start | bytes 786440 | tf_op jit(solution)/shard_map/ppermute | solution.py:56
  50.7 2.4 %collective-permute-start.13 = (bf16[128,1024]{1,0:T(8,128)(2,1)S(1)}, bf16[128,1024]{1,0:T(8,128)(2,1)S(1)}, u32[]{:S(2)}, u32[]{:S(2)}) collective-permute-start(bf16[128,1024]{1,0:T(8,128)(2,1)S(1)} %collective-permute-done.refs_2_), channel_id=1, source_target_pairs={{0,1},{1,0},{4,5},{5,4},{8,9},{9,8},{12,13},{13,12},{16,17},{17,16... | collective-permute-start | bytes 786440 | tf_op jit(solution)/shard_map/ppermute | solution.py:56
  53.1 0.3 collective-permute-done.6.refs_0_
  53.4 1.9 %collective-permute-start.7 = (bf16[128,1024]{1,0:T(8,128)(2,1)S(1)}, bf16[128,1024]{1,0:T(8,128)(2,1)S(1)}, u32[]{:S(2)}, u32[]{:S(2)}) collective-permute-start(bf16[128,1024]{1,0:T(8,128)(2,1)S(1)} %collective-permute-done.6.refs_0_), channel_id=1, source_target_pairs={{0,4},{1,5},{4,8},{5,9},{8,12},{9,13},{12,16},{13,17},{16,20},{17,... | collective-permute-start | bytes 786440 | tf_op jit(solution)/shard_map/ppermute | solution.py:56
  55.3 3.7 %collective-permute-done.2.refs_2_ = bf16[128,1024]{1,0:T(8,128)(2,1)S(1)} collective-permute-done((bf16[128,1024]{1,0:T(8,128)(2,1)S(1)}, bf16[128,1024]{1,0:T(8,128)(2,1)S(1)}, u32[]{:S(2)}, u32[]{:S(2)}) %collective-permute-start.2) | collective-permute-done | bytes 262176 | tf_op jit(solution)/shard_map/ppermute | solution.py:56
  59.0 1.9 %collective-permute-start.3 = (bf16[128,1024]{1,0:T(8,128)(2,1)S(1)}, bf16[128,1024]{1,0:T(8,128)(2,1)S(1)}, u32[]{:S(2)}, u32[]{:S(2)}) collective-permute-start(bf16[128,1024]{1,0:T(8,128)(2,1)S(1)} %collective-permute-done.2.refs_2_), channel_id=1, source_target_pairs={{0,4},{1,5},{4,8},{5,9},{8,12},{9,13},{12,16},{13,17},{16,20},{17,... | collective-permute-start | bytes 786440 | tf_op jit(solution)/shard_map/ppermute | solution.py:56
  61.0 0.0 collective-permute-done.14.refs_1_
  61.0 0.0 copy-start.1
  61.0 0.7 copy-done.1
  61.7 3.3 %collective-permute-start.10 = (bf16[128,1024]{1,0:T(8,128)(2,1)S(1)}, bf16[128,1024]{1,0:T(8,128)(2,1)}, u32[]{:S(2)}, u32[]{:S(2)}) collective-permute-start(bf16[128,1024]{1,0:T(8,128)(2,1)S(1)} %collective-permute-done.6.refs_0_), channel_id=1, source_target_pairs={{0,1},{1,0},{4,5},{5,4},{8,9},{9,8},{12,13},{13,12},{16,17},{17,16... | collective-permute-start | bytes 786440 | tf_op jit(solution)/shard_map/ppermute | solution.py:56
  65.0 0.0 collective-permute-done.12.refs_1_
  65.0 1.9 %collective-permute-start.11 = (bf16[128,1024]{1,0:T(8,128)(2,1)S(1)}, bf16[128,1024]{1,0:T(8,128)(2,1)}, u32[]{:S(2)}, u32[]{:S(2)}) collective-permute-start(bf16[128,1024]{1,0:T(8,128)(2,1)S(1)} %collective-permute-done.1.refs_2_), channel_id=1, source_target_pairs={{0,1},{1,0},{4,5},{5,4},{8,9},{9,8},{12,13},{13,12},{16,17},{17,16... | collective-permute-start | bytes 786440 | tf_op jit(solution)/shard_map/ppermute | solution.py:56
  67.0 0.0 collective-permute-done.13.refs_3_
  67.0 2.4 %collective-permute-start.9 = (bf16[128,1024]{1,0:T(8,128)(2,1)S(1)}, bf16[128,1024]{1,0:T(8,128)(2,1)S(1)}, u32[]{:S(2)}, u32[]{:S(2)}) collective-permute-start(bf16[128,1024]{1,0:T(8,128)(2,1)S(1)} %collective-permute-done.2.refs_2_), channel_id=1, source_target_pairs={{0,1},{1,0},{4,5},{5,4},{8,9},{9,8},{12,13},{13,12},{16,17},{17,16... | collective-permute-start | bytes 786440 | tf_op jit(solution)/shard_map/ppermute | solution.py:56
  69.4 0.0 collective-permute-done.7.refs_0_
  69.4 2.2 %collective-permute-start.8 = (bf16[128,1024]{1,0:T(8,128)(2,1)S(1)}, bf16[128,1024]{1,0:T(8,128)(2,1)}, u32[]{:S(2)}, u32[]{:S(2)}) collective-permute-start(bf16[128,1024]{1,0:T(8,128)(2,1)S(1)} %collective-permute-done.7.refs_0_), channel_id=1, source_target_pairs={{0,1},{1,0},{4,5},{5,4},{8,9},{9,8},{12,13},{13,12},{16,17},{17,16... | collective-permute-start | bytes 786440 | tf_op jit(solution)/shard_map/ppermute | solution.py:56
  71.6 1.4 %collective-permute-done.3.refs_0_ = bf16[128,1024]{1,0:T(8,128)(2,1)S(1)} collective-permute-done((bf16[128,1024]{1,0:T(8,128)(2,1)S(1)}, bf16[128,1024]{1,0:T(8,128)(2,1)S(1)}, u32[]{:S(2)}, u32[]{:S(2)}) %collective-permute-start.3) | collective-permute-done | bytes 262176 | tf_op jit(solution)/shard_map/ppermute | solution.py:56
  73.0 4.1 %collective-permute-start.4 = (bf16[128,1024]{1,0:T(8,128)(2,1)S(1)}, bf16[128,1024]{1,0:T(8,128)(2,1)S(1)}, u32[]{:S(2)}, u32[]{:S(2)}) collective-permute-start(bf16[128,1024]{1,0:T(8,128)(2,1)S(1)} %collective-permute-done.3.refs_0_), channel_id=1, source_target_pairs={{0,1},{1,0},{4,5},{5,4},{8,9},{9,8},{12,13},{13,12},{16,17},{17,16... | collective-permute-start | bytes 786440 | tf_op jit(solution)/shard_map/ppermute | solution.py:56
  77.1 0.0 copy-start.4
  77.1 0.0 copy-start.3
  77.2 0.1 pad_add_fusion.where_ref
  77.2 0.0 copy-done
  77.2 0.6 copy-done.4
  77.8 0.0 copy-done.3
  77.8 0.0 copy-start.2
  77.8 0.9 %copy-done.2 = bf16[128,1024]{1,0:T(8,128)(2,1)S(1)} copy-done((bf16[128,1024]{1,0:T(8,128)(2,1)S(1)}, bf16[128,1024]{1,0:T(8,128)(2,1)}, u32[]{:S(2)}) %copy-start.2) | copy-done | bytes 262168
  78.8 2.1 %shard_map.55 = (f32[4,128,512]{2,1,0:T(8,128)S(1)}, f32[8,512]{1,0:T(8,128)S(1)}) custom-call(s32[2]{0:T(128)S(1)} %pad_add_fusion.where_ref, s32[512]{0:T(512)S(1)} %copy-done.3, s32[512]{0:T(512)S(1)} %copy-done.4, bf16[128,2048]{1,0:T(8,128)(2,1)S(1)} %copy-done, bf16[128,1024]{1,0:T(8,128)(2,1)S(1)} %constant_dynamic-update-slice_fusion.refs_0_, ...), custom_call_target="tpu_custom_call" | custom-call | flops 268435456 | bytes 1572864 | tf_op jit(solution)/shard_map/pallas_call | solution.py:140
  80.9 3.0 %shard_map.56 = (f32[4,128,512]{2,1,0:T(8,128)S(1)}, f32[8,512]{1,0:T(8,128)S(1)}) custom-call(s32[2]{0:T(128)S(1)} %pad_add_fusion.where_ref, s32[512]{0:T(512)S(1)} %copy-done.3, s32[512]{0:T(512)S(1)} %copy-done.4, bf16[128,2048]{1,0:T(8,128)(2,1)S(1)} %copy-done, bf16[128,1024]{1,0:T(8,128)(2,1)S(1)} %collective-permute-done.5.refs_0_, ...), custom_call_target="tpu_custom_call" | custom-call | flops 536870912 | bytes 2097152 | tf_op jit(solution)/shard_map/pallas_call | solution.py:140
  83.9 0.0 collective-permute-done.10.refs_1_
  83.9 0.0 collective-permute-done.11.refs_3_
  83.9 3.4 %shard_map.57 = (f32[4,128,512]{2,1,0:T(8,128)S(1)}, f32[8,512]{1,0:T(8,128)S(1)}) custom-call(s32[2]{0:T(128)S(1)} %pad_add_fusion.where_ref, s32[512]{0:T(512)S(1)} %copy-done.3, s32[512]{0:T(512)S(1)} %copy-done.4, bf16[128,2048]{1,0:T(8,128)(2,1)S(1)} %copy-done, bf16[128,1024]{1,0:T(8,128)(2,1)S(1)} %collective-permute-done.6.refs_0_, ...), custom_call_target="tpu_custom_call" | custom-call | flops 536870912 | bytes 2097152 | tf_op jit(solution)/shard_map/pallas_call | solution.py:140
  87.3 0.0 collective-permute-done.9.refs_3_
  87.3 0.0 collective-permute-done.8.refs_1_
  87.4 3.3 %shard_map.58 = (f32[4,128,512]{2,1,0:T(8,128)S(1)}, f32[8,512]{1,0:T(8,128)S(1)}) custom-call(s32[2]{0:T(128)S(1)} %pad_add_fusion.where_ref, s32[512]{0:T(512)S(1)} %copy-done.3, s32[512]{0:T(512)S(1)} %copy-done.4, bf16[128,2048]{1,0:T(8,128)(2,1)S(1)} %copy-done, bf16[128,1024]{1,0:T(8,128)(2,1)S(1)} %collective-permute-done.7.refs_0_, ...), custom_call_target="tpu_custom_call" | custom-call | flops 536870912 | bytes 2097152 | tf_op jit(solution)/shard_map/pallas_call | solution.py:140
  90.7 0.0 collective-permute-done.4.refs_1_
  90.7 3.0 %shard_map.59 = bf16[128,2048]{1,0:T(8,128)(2,1)} custom-call(s32[2]{0:T(128)S(1)} %pad_add_fusion.where_ref, s32[512]{0:T(512)S(1)} %copy-done.3, s32[512]{0:T(512)S(1)} %copy-done.4, bf16[128,2048]{1,0:T(8,128)(2,1)S(1)} %copy-done, bf16[128,1024]{1,0:T(8,128)(2,1)S(1)} %collective-permute-done.3.refs_0_, ...), custom_call_target="tpu_custom_call" | custom-call | flops 268435456 | bytes 1572864 | tf_op jit(solution)/shard_map/pallas_call | solution.py:140
Async XLA Ops:
  0.0 77.2 %copy-start = (bf16[128,2048]{1,0:T(8,128)(2,1)S(1)}, bf16[128,2048]{1,0:T(8,128)(2,1)}, u32[]{:S(2)}) copy-start(bf16[128,2048]{1,0:T(8,128)(2,1)} %query_ref.9) | copy-start | bytes 1572868
  1.9 16.8 %collective-permute-start = (bf16[128,1024]{1,0:T(8,128)(2,1)S(1)}, bf16[128,1024]{1,0:T(8,128)(2,1)S(1)}, u32[]{:S(2)}, u32[]{:S(2)}) collective-permute-start(bf16[128,1024]{1,0:T(8,128)(2,1)S(1)} %constant_dynamic-update-slice_fusion.refs_0_), channel_id=1, source_target_pairs={{0,2},{1,3},{4,6},{5,7},{8,10},{9,11},{12,14},{13,15},{16,18},{17,... | collective-permute-start | bytes 786440 | tf_op jit(solution)/shard_map/ppermute | solution.py:56
  10.2 28.7 %collective-permute-start.5 = (bf16[128,1024]{1,0:T(8,128)(2,1)S(1)}, bf16[128,1024]{1,0:T(8,128)(2,1)S(1)}, u32[]{:S(2)}, u32[]{:S(2)}) collective-permute-start(bf16[128,1024]{1,0:T(8,128)(2,1)S(1)} %constant_dynamic-update-slice_fusion.refs_0_), channel_id=1, source_target_pairs={{0,4},{1,5},{4,8},{5,9},{8,12},{9,13},{12,16},{13,17},{16,20},{17,... | collective-permute-start | bytes 786440 | tf_op jit(solution)/shard_map/ppermute | solution.py:56
  18.7 24.7 %collective-permute-start.1 = (bf16[128,1024]{1,0:T(8,128)(2,1)S(1)}, bf16[128,1024]{1,0:T(8,128)(2,1)S(1)}, u32[]{:S(2)}, u32[]{:S(2)}) collective-permute-start(bf16[128,1024]{1,0:T(8,128)(2,1)S(1)} %collective-permute-done.refs_2_), channel_id=1, source_target_pairs={{0,4},{1,5},{4,8},{5,9},{8,12},{9,13},{12,16},{13,17},{16,20},{17,... | collective-permute-start | bytes 786440 | tf_op jit(solution)/shard_map/ppermute | solution.py:56
  38.8 14.6 %collective-permute-start.6 = (bf16[128,1024]{1,0:T(8,128)(2,1)S(1)}, bf16[128,1024]{1,0:T(8,128)(2,1)S(1)}, u32[]{:S(2)}, u32[]{:S(2)}) collective-permute-start(bf16[128,1024]{1,0:T(8,128)(2,1)S(1)} %collective-permute-done.5.refs_0_), channel_id=1, source_target_pairs={{0,4},{1,5},{4,8},{5,9},{8,12},{9,13},{12,16},{13,17},{16,20},{17,... | collective-permute-start | bytes 786440 | tf_op jit(solution)/shard_map/ppermute | solution.py:56
  43.3 15.7 %collective-permute-start.2 = (bf16[128,1024]{1,0:T(8,128)(2,1)S(1)}, bf16[128,1024]{1,0:T(8,128)(2,1)S(1)}, u32[]{:S(2)}, u32[]{:S(2)}) collective-permute-start(bf16[128,1024]{1,0:T(8,128)(2,1)S(1)} %collective-permute-done.1.refs_2_), channel_id=1, source_target_pairs={{0,4},{1,5},{4,8},{5,9},{8,12},{9,13},{12,16},{13,17},{16,20},{17,... | collective-permute-start | bytes 786440 | tf_op jit(solution)/shard_map/ppermute | solution.py:56
  45.3 15.7 %collective-permute-start.14 = (bf16[128,1024]{1,0:T(8,128)(2,1)S(1)}, bf16[128,1024]{1,0:T(8,128)(2,1)S(1)}, u32[]{:S(2)}, u32[]{:S(2)}) collective-permute-start(bf16[128,1024]{1,0:T(8,128)(2,1)S(1)} %constant_dynamic-update-slice_fusion.refs_0_), channel_id=1, source_target_pairs={{0,1},{1,0},{4,5},{5,4},{8,9},{9,8},{12,13},{13,12},{16,17},{17,16... | collective-permute-start | bytes 786440 | tf_op jit(solution)/shard_map/ppermute | solution.py:56
  48.8 16.2 %collective-permute-start.12 = (bf16[128,1024]{1,0:T(8,128)(2,1)S(1)}, bf16[128,1024]{1,0:T(8,128)(2,1)S(1)}, u32[]{:S(2)}, u32[]{:S(2)}) collective-permute-start(bf16[128,1024]{1,0:T(8,128)(2,1)S(1)} %collective-permute-done.5.refs_0_), channel_id=1, source_target_pairs={{0,1},{1,0},{4,5},{5,4},{8,9},{9,8},{12,13},{13,12},{16,17},{17,16... | collective-permute-start | bytes 786440 | tf_op jit(solution)/shard_map/ppermute | solution.py:56
  50.7 16.3 %collective-permute-start.13 = (bf16[128,1024]{1,0:T(8,128)(2,1)S(1)}, bf16[128,1024]{1,0:T(8,128)(2,1)S(1)}, u32[]{:S(2)}, u32[]{:S(2)}) collective-permute-start(bf16[128,1024]{1,0:T(8,128)(2,1)S(1)} %collective-permute-done.refs_2_), channel_id=1, source_target_pairs={{0,1},{1,0},{4,5},{5,4},{8,9},{9,8},{12,13},{13,12},{16,17},{17,16... | collective-permute-start | bytes 786440 | tf_op jit(solution)/shard_map/ppermute | solution.py:56
  53.4 16.0 %collective-permute-start.7 = (bf16[128,1024]{1,0:T(8,128)(2,1)S(1)}, bf16[128,1024]{1,0:T(8,128)(2,1)S(1)}, u32[]{:S(2)}, u32[]{:S(2)}) collective-permute-start(bf16[128,1024]{1,0:T(8,128)(2,1)S(1)} %collective-permute-done.6.refs_0_), channel_id=1, source_target_pairs={{0,4},{1,5},{4,8},{5,9},{8,12},{9,13},{12,16},{13,17},{16,20},{17,... | collective-permute-start | bytes 786440 | tf_op jit(solution)/shard_map/ppermute | solution.py:56
  59.0 14.0 %collective-permute-start.3 = (bf16[128,1024]{1,0:T(8,128)(2,1)S(1)}, bf16[128,1024]{1,0:T(8,128)(2,1)S(1)}, u32[]{:S(2)}, u32[]{:S(2)}) collective-permute-start(bf16[128,1024]{1,0:T(8,128)(2,1)S(1)} %collective-permute-done.2.refs_2_), channel_id=1, source_target_pairs={{0,4},{1,5},{4,8},{5,9},{8,12},{9,13},{12,16},{13,17},{16,20},{17,... | collective-permute-start | bytes 786440 | tf_op jit(solution)/shard_map/ppermute | solution.py:56
  61.0 0.7 copy-start.1
  61.7 22.2 %collective-permute-start.10 = (bf16[128,1024]{1,0:T(8,128)(2,1)S(1)}, bf16[128,1024]{1,0:T(8,128)(2,1)}, u32[]{:S(2)}, u32[]{:S(2)}) collective-permute-start(bf16[128,1024]{1,0:T(8,128)(2,1)S(1)} %collective-permute-done.6.refs_0_), channel_id=1, source_target_pairs={{0,1},{1,0},{4,5},{5,4},{8,9},{9,8},{12,13},{13,12},{16,17},{17,16... | collective-permute-start | bytes 786440 | tf_op jit(solution)/shard_map/ppermute | solution.py:56
  65.0 18.9 %collective-permute-start.11 = (bf16[128,1024]{1,0:T(8,128)(2,1)S(1)}, bf16[128,1024]{1,0:T(8,128)(2,1)}, u32[]{:S(2)}, u32[]{:S(2)}) collective-permute-start(bf16[128,1024]{1,0:T(8,128)(2,1)S(1)} %collective-permute-done.1.refs_2_), channel_id=1, source_target_pairs={{0,1},{1,0},{4,5},{5,4},{8,9},{9,8},{12,13},{13,12},{16,17},{17,16... | collective-permute-start | bytes 786440 | tf_op jit(solution)/shard_map/ppermute | solution.py:56
  67.0 20.3 %collective-permute-start.9 = (bf16[128,1024]{1,0:T(8,128)(2,1)S(1)}, bf16[128,1024]{1,0:T(8,128)(2,1)S(1)}, u32[]{:S(2)}, u32[]{:S(2)}) collective-permute-start(bf16[128,1024]{1,0:T(8,128)(2,1)S(1)} %collective-permute-done.2.refs_2_), channel_id=1, source_target_pairs={{0,1},{1,0},{4,5},{5,4},{8,9},{9,8},{12,13},{13,12},{16,17},{17,16... | collective-permute-start | bytes 786440 | tf_op jit(solution)/shard_map/ppermute | solution.py:56
  69.4 17.9 %collective-permute-start.8 = (bf16[128,1024]{1,0:T(8,128)(2,1)S(1)}, bf16[128,1024]{1,0:T(8,128)(2,1)}, u32[]{:S(2)}, u32[]{:S(2)}) collective-permute-start(bf16[128,1024]{1,0:T(8,128)(2,1)S(1)} %collective-permute-done.7.refs_0_), channel_id=1, source_target_pairs={{0,1},{1,0},{4,5},{5,4},{8,9},{9,8},{12,13},{13,12},{16,17},{17,16... | collective-permute-start | bytes 786440 | tf_op jit(solution)/shard_map/ppermute | solution.py:56
  73.0 17.7 %collective-permute-start.4 = (bf16[128,1024]{1,0:T(8,128)(2,1)S(1)}, bf16[128,1024]{1,0:T(8,128)(2,1)S(1)}, u32[]{:S(2)}, u32[]{:S(2)}) collective-permute-start(bf16[128,1024]{1,0:T(8,128)(2,1)S(1)} %collective-permute-done.3.refs_0_), channel_id=1, source_target_pairs={{0,1},{1,0},{4,5},{5,4},{8,9},{9,8},{12,13},{13,12},{16,17},{17,16... | collective-permute-start | bytes 786440 | tf_op jit(solution)/shard_map/ppermute | solution.py:56
  77.1 0.7 copy-start.4
  77.1 0.7 copy-start.3
  77.8 0.9 %copy-start.2 = (bf16[128,1024]{1,0:T(8,128)(2,1)S(1)}, bf16[128,1024]{1,0:T(8,128)(2,1)}, u32[]{:S(2)}) copy-start(bf16[128,1024]{1,0:T(8,128)(2,1)} %copy-done.1) | copy-start | bytes 786436

commit v2 on v1

v2 whole, which is shorter than its diff:
```python
import functools
import math

import jax
import jax.numpy as jnp
from jax import lax
from jax.experimental import pallas as pl
from jax.experimental.pallas import tpu as pltpu
from jax.sharding import PartitionSpec as P

HEAD_DIM = 128
FRAME_TOK = 128
CYCLE = 4
NEGATIVE = -1e30
SCALE = math.log2(math.e) * HEAD_DIM ** (-0.5)

NX, NYLO, NYHI, NZ, NC = 4, 4, 2, 8, 2
AXES = ("blk", "head")
BLOCKS, GROUP_DEV = NX * NYLO * NZ, NYHI * NC
GROUP = 4


def flat(place):
    x, y, z, c = place
    return ((x * NYLO + y % NYLO) * NZ + z) * (NYHI * NC) + (y // NYLO) * NC + c


def places():
    for x in range(NX):
        for y in range(NYLO * NYHI):
            for z in range(NZ):
                for c in range(NC):
                    yield (x, y, z, c)


def next_group(place):
    x, y, z, c = place
    z += 1
    if z == NZ:
        z = 0
        if y % NYLO == NYLO - 1:
            x = (x + 1) % NX
        y = (y + 1) % (NYLO * NYHI)
    return (x, y, z, c)


def other_column(place):
    x, y, z, c = place
    return (x, (y + NYLO) % (NYLO * NYHI), z, c)


def other_core(place):
    x, y, z, c = place
    return (x, y, z, 1 - c)


def moved(value, target, sources=lambda place: True):
    return lax.ppermute(value, AXES, [(flat(p), flat(target(p))) for p in places() if sources(p)])


def inside(value):
    return moved(value, next_group, lambda place: place[2] != NZ - 1)


def onward(value):
    return moved(value, next_group, lambda place: place[2] == NZ - 1)


def after(value, *others):
    return lax.optimization_barrier((value, *others))[0]


def kv_heads_of(piece):
    return piece.shape[1] // (2 * HEAD_DIM)


def head_rows(query_ref, c):
    return jnp.concatenate(
        [query_ref[:, (GROUP * c + r) * HEAD_DIM:(GROUP * c + r + 1) * HEAD_DIM] for r in range(GROUP)], axis=0
    )


def piece_frame(blk, head, tag):
    offset, column = tag
    source = lax.rem(blk - offset + BLOCKS, BLOCKS)
    crossed = jnp.where(source // (NYLO * NZ) != blk // (NYLO * NZ), 1, 0)
    side = lax.rem(head // NC + crossed + column, NYHI)
    return source * GROUP_DEV + side * NC + lax.rem(head, NC)


def attend_kernel(tags, sets, first, sent, where_ref, frame_ref, count_ref, *refs):
    query_refs, refs = refs[: len(sets)], refs[len(sets):]
    pieces, refs = refs[: len(tags)], refs[len(tags):]
    if first:
        states_in, states_out = None, refs
    else:
        states_in, states_out = refs[: 2 * len(sets)], refs[2 * len(sets):]
    blk, head = where_ref[0], where_ref[1]
    kv_heads = kv_heads_of(pieces[0])
    rows = GROUP * FRAME_TOK
    key_tok = lax.broadcasted_iota(jnp.int32, (FRAME_TOK, rows), 0)
    query_tok = lax.rem(lax.broadcasted_iota(jnp.int32, (FRAME_TOK, rows), 1), FRAME_TOK)
    allowed = []
    for mate in sets:
        core = lax.rem(head + mate, NC)
        query_pos = frame_ref[blk * GROUP_DEV + head - lax.rem(head, NC) + core]
        parts = []
        for tag in tags:
            frame = piece_frame(blk, head, tag)
            if tag == (0, 0) and mate == 0:
                parts.append((key_tok <= query_tok) & (key_tok < count_ref[frame]))
            else:
                limit = jnp.where(frame_ref[frame] < query_pos, count_ref[frame], 0)
                parts.append(key_tok < limit)
        allowed.append(parts)
    stats = []
    todo = [(i, c) for i in range(len(sets)) for c in range(kv_heads)]

    def score(i, c):
        keys = [p[:, c * HEAD_DIM:(c + 1) * HEAD_DIM] for p in pieces]
        scores = lax.dot_general(
            jnp.concatenate(keys, axis=0) if len(keys) > 1 else keys[0], head_rows(query_refs[i], c),
            (((1,), (1,)), ((), ())), preferred_element_type=jnp.float32,
        )
        masked = [
            jnp.where(allowed[i][f], scores[f * FRAME_TOK:(f + 1) * FRAME_TOK], NEGATIVE) for f in range(len(tags))
        ]
        return jnp.concatenate(masked, axis=0) if len(masked) > 1 else masked[0]

    def weigh(i, c, scores):
        top = jnp.max(scores, axis=0, keepdims=True)
        shrink = None
        if not first:
            stat = states_in[2 * i + 1]
            old = stat[c:c + 1, :]
            top = jnp.maximum(top, old)
            shrink = jnp.exp2((old - top) * SCALE)
        weights = jnp.exp2((scores - top) * SCALE)
        total = jnp.sum(weights, axis=0, keepdims=True)
        if not first:
            total = total + stat[kv_heads + c:kv_heads + c + 1, :] * shrink
        return weights.astype(jnp.bfloat16), top, total, shrink

    def gather(i, c, weights, top, total, shrink):
        values = [p[:, (kv_heads + c) * HEAD_DIM:(kv_heads + c + 1) * HEAD_DIM] for p in pieces]
        weighted = lax.dot_general(
            jnp.concatenate(values, axis=0) if len(values) > 1 else values[0], weights,
            (((0,), (0,)), ((), ())), preferred_element_type=jnp.float32,
        )
        if not first:
            weighted = weighted + states_in[2 * i][c] * shrink
        if sent:
            states_out[0][c * HEAD_DIM:(c + 1) * HEAD_DIM, :] = weighted.astype(jnp.bfloat16)
            stats.append((top, total))
        else:
            states_out[2 * i][c] = weighted
            states_out[2 * i + 1][c:c + 1, :] = top
            states_out[2 * i + 1][kv_heads + c:kv_heads + c + 1, :] = total

    scores = score(*todo[0])
    before = None
    for n, item in enumerate(todo):
        following = score(*todo[n + 1]) if n + 1 < len(todo) else None
        done = weigh(*item, scores)
        if before is not None:
            gather(*todo[n - 1], *before)
        scores, before = following, done
    gather(*todo[-1], *before)
    if sent:
        rest = jnp.concatenate([top for top, _ in stats] + [total for _, total in stats], axis=0)
        parts = []
        for _ in range(3):
            parts.append(rest.astype(jnp.bfloat16).astype(jnp.float32))
            rest = rest - parts[-1]
        packed = jnp.concatenate(parts + [jnp.zeros_like(rest)], axis=0)
        states_out[0][kv_heads * HEAD_DIM:, :] = packed.astype(jnp.bfloat16)


def merge_kernel(acc_ref, stat_ref, got_ref, out_ref):
    kv_heads = acc_ref.shape[0]
    wide = kv_heads * HEAD_DIM
    parts = got_ref[wide:wide + 32, :].astype(jnp.float32)
    got_stat = parts[:8] + parts[8:16] + parts[16:24]
    for c in range(kv_heads):
        top, total = stat_ref[c:c + 1, :], stat_ref[kv_heads + c:kv_heads + c + 1, :]
        got_top, got_total = got_stat[c:c + 1, :], got_stat[kv_heads + c:kv_heads + c + 1, :]
        most = jnp.maximum(top, got_top)
        mine, theirs = jnp.exp2((top - most) * SCALE), jnp.exp2((got_top - most) * SCALE)
        share = 1.0 / (total * mine + got_total * theirs)
        result = acc_ref[c] * (mine * share) + got_ref[c * HEAD_DIM:(c + 1) * HEAD_DIM, :].astype(jnp.float32) * (theirs * share)
        for r in range(GROUP):
            out_ref[:, (GROUP * c + r) * HEAD_DIM:(GROUP * c + r + 1) * HEAD_DIM] = (
                result[:, r * FRAME_TOK:(r + 1) * FRAME_TOK].T.astype(jnp.bfloat16)
            )


IN_SMEM = pl.BlockSpec(memory_space=pltpu.SMEM)
IN_VMEM = pl.BlockSpec(memory_space=pltpu.VMEM)
PARAMS = pltpu.CompilerParams(vmem_limit_bytes=48 * 1024 * 1024)


def attend(tags, sets, state, tables, queries, pieces, sent=False):
    kv_heads = kv_heads_of(pieces[0])
    rows = GROUP * FRAME_TOK
    out_shape = (
        jax.ShapeDtypeStruct((kv_heads, HEAD_DIM, rows), jnp.float32),
        jax.ShapeDtypeStruct((2 * kv_heads, rows), jnp.float32),
    ) * len(sets)
    if sent:
        out_shape = jax.ShapeDtypeStruct((kv_heads * HEAD_DIM + 32, rows), jnp.bfloat16)
    scores = rows * len(pieces) * FRAME_TOK * kv_heads * len(sets)
    return pl.pallas_call(
        functools.partial(attend_kernel, tags, sets, state is None, sent),
        out_shape=out_shape,
        in_specs=[IN_SMEM] * 3 + [IN_VMEM] * (len(sets) + len(pieces) + (0 if state is None else 2 * len(sets))),
        out_specs=IN_VMEM if sent else (IN_VMEM,) * (2 * len(sets)),
        compiler_params=PARAMS,
        cost_estimate=pl.CostEstimate(
            flops=4 * HEAD_DIM * scores, bytes_accessed=1024 * 1024, transcendentals=scores
        ),
    )(*tables, *queries, *pieces, *(() if state is None else state))


def merge(state, got, shape):
    return pl.pallas_call(
        merge_kernel,
        out_shape=jax.ShapeDtypeStruct(shape, jnp.bfloat16),
        in_specs=[IN_VMEM] * 3,
        out_specs=IN_VMEM,
        compiler_params=PARAMS,
        cost_estimate=pl.CostEstimate(flops=4 * shape[0] * shape[1], bytes_accessed=3 * 1024 * 1024, transcendentals=0),
    )(*state, got)


def on_device(queries, keys, values, frame_of, counts):
    blk = lax.axis_index("blk")
    where = jnp.stack([blk, lax.axis_index("head")]).astype(jnp.int32)
    starts_line = lax.rem(blk, NZ) == 0
    tables = (where, frame_of, counts)

    def either(first, other):
        return jnp.where(starts_line, first, other)

    own = jnp.concatenate([keys, values], axis=1)
    cross0 = moved(own, other_column)
    near1 = moved(own, next_group)
    both = (queries, moved(after(queries, near1), other_core))

    in_cross1, on_cross1 = inside(cross0), onward(cross0)
    near2 = moved(near1, next_group)
    state = attend(((0, 0), (0, 1), (1, 0)), (0, 1), None, tables, both, (own, cross0, near1))

    on_cross2 = onward(in_cross1)
    cross1 = either(on_cross1, in_cross1)
    in_cross2 = inside(after(cross1, state[1]))
    near3 = moved(near2, next_group)
    state = attend(((1, 1), (2, 0)), (0, 1), state, tables, both, (cross1, near2))

    on_cross3 = onward(in_cross2)
    cross2 = either(on_cross2, in_cross2)
    in_cross3 = inside(after(cross2, state[1]))
    state = attend(((2, 1), (3, 0)), (0, 1), state, tables, both, (cross2, near3))

    cross3 = either(on_cross3, in_cross3)
    got = moved(attend(((3, 1),), (1,), state[2:], tables, both[1:], (cross3,), True), other_core)
    own_state = attend(((3, 1),), (0,), state[:2], tables, both[:1], (cross3,))
    return merge(own_state, got, queries.shape)


def solution(mesh):
    in_specs = (
        P(("blk", "head"), None),
        P(("blk", "head"), None),
        P(("blk", "head"), None),
        P(),
        P(),
    )
    out_specs = P(("blk", "head"), None)
    return jax.shard_map(
        on_device, mesh=mesh, in_specs=in_specs, out_specs=out_specs, check_vma=False
    )
```

time: 94.3 us -> 82.6 us (0.88)
  starting transfers between devices: 44.8 us -> 35.9 us
  local copies, waits for them, and re-layouts: 4.14 us -> 0.99 us
  waiting for transfers between devices: 29.6 us -> 32 us
  Pallas kernels: 14.8 us -> 12.9 us
    ppermute x15 -> x12, starting transfers between devices: 44.8 us -> 35.9 us  [moved(): lax.ppermute(value, AXES, [(flat(p), flat(target(p))) for p in places() i...]
    ppermute x15 -> x12, waiting for transfers between devices: 29.6 us -> 32 us  [moved(): lax.ppermute(value, AXES, [(flat(p), flat(target(p))) for p in places() i...]
    unnamed x11 -> x9, local copies, waits for them, and re-layouts: 3.23 us -> 0.97 us
    pallas_call x5 -> x6, Pallas kernels: 14.8 us -> 12.9 us  [the longest x5 11.8 us: attend(): pl.pallas_call(functools.partial(attend_kernel, tags, sets, state is None...]
  transfers between devices with their start and end apart: 15 -> 12, of which waited for: 6 -> 8; matrix products, arithmetic and copies ran while one was open for 0% -> 0% of each run, Pallas kernels for 13% -> 13%
where the time goes in v2:
time: 82.6 us; the launch traced here: 82.2 us
  starting transfers between devices  35.9 us (43%)
  waiting for transfers between devices  32 us (39%)
  Pallas kernels  12.9 us (16%)
  local copies, waits for them, and re-layouts  0.99 us (1%)
    ppermute x12, starting transfers between devices, moved(): lax.ppermute(value, AXES, [(flat(p), flat(target(p))) for p in places() i...  35.9 us
    ppermute x12, waiting for transfers between devices, moved(): lax.ppermute(value, AXES, [(flat(p), flat(target(p))) for p in places() i...  32 us
    pallas_call x5, Pallas kernels, attend(): pl.pallas_call(functools.partial(attend_kernel, tags, sets, state is None...  11.8 us
  transfers between devices with their start and end apart: 12, of which 8 were waited for; matrix products, arithmetic and copies ran while one was open for 0% of the time, Pallas kernels for 13%

profile of v2, /device:TPU:1, one launch (start us, length us, event | category | flops | bytes accessed | tf_op | source)
XLA Modules:
  0.0 82.2 jit_solution(840536457146000012)
XLA Ops:
  0.0 0.0 copy-start.3
  0.0 0.9 %constant_dynamic-update-slice_fusion.1 = bf16[128,1024]{1,0:T(8,128)(2,1)S(1)} fusion(bf16[128,512]{1,0:T(8,128)(2,1)} %param.6), kind=kLoop, calls=%fused_computation.4 | loop fusion | bytes 262144
  1.0 0.0 copy-done.3
  1.0 0.0 copy-start
  1.0 5.0 %collective-permute-start.3 = (bf16[128,1024]{1,0:T(8,128)(2,1)S(1)}, bf16[128,1024]{1,0:T(8,128)(2,1)S(1)}, u32[]{:S(2)}, u32[]{:S(2)}) collective-permute-start(bf16[128,1024]{1,0:T(8,128)(2,1)S(1)} %constant_dynamic-update-slice_fusion.refs_2_), channel_id=1, source_target_pairs={{0,4},{1,5},{4,8},{5,9},{8,12},{9,13},{12,16},{13,17},{16,20},{17,... | collective-permute-start | bytes 786440 | tf_op jit(solution)/shard_map/ppermute | solution.py:58
  6.0 7.5 %collective-permute-start = (bf16[128,1024]{1,0:T(8,128)(2,1)S(1)}, bf16[128,1024]{1,0:T(8,128)(2,1)S(1)}, u32[]{:S(2)}, u32[]{:S(2)}) collective-permute-start(bf16[128,1024]{1,0:T(8,128)(2,1)S(1)} %constant_dynamic-update-slice_fusion.refs_2_), channel_id=1, source_target_pairs={{0,2},{1,3},{4,6},{5,7},{8,10},{9,11},{12,14},{13,15},{16,18},{17,... | collective-permute-start | bytes 786440 | tf_op jit(solution)/shard_map/ppermute | solution.py:58
  13.4 10.3 %collective-permute-done.3.refs_4_ = bf16[128,1024]{1,0:T(8,128)(2,1)S(1)} collective-permute-done((bf16[128,1024]{1,0:T(8,128)(2,1)S(1)}, bf16[128,1024]{1,0:T(8,128)(2,1)S(1)}, u32[]{:S(2)}, u32[]{:S(2)}) %collective-permute-start.3) | collective-permute-done | bytes 262176 | tf_op jit(solution)/shard_map/ppermute | solution.py:58
  23.7 3.2 %collective-permute-start.4 = (bf16[128,2048]{1,0:T(8,128)(2,1)}, bf16[128,2048]{1,0:T(8,128)(2,1)S(1)}, u32[]{:S(2)}, u32[]{:S(2)}) collective-permute-start(bf16[128,2048]{1,0:T(8,128)(2,1)} %refs_0_.7), channel_id=1, source_target_pairs={{0,1},{1,0},{4,5},{5,4},{8,9},{9,8},{12,13},{13,12},{16,17},{17,16... | collective-permute-start | bytes 1572872 | tf_op jit(solution)/shard_map/ppermute | solution.py:58
  26.9 0.0 collective-permute-done.refs_3_
  26.9 1.3 %collective-permute-start.2 = (bf16[128,1024]{1,0:T(8,128)(2,1)S(1)}, bf16[128,1024]{1,0:T(8,128)(2,1)S(1)}, u32[]{:S(2)}, u32[]{:S(2)}) collective-permute-start(bf16[128,1024]{1,0:T(8,128)(2,1)S(1)} %collective-permute-done.refs_3_), channel_id=1, source_target_pairs={{0,4},{1,5},{4,8},{5,9},{8,12},{9,13},{12,16},{13,17},{16,20},{17,... | collective-permute-start | bytes 786440 | tf_op jit(solution)/shard_map/ppermute | solution.py:58
  28.2 1.3 %collective-permute-start.1 = (bf16[128,1024]{1,0:T(8,128)(2,1)S(1)}, bf16[128,1024]{1,0:T(8,128)(2,1)S(1)}, u32[]{:S(2)}, u32[]{:S(2)}) collective-permute-start(bf16[128,1024]{1,0:T(8,128)(2,1)S(1)} %collective-permute-done.refs_3_), channel_id=1, source_target_pairs={{28,32},{29,33},{60,64},{61,65},{92,96},{93,97},{124,130},{125,131... | collective-permute-start | bytes 786440 | tf_op jit(solution)/shard_map/ppermute | solution.py:58
  29.6 0.1 pad_add_fusion.where_ref
  29.6 0.0 copy-start.1
  29.6 0.0 copy-start.2
  29.6 2.0 %collective-permute-start.8 = (bf16[128,1024]{1,0:T(8,128)(2,1)S(1)}, bf16[128,1024]{1,0:T(8,128)(2,1)S(1)}, u32[]{:S(2)}, u32[]{:S(2)}) collective-permute-start(bf16[128,1024]{1,0:T(8,128)(2,1)S(1)} %collective-permute-done.3.refs_4_), channel_id=1, source_target_pairs={{0,4},{1,5},{4,8},{5,9},{8,12},{9,13},{12,16},{13,17},{16,20},{17,... | collective-permute-start | bytes 786440 | tf_op jit(solution)/shard_map/ppermute | solution.py:58
  31.7 2.5 %collective-permute-done.2 = bf16[128,1024]{1,0:T(8,128)(2,1)S(1)} collective-permute-done((bf16[128,1024]{1,0:T(8,128)(2,1)S(1)}, bf16[128,1024]{1,0:T(8,128)(2,1)S(1)}, u32[]{:S(2)}, u32[]{:S(2)}) %collective-permute-start.2) | collective-permute-done | bytes 262176 | tf_op jit(solution)/shard_map/ppermute | solution.py:58
  34.1 1.3 %collective-permute-start.7 = (bf16[128,1024]{1,0:T(8,128)(2,1)S(1)}, bf16[128,1024]{1,0:T(8,128)(2,1)S(1)}, u32[]{:S(2)}, u32[]{:S(2)}) collective-permute-start(bf16[128,1024]{1,0:T(8,128)(2,1)S(1)} %collective-permute-done.2), channel_id=1, source_target_pairs={{28,32},{29,33},{60,64},{61,65},{92,96},{93,97},{124,130},{125,131... | collective-permute-start | bytes 786440 | tf_op jit(solution)/shard_map/ppermute | solution.py:58
  35.4 8.0 %collective-permute-done.1 = bf16[128,1024]{1,0:T(8,128)(2,1)S(1)} collective-permute-done((bf16[128,1024]{1,0:T(8,128)(2,1)S(1)}, bf16[128,1024]{1,0:T(8,128)(2,1)S(1)}, u32[]{:S(2)}, u32[]{:S(2)}) %collective-permute-start.1) | collective-permute-done | bytes 262176 | tf_op jit(solution)/shard_map/ppermute | solution.py:58
  43.5 0.0 collective-permute-done.4.refs_1_.refs_0_
  43.5 0.0 copy-done
  43.5 0.0 copy-done.1
  43.5 0.0 copy-done.2
  43.5 3.3 %shard_map.55 = (f32[4,128,512]{2,1,0:T(8,128)S(1)}, f32[8,512]{1,0:T(8,128)S(1)}, f32[4,128,512]{2,1,0:T(8,128)S(1)}, f32[8,512]{1,0:T(8,128)S(1)}) custom-call(s32[2]{0:T(128)S(1)} %pad_add_fusion.where_ref, s32[512]{0:T(512)S(1)} %copy-done.1, s32[512]{0:T(512)S(1)} %copy-done.2, bf16[128,2048]{1,0:T(8,128)(2,1)S(1)} %copy-done, ...), custom_call_target="tpu_custom_call" | custom-call | flops 805306368 | bytes 1048576 | tf_op jit(solution)/shard_map/pallas_call | solution.py:212
  46.8 1.3 %collective-permute-start.5 = (bf16[128,1024]{1,0:T(8,128)(2,1)S(1)}, bf16[128,1024]{1,0:T(8,128)(2,1)S(1)}, u32[]{:S(2)}, u32[]{:S(2)}) collective-permute-start(bf16[128,1024]{1,0:T(8,128)(2,1)S(1)} %broadcast_select_fusion.2.refs_2_), channel_id=1, source_target_pairs={{0,4},{1,5},{4,8},{5,9},{8,12},{9,13},{12,16},{13,17},{16,20},{17,... | collective-permute-start | bytes 786440 | tf_op jit(solution)/shard_map/ppermute | solution.py:58
  48.1 0.9 %collective-permute-done.8.refs_3_ = bf16[128,1024]{1,0:T(8,128)(2,1)S(1)} collective-permute-done((bf16[128,1024]{1,0:T(8,128)(2,1)S(1)}, bf16[128,1024]{1,0:T(8,128)(2,1)S(1)}, u32[]{:S(2)}, u32[]{:S(2)}) %collective-permute-start.8) | collective-permute-done | bytes 262176 | tf_op jit(solution)/shard_map/ppermute | solution.py:58
  49.0 1.9 %collective-permute-start.10 = (bf16[128,1024]{1,0:T(8,128)(2,1)S(1)}, bf16[128,1024]{1,0:T(8,128)(2,1)S(1)}, u32[]{:S(2)}, u32[]{:S(2)}) collective-permute-start(bf16[128,1024]{1,0:T(8,128)(2,1)S(1)} %collective-permute-done.8.refs_3_), channel_id=1, source_target_pairs={{0,4},{1,5},{4,8},{5,9},{8,12},{9,13},{12,16},{13,17},{16,20},{17,... | collective-permute-start | bytes 786440 | tf_op jit(solution)/shard_map/ppermute | solution.py:58
  51.0 2.8 %shard_map.56 = (f32[4,128,512]{2,1,0:T(8,128)S(1)}, f32[8,512]{1,0:T(8,128)S(1)}, f32[4,128,512]{2,1,0:T(8,128)S(1)}, f32[8,512]{1,0:T(8,128)S(1)}) custom-call(s32[2]{0:T(128)S(1)} %pad_add_fusion.where_ref, s32[512]{0:T(512)S(1)} %copy-done.1, s32[512]{0:T(512)S(1)} %copy-done.2, bf16[128,2048]{1,0:T(8,128)(2,1)S(1)} %copy-done, ...), custom_call_target="tpu_custom_call" | custom-call | flops 536870912 | bytes 1048576 | tf_op jit(solution)/shard_map/pallas_call | solution.py:212
  53.8 0.8 %collective-permute-done.7 = bf16[128,1024]{1,0:T(8,128)(2,1)S(1)} collective-permute-done((bf16[128,1024]{1,0:T(8,128)(2,1)S(1)}, bf16[128,1024]{1,0:T(8,128)(2,1)S(1)}, u32[]{:S(2)}, u32[]{:S(2)}) %collective-permute-start.7) | collective-permute-done | bytes 262176 | tf_op jit(solution)/shard_map/ppermute | solution.py:58
  54.7 0.0 collective-permute-done.5
  54.7 1.3 %collective-permute-start.9 = (bf16[128,1024]{1,0:T(8,128)(2,1)S(1)}, bf16[128,1024]{1,0:T(8,128)(2,1)S(1)}, u32[]{:S(2)}, u32[]{:S(2)}) collective-permute-start(bf16[128,1024]{1,0:T(8,128)(2,1)S(1)} %broadcast_select_fusion.1.refs_2_), channel_id=1, source_target_pairs={{0,4},{1,5},{4,8},{5,9},{8,12},{9,13},{12,16},{13,17},{16,20},{17,... | collective-permute-start | bytes 786440 | tf_op jit(solution)/shard_map/ppermute | solution.py:58
  56.0 1.3 %collective-permute-start.6 = (bf16[128,1024]{1,0:T(8,128)(2,1)S(1)}, bf16[128,1024]{1,0:T(8,128)(2,1)S(1)}, u32[]{:S(2)}, u32[]{:S(2)}) collective-permute-start(bf16[128,1024]{1,0:T(8,128)(2,1)S(1)} %collective-permute-done.5), channel_id=1, source_target_pairs={{28,32},{29,33},{60,64},{61,65},{92,96},{93,97},{124,130},{125,131... | collective-permute-start | bytes 786440 | tf_op jit(solution)/shard_map/ppermute | solution.py:58
  57.3 4.3 %collective-permute-done.10.refs_3_ = bf16[128,1024]{1,0:T(8,128)(2,1)S(1)} collective-permute-done((bf16[128,1024]{1,0:T(8,128)(2,1)S(1)}, bf16[128,1024]{1,0:T(8,128)(2,1)S(1)}, u32[]{:S(2)}, u32[]{:S(2)}) %collective-permute-start.10) | collective-permute-done | bytes 262176 | tf_op jit(solution)/shard_map/ppermute | solution.py:58
  61.6 2.8 %shard_map.57 = (f32[4,128,512]{2,1,0:T(8,128)S(1)}, f32[8,512]{1,0:T(8,128)S(1)}, f32[4,128,512]{2,1,0:T(8,128)S(1)}, f32[8,512]{1,0:T(8,128)S(1)}) custom-call(s32[2]{0:T(128)S(1)} %pad_add_fusion.where_ref, s32[512]{0:T(512)S(1)} %copy-done.1, s32[512]{0:T(512)S(1)} %copy-done.2, bf16[128,2048]{1,0:T(8,128)(2,1)S(1)} %copy-done, ...), custom_call_target="tpu_custom_call" | custom-call | flops 536870912 | bytes 1048576 | tf_op jit(solution)/shard_map/pallas_call | solution.py:212
  64.4 0.0 collective-permute-done.9
  64.4 5.0 %collective-permute-done.6 = bf16[128,1024]{1,0:T(8,128)(2,1)S(1)} collective-permute-done((bf16[128,1024]{1,0:T(8,128)(2,1)S(1)}, bf16[128,1024]{1,0:T(8,128)(2,1)S(1)}, u32[]{:S(2)}, u32[]{:S(2)}) %collective-permute-start.6) | collective-permute-done | bytes 262176 | tf_op jit(solution)/shard_map/ppermute | solution.py:58
  69.5 1.4 %shard_map.59 = bf16[544,512]{1,0:T(8,128)(2,1)S(1)} custom-call(s32[2]{0:T(128)S(1)} %pad_add_fusion.where_ref, s32[512]{0:T(512)S(1)} %copy-done.1, s32[512]{0:T(512)S(1)} %copy-done.2, bf16[128,2048]{1,0:T(8,128)(2,1)S(1)} %collective-permute-done.4.refs_1_.refs_0_, bf16[128,1024]{1,0:T(8,128)(2,1)S(1)} %broadcast_select_fusion.refs_1_, ...), custom_call_target="tpu_custom_call" | custom-call | flops 134217728 | bytes 1048576 | tf_op jit(solution)/shard_map/pallas_call | solution.py:212
  70.9 8.6 %collective-permute-start.11 = (bf16[544,512]{1,0:T(8,128)(2,1)S(1)}, bf16[544,512]{1,0:T(8,128)(2,1)S(1)}, u32[]{:S(2)}, u32[]{:S(2)}) collective-permute-start(bf16[544,512]{1,0:T(8,128)(2,1)S(1)} %shard_map.59), channel_id=1, source_target_pairs={{0,1},{1,0},{4,5},{5,4},{8,9},{9,8},{12,13},{13,12},{16,17},{17,16... | collective-permute-start | bytes 1671176 | tf_op jit(solution)/shard_map/ppermute | solution.py:58
  79.5 1.4 %shard_map.58 = (f32[4,128,512]{2,1,0:T(8,128)S(1)}, f32[8,512]{1,0:T(8,128)S(1)}) custom-call(s32[2]{0:T(128)S(1)} %pad_add_fusion.where_ref, s32[512]{0:T(512)S(1)} %copy-done.1, s32[512]{0:T(512)S(1)} %copy-done.2, bf16[128,2048]{1,0:T(8,128)(2,1)S(1)} %copy-done, bf16[128,1024]{1,0:T(8,128)(2,1)S(1)} %broadcast_select_fusion.refs_1_, ...), custom_call_target="tpu_custom_call" | custom-call | flops 134217728 | bytes 1048576 | tf_op jit(solution)/shard_map/pallas_call | solution.py:212
  80.9 0.2 collective-permute-done.11.got_ref
  81.1 1.1 %shard_map.60 = bf16[128,2048]{1,0:T(8,128)(2,1)} custom-call(f32[4,128,512]{2,1,0:T(8,128)S(1)} %get-tuple-element.35.acc_ref, f32[8,512]{1,0:T(8,128)S(1)} %get-tuple-element.36.stat_ref, bf16[544,512]{1,0:T(8,128)(2,1)S(1)} %collective-permute-done.11.got_ref), custom_call_target="tpu_custom_call" | custom-call | flops 1048576 | bytes 3145728 | tf_op jit(solution)/shard_map/pallas_call | solution.py:225
  (4 shorter events, 0.1 us)
Async XLA Ops:
  0.0 1.0 %copy-start.3 = (bf16[128,512]{1,0:T(8,128)(2,1)S(1)}, bf16[128,512]{1,0:T(8,128)(2,1)}, u32[]{:S(2)}) copy-start(bf16[128,512]{1,0:T(8,128)(2,1)} %param.7) | copy-start | bytes 393220
  1.0 42.5 %copy-start = (bf16[128,2048]{1,0:T(8,128)(2,1)S(1)}, bf16[128,2048]{1,0:T(8,128)(2,1)}, u32[]{:S(2)}) copy-start(bf16[128,2048]{1,0:T(8,128)(2,1)} %refs_0_.7) | copy-start | bytes 1572868
  1.0 22.8 %collective-permute-start.3 = (bf16[128,1024]{1,0:T(8,128)(2,1)S(1)}, bf16[128,1024]{1,0:T(8,128)(2,1)S(1)}, u32[]{:S(2)}, u32[]{:S(2)}) collective-permute-start(bf16[128,1024]{1,0:T(8,128)(2,1)S(1)} %constant_dynamic-update-slice_fusion.refs_2_), channel_id=1, source_target_pairs={{0,4},{1,5},{4,8},{5,9},{8,12},{9,13},{12,16},{13,17},{16,20},{17,... | collective-permute-start | bytes 786440 | tf_op jit(solution)/shard_map/ppermute | solution.py:58
  6.0 21.0 %collective-permute-start = (bf16[128,1024]{1,0:T(8,128)(2,1)S(1)}, bf16[128,1024]{1,0:T(8,128)(2,1)S(1)}, u32[]{:S(2)}, u32[]{:S(2)}) collective-permute-start(bf16[128,1024]{1,0:T(8,128)(2,1)S(1)} %constant_dynamic-update-slice_fusion.refs_2_), channel_id=1, source_target_pairs={{0,2},{1,3},{4,6},{5,7},{8,10},{9,11},{12,14},{13,15},{16,18},{17,... | collective-permute-start | bytes 786440 | tf_op jit(solution)/shard_map/ppermute | solution.py:58
  23.7 19.7 %collective-permute-start.4 = (bf16[128,2048]{1,0:T(8,128)(2,1)}, bf16[128,2048]{1,0:T(8,128)(2,1)S(1)}, u32[]{:S(2)}, u32[]{:S(2)}) collective-permute-start(bf16[128,2048]{1,0:T(8,128)(2,1)} %refs_0_.7), channel_id=1, source_target_pairs={{0,1},{1,0},{4,5},{5,4},{8,9},{9,8},{12,13},{13,12},{16,17},{17,16... | collective-permute-start | bytes 1572872 | tf_op jit(solution)/shard_map/ppermute | solution.py:58
  26.9 7.2 %collective-permute-start.2 = (bf16[128,1024]{1,0:T(8,128)(2,1)S(1)}, bf16[128,1024]{1,0:T(8,128)(2,1)S(1)}, u32[]{:S(2)}, u32[]{:S(2)}) collective-permute-start(bf16[128,1024]{1,0:T(8,128)(2,1)S(1)} %collective-permute-done.refs_3_), channel_id=1, source_target_pairs={{0,4},{1,5},{4,8},{5,9},{8,12},{9,13},{12,16},{13,17},{16,20},{17,... | collective-permute-start | bytes 786440 | tf_op jit(solution)/shard_map/ppermute | solution.py:58
  28.2 15.2 %collective-permute-start.1 = (bf16[128,1024]{1,0:T(8,128)(2,1)S(1)}, bf16[128,1024]{1,0:T(8,128)(2,1)S(1)}, u32[]{:S(2)}, u32[]{:S(2)}) collective-permute-start(bf16[128,1024]{1,0:T(8,128)(2,1)S(1)} %collective-permute-done.refs_3_), channel_id=1, source_target_pairs={{28,32},{29,33},{60,64},{61,65},{92,96},{93,97},{124,130},{125,131... | collective-permute-start | bytes 786440 | tf_op jit(solution)/shard_map/ppermute | solution.py:58
  29.6 13.8 %copy-start.1 = (s32[512]{0:T(512)S(1)}, s32[512]{0:T(512)}, u32[]{:S(2)}) copy-start(s32[512]{0:T(512)} %frame_ref.9) | copy-start | bytes 6148
  29.6 13.9 %copy-start.2 = (s32[512]{0:T(512)S(1)}, s32[512]{0:T(512)}, u32[]{:S(2)}) copy-start(s32[512]{0:T(512)} %count_ref.9) | copy-start | bytes 6148
  29.6 19.4 %collective-permute-start.8 = (bf16[128,1024]{1,0:T(8,128)(2,1)S(1)}, bf16[128,1024]{1,0:T(8,128)(2,1)S(1)}, u32[]{:S(2)}, u32[]{:S(2)}) collective-permute-start(bf16[128,1024]{1,0:T(8,128)(2,1)S(1)} %collective-permute-done.3.refs_4_), channel_id=1, source_target_pairs={{0,4},{1,5},{4,8},{5,9},{8,12},{9,13},{12,16},{13,17},{16,20},{17,... | collective-permute-start | bytes 786440 | tf_op jit(solution)/shard_map/ppermute | solution.py:58
  34.1 20.5 %collective-permute-start.7 = (bf16[128,1024]{1,0:T(8,128)(2,1)S(1)}, bf16[128,1024]{1,0:T(8,128)(2,1)S(1)}, u32[]{:S(2)}, u32[]{:S(2)}) collective-permute-start(bf16[128,1024]{1,0:T(8,128)(2,1)S(1)} %collective-permute-done.2), channel_id=1, source_target_pairs={{28,32},{29,33},{60,64},{61,65},{92,96},{93,97},{124,130},{125,131... | collective-permute-start | bytes 786440 | tf_op jit(solution)/shard_map/ppermute | solution.py:58
  46.8 7.9 %collective-permute-start.5 = (bf16[128,1024]{1,0:T(8,128)(2,1)S(1)}, bf16[128,1024]{1,0:T(8,128)(2,1)S(1)}, u32[]{:S(2)}, u32[]{:S(2)}) collective-permute-start(bf16[128,1024]{1,0:T(8,128)(2,1)S(1)} %broadcast_select_fusion.2.refs_2_), channel_id=1, source_target_pairs={{0,4},{1,5},{4,8},{5,9},{8,12},{9,13},{12,16},{13,17},{16,20},{17,... | collective-permute-start | bytes 786440 | tf_op jit(solution)/shard_map/ppermute | solution.py:58
  49.0 12.5 %collective-permute-start.10 = (bf16[128,1024]{1,0:T(8,128)(2,1)S(1)}, bf16[128,1024]{1,0:T(8,128)(2,1)S(1)}, u32[]{:S(2)}, u32[]{:S(2)}) collective-permute-start(bf16[128,1024]{1,0:T(8,128)(2,1)S(1)} %collective-permute-done.8.refs_3_), channel_id=1, source_target_pairs={{0,4},{1,5},{4,8},{5,9},{8,12},{9,13},{12,16},{13,17},{16,20},{17,... | collective-permute-start | bytes 786440 | tf_op jit(solution)/shard_map/ppermute | solution.py:58
  54.7 9.7 %collective-permute-start.9 = (bf16[128,1024]{1,0:T(8,128)(2,1)S(1)}, bf16[128,1024]{1,0:T(8,128)(2,1)S(1)}, u32[]{:S(2)}, u32[]{:S(2)}) collective-permute-start(bf16[128,1024]{1,0:T(8,128)(2,1)S(1)} %broadcast_select_fusion.1.refs_2_), channel_id=1, source_target_pairs={{0,4},{1,5},{4,8},{5,9},{8,12},{9,13},{12,16},{13,17},{16,20},{17,... | collective-permute-start | bytes 786440 | tf_op jit(solution)/shard_map/ppermute | solution.py:58
  56.0 13.4 %collective-permute-start.6 = (bf16[128,1024]{1,0:T(8,128)(2,1)S(1)}, bf16[128,1024]{1,0:T(8,128)(2,1)S(1)}, u32[]{:S(2)}, u32[]{:S(2)}) collective-permute-start(bf16[128,1024]{1,0:T(8,128)(2,1)S(1)} %collective-permute-done.5), channel_id=1, source_target_pairs={{28,32},{29,33},{60,64},{61,65},{92,96},{93,97},{124,130},{125,131... | collective-permute-start | bytes 786440 | tf_op jit(solution)/shard_map/ppermute | solution.py:58
  70.9 10.2 %collective-permute-start.11 = (bf16[544,512]{1,0:T(8,128)(2,1)S(1)}, bf16[544,512]{1,0:T(8,128)(2,1)S(1)}, u32[]{:S(2)}, u32[]{:S(2)}) collective-permute-start(bf16[544,512]{1,0:T(8,128)(2,1)S(1)} %shard_map.59), channel_id=1, source_target_pairs={{0,1},{1,0},{4,5},{5,4},{8,9},{9,8},{12,13},{13,12},{16,17},{17,16... | collective-permute-start | bytes 1671176 | tf_op jit(solution)/shard_map/ppermute | solution.py:58

commit v3 on v2

--- a/solution.py
+++ b/solution.py
@@ -242,25 +242,22 @@
         return jnp.where(starts_line, first, other)
 
     own = jnp.concatenate([keys, values], axis=1)
+    rows = own.shape[0]
+    near1 = moved(own, next_group)
     cross0 = moved(own, other_column)
-    near1 = moved(own, next_group)
+    in_near2 = inside(near1)
     both = (queries, moved(after(queries, near1), other_core))
-
-    in_cross1, on_cross1 = inside(cross0), onward(cross0)
-    near2 = moved(near1, next_group)
+    on_first = onward(jnp.concatenate([cross0, near1], axis=0))
+    in_cross1 = inside(after(cross0, in_near2))
+    on_second = onward(jnp.concatenate([in_cross1, in_near2], axis=0))
+    cross1, near2 = either(on_first[:rows], in_cross1), either(on_first[rows:], in_near2)
     state = attend(((0, 0), (0, 1), (1, 0)), (0, 1), None, tables, both, (own, cross0, near1))
-
-    on_cross2 = onward(in_cross1)
-    cross1 = either(on_cross1, in_cross1)
     in_cross2 = inside(after(cross1, state[1]))
-    near3 = moved(near2, next_group)
-    state = attend(((1, 1), (2, 0)), (0, 1), state, tables, both, (cross1, near2))
-
+    in_near3 = inside(near2)
     on_cross3 = onward(in_cross2)
-    cross2 = either(on_cross2, in_cross2)
-    in_cross3 = inside(after(cross2, state[1]))
-    state = attend(((2, 1), (3, 0)), (0, 1), state, tables, both, (cross2, near3))
-
+    cross2, near3 = either(on_second[:rows], in_cross2), either(on_second[rows:], in_near3)
+    in_cross3 = inside(cross2)
+    state = attend(((2, 0), (1, 1), (3, 0), (2, 1)), (0, 1), state, tables, both, (near2, cross1, near3, cross2))
     cross3 = either(on_cross3, in_cross3)
     got = moved(attend(((3, 1),), (1,), state[2:], tables, both[1:], (cross3,), True), other_core)
     own_state = attend(((3, 1),), (0,), state[:2], tables, both[:1], (cross3,))

time: 82.6 us -> 78.5 us (0.950)
  waiting for transfers between devices: 32 us -> 27.2 us
  starting transfers between devices: 35.9 us -> 37.2 us
    ppermute x12, waiting for transfers between devices: 32 us -> 27.2 us  [moved(): lax.ppermute(value, AXES, [(flat(p), flat(target(p))) for p in places() i...]
    ppermute x12, starting transfers between devices: 35.9 us -> 37.2 us  [moved(): lax.ppermute(value, AXES, [(flat(p), flat(target(p))) for p in places() i...]
    pallas_call x5 -> x4, Pallas kernels: 11.8 us -> 11 us  [attend(): pl.pallas_call(functools.partial(attend_kernel, tags, sets, state is None...]
  transfers between devices with their start and end apart: 12 -> 12, of which waited for: 8 -> 7; matrix products, arithmetic and copies ran while one was open for 0% -> 0% of each run, Pallas kernels for 13% -> 12%
where the time goes in v3:
time: 78.5 us; the launch traced here: 78.1 us
  starting transfers between devices  37.2 us (47%)
  waiting for transfers between devices  27.2 us (35%)
  Pallas kernels  12.1 us (15%)
  local copies, waits for them, and re-layouts  0.99 us (1%)
    ppermute x12, starting transfers between devices, moved(): lax.ppermute(value, AXES, [(flat(p), flat(target(p))) for p in places() i...  37.2 us
    ppermute x12, waiting for transfers between devices, moved(): lax.ppermute(value, AXES, [(flat(p), flat(target(p))) for p in places() i...  27.2 us
    pallas_call x4, Pallas kernels, attend(): pl.pallas_call(functools.partial(attend_kernel, tags, sets, state is None...  11 us
  transfers between devices with their start and end apart: 12, of which 7 were waited for; matrix products, arithmetic and copies ran while one was open for 0% of the time, Pallas kernels for 12%

profile of v3, /device:TPU:1, one launch (start us, length us, event | category | flops | bytes accessed | tf_op | source)
XLA Modules:
  0.0 78.1 jit_solution(14480014435712305434)
XLA Ops:
  0.0 0.0 copy-start.4
  0.0 0.9 %constant_dynamic-update-slice_fusion.1 = bf16[128,1024]{1,0:T(8,128)(2,1)S(1)} fusion(bf16[128,512]{1,0:T(8,128)(2,1)} %param.6), kind=kLoop, calls=%fused_computation.8 | loop fusion | bytes 262144
  1.0 0.0 copy-done.4
  1.0 4.8 %collective-permute-start.1 = (bf16[128,1024]{1,0:T(8,128)(2,1)S(1)}, bf16[128,1024]{1,0:T(8,128)(2,1)S(1)}, u32[]{:S(2)}, u32[]{:S(2)}) collective-permute-start(bf16[128,1024]{1,0:T(8,128)(2,1)S(1)} %constant_dynamic-update-slice_fusion.refs_2_), channel_id=1, source_target_pairs={{0,4},{1,5},{4,8},{5,9},{8,12},{9,13},{12,16},{13,17},{16,20},{17,... | collective-permute-start | bytes 786440 | tf_op jit(solution)/shard_map/ppermute | solution.py:58
  5.8 7.5 %collective-permute-start = (bf16[128,1024]{1,0:T(8,128)(2,1)S(1)}, bf16[128,1024]{1,0:T(8,128)(2,1)S(1)}, u32[]{:S(2)}, u32[]{:S(2)}) collective-permute-start(bf16[128,1024]{1,0:T(8,128)(2,1)S(1)} %constant_dynamic-update-slice_fusion.refs_2_), channel_id=1, source_target_pairs={{0,2},{1,3},{4,6},{5,7},{8,10},{9,11},{12,14},{13,15},{16,18},{17,... | collective-permute-start | bytes 786440 | tf_op jit(solution)/shard_map/ppermute | solution.py:58
  13.3 10.3 %collective-permute-done.1.refs_4_ = bf16[128,1024]{1,0:T(8,128)(2,1)S(1)} collective-permute-done((bf16[128,1024]{1,0:T(8,128)(2,1)S(1)}, bf16[128,1024]{1,0:T(8,128)(2,1)S(1)}, u32[]{:S(2)}, u32[]{:S(2)}) %collective-permute-start.1) | collective-permute-done | bytes 262176 | tf_op jit(solution)/shard_map/ppermute | solution.py:58
  23.6 1.3 %collective-permute-start.3 = (bf16[128,1024]{1,0:T(8,128)(2,1)S(1)}, bf16[128,1024]{1,0:T(8,128)(2,1)S(1)}, u32[]{:S(2)}, u32[]{:S(2)}) collective-permute-start(bf16[128,1024]{1,0:T(8,128)(2,1)S(1)} %collective-permute-done.1.refs_4_), channel_id=1, source_target_pairs={{0,4},{1,5},{4,8},{5,9},{8,12},{9,13},{12,16},{13,17},{16,20},{17,... | collective-permute-start | bytes 786440 | tf_op jit(solution)/shard_map/ppermute | solution.py:58
  24.9 3.2 %collective-permute-start.5 = (bf16[128,2048]{1,0:T(8,128)(2,1)}, bf16[128,2048]{1,0:T(8,128)(2,1)S(1)}, u32[]{:S(2)}, u32[]{:S(2)}) collective-permute-start(bf16[128,2048]{1,0:T(8,128)(2,1)} %refs_0_.5), channel_id=1, source_target_pairs={{0,1},{1,0},{4,5},{5,4},{8,9},{9,8},{12,13},{13,12},{16,17},{17,16... | collective-permute-start | bytes 1572872 | tf_op jit(solution)/shard_map/ppermute | solution.py:58
  28.1 0.0 collective-permute-done.refs_3_
  28.1 1.3 %collective-permute-start.2 = (bf16[256,1024]{1,0:T(8,128)(2,1)S(1)}, bf16[256,1024]{1,0:T(8,128)(2,1)S(1)}, u32[]{:S(2)}, u32[]{:S(2)}) collective-permute-start(bf16[256,1024]{1,0:T(8,128)(2,1)S(1)} %pad_maximum_fusion), channel_id=1, source_target_pairs={{28,32},{29,33},{60,64},{61,65},{92,96},{93,97},{124,130},{125,131... | collective-permute-start | bytes 1572872 | tf_op jit(solution)/shard_map/ppermute | solution.py:58
  29.4 0.0 collective-permute-done.3
  29.5 4.1 %collective-permute-start.4 = (bf16[128,1024]{1,0:T(8,128)(2,1)S(1)}, bf16[128,1024]{1,0:T(8,128)(2,1)S(1)}, u32[]{:S(2)}, u32[]{:S(2)}) collective-permute-start(bf16[128,1024]{1,0:T(8,128)(2,1)S(1)} %collective-permute-done.refs_3_), channel_id=1, source_target_pairs={{0,4},{1,5},{4,8},{5,9},{8,12},{9,13},{12,16},{13,17},{16,20},{17,... | collective-permute-start | bytes 786440 | tf_op jit(solution)/shard_map/ppermute | solution.py:58
  33.6 0.1 pad_add_fusion.where_ref
  33.7 0.0 copy-start
  33.7 0.0 copy-start.2
  33.7 0.0 copy-start.3
  33.7 3.6 %collective-permute-done.4 = bf16[128,1024]{1,0:T(8,128)(2,1)S(1)} collective-permute-done((bf16[128,1024]{1,0:T(8,128)(2,1)S(1)}, bf16[128,1024]{1,0:T(8,128)(2,1)S(1)}, u32[]{:S(2)}, u32[]{:S(2)}) %collective-permute-start.4) | collective-permute-done | bytes 262176 | tf_op jit(solution)/shard_map/ppermute | solution.py:58
  37.3 1.3 %collective-permute-start.8 = (bf16[256,1024]{1,0:T(8,128)(2,1)S(1)}, bf16[256,1024]{1,0:T(8,128)(2,1)S(1)}, u32[]{:S(2)}, u32[]{:S(2)}) collective-permute-start(bf16[256,1024]{1,0:T(8,128)(2,1)S(1)} %pad_maximum_fusion.1), channel_id=1, source_target_pairs={{28,32},{29,33},{60,64},{61,65},{92,96},{93,97},{124,130},{125,131... | collective-permute-start | bytes 1572872 | tf_op jit(solution)/shard_map/ppermute | solution.py:58
  38.6 0.0 collective-permute-done.5.refs_1_.refs_0_
  38.6 0.0 copy-done
  38.6 0.0 copy-done.2
  38.6 0.0 copy-done.3
  38.6 3.3 %shard_map.55 = (f32[4,128,512]{2,1,0:T(8,128)S(1)}, f32[8,512]{1,0:T(8,128)S(1)}, f32[4,128,512]{2,1,0:T(8,128)S(1)}, f32[8,512]{1,0:T(8,128)S(1)}) custom-call(s32[2]{0:T(128)S(1)} %pad_add_fusion.where_ref, s32[512]{0:T(512)S(1)} %copy-done.2, s32[512]{0:T(512)S(1)} %copy-done.3, bf16[128,2048]{1,0:T(8,128)(2,1)S(1)} %copy-done, ...), custom_call_target="tpu_custom_call" | custom-call | flops 805306368 | bytes 1048576 | tf_op jit(solution)/shard_map/pallas_call | solution.py:212
  42.0 0.0 copy-start.1
  42.0 5.7 %collective-permute-done.2 = bf16[256,1024]{1,0:T(8,128)(2,1)S(1)} collective-permute-done((bf16[256,1024]{1,0:T(8,128)(2,1)S(1)}, bf16[256,1024]{1,0:T(8,128)(2,1)S(1)}, u32[]{:S(2)}, u32[]{:S(2)}) %collective-permute-start.2) | collective-permute-done | bytes 524320 | tf_op jit(solution)/shard_map/ppermute | solution.py:58
  47.6 0.1 slice_select_fusion.1
  47.7 1.3 %collective-permute-start.6 = (bf16[128,1024]{1,0:T(8,128)(2,1)S(1)}, bf16[128,1024]{1,0:T(8,128)(2,1)S(1)}, u32[]{:S(2)}, u32[]{:S(2)}) collective-permute-start(bf16[128,1024]{1,0:T(8,128)(2,1)S(1)} %get-tuple-element.21.refs_3_), channel_id=1, source_target_pairs={{0,4},{1,5},{4,8},{5,9},{8,12},{9,13},{12,16},{13,17},{16,20},{17,... | collective-permute-start | bytes 786440 | tf_op jit(solution)/shard_map/ppermute | solution.py:58
  49.0 1.3 %collective-permute-start.10 = (bf16[128,1024]{1,0:T(8,128)(2,1)S(1)}, bf16[128,1024]{1,0:T(8,128)(2,1)S(1)}, u32[]{:S(2)}, u32[]{:S(2)}) collective-permute-start(bf16[128,1024]{1,0:T(8,128)(2,1)S(1)} %get-tuple-element.33.refs_2_), channel_id=1, source_target_pairs={{0,4},{1,5},{4,8},{5,9},{8,12},{9,13},{12,16},{13,17},{16,20},{17,... | collective-permute-start | bytes 786440 | tf_op jit(solution)/shard_map/ppermute | solution.py:58
  50.3 2.0 %collective-permute-done.6 = bf16[128,1024]{1,0:T(8,128)(2,1)S(1)} collective-permute-done((bf16[128,1024]{1,0:T(8,128)(2,1)S(1)}, bf16[128,1024]{1,0:T(8,128)(2,1)S(1)}, u32[]{:S(2)}, u32[]{:S(2)}) %collective-permute-start.6) | collective-permute-done | bytes 262176 | tf_op jit(solution)/shard_map/ppermute | solution.py:58
  52.3 1.3 %collective-permute-start.7 = (bf16[128,1024]{1,0:T(8,128)(2,1)S(1)}, bf16[128,1024]{1,0:T(8,128)(2,1)S(1)}, u32[]{:S(2)}, u32[]{:S(2)}) collective-permute-start(bf16[128,1024]{1,0:T(8,128)(2,1)S(1)} %collective-permute-done.6), channel_id=1, source_target_pairs={{28,32},{29,33},{60,64},{61,65},{92,96},{93,97},{124,130},{125,131... | collective-permute-start | bytes 786440 | tf_op jit(solution)/shard_map/ppermute | solution.py:58
  53.6 2.5 %collective-permute-done.10 = bf16[128,1024]{1,0:T(8,128)(2,1)S(1)} collective-permute-done((bf16[128,1024]{1,0:T(8,128)(2,1)S(1)}, bf16[128,1024]{1,0:T(8,128)(2,1)S(1)}, u32[]{:S(2)}, u32[]{:S(2)}) %collective-permute-start.10) | collective-permute-done | bytes 262176 | tf_op jit(solution)/shard_map/ppermute | solution.py:58
  56.0 3.0 %collective-permute-done.8 = bf16[256,1024]{1,0:T(8,128)(2,1)S(1)} collective-permute-done((bf16[256,1024]{1,0:T(8,128)(2,1)S(1)}, bf16[256,1024]{1,0:T(8,128)(2,1)S(1)}, u32[]{:S(2)}, u32[]{:S(2)}) %collective-permute-start.8) | collective-permute-done | bytes 524320 | tf_op jit(solution)/shard_map/ppermute | solution.py:58
  59.0 0.1 slice_select_fusion
  59.1 0.0 copy-done.1
  59.1 1.3 %collective-permute-start.9 = (bf16[128,1024]{1,0:T(8,128)(2,1)S(1)}, bf16[128,1024]{1,0:T(8,128)(2,1)S(1)}, u32[]{:S(2)}, u32[]{:S(2)}) collective-permute-start(bf16[128,1024]{1,0:T(8,128)(2,1)S(1)} %get-tuple-element.32.refs_5_), channel_id=1, source_target_pairs={{0,4},{1,5},{4,8},{5,9},{8,12},{9,13},{12,16},{13,17},{16,20},{17,... | collective-permute-start | bytes 786440 | tf_op jit(solution)/shard_map/ppermute | solution.py:58
  60.4 4.9 %shard_map.56 = (f32[4,128,512]{2,1,0:T(8,128)S(1)}, f32[8,512]{1,0:T(8,128)S(1)}, f32[4,128,512]{2,1,0:T(8,128)S(1)}, f32[8,512]{1,0:T(8,128)S(1)}) custom-call(s32[2]{0:T(128)S(1)} %pad_add_fusion.where_ref, s32[512]{0:T(512)S(1)} %copy-done.2, s32[512]{0:T(512)S(1)} %copy-done.3, bf16[128,2048]{1,0:T(8,128)(2,1)S(1)} %copy-done, ...), custom_call_target="tpu_custom_call" | custom-call | flops 1073741824 | bytes 1048576 | tf_op jit(solution)/shard_map/pallas_call | solution.py:212
  65.3 0.0 collective-permute-done.7
  65.3 0.0 collective-permute-done.9
  65.4 1.4 %shard_map.58 = bf16[544,512]{1,0:T(8,128)(2,1)S(1)} custom-call(s32[2]{0:T(128)S(1)} %pad_add_fusion.where_ref, s32[512]{0:T(512)S(1)} %copy-done.2, s32[512]{0:T(512)S(1)} %copy-done.3, bf16[128,2048]{1,0:T(8,128)(2,1)S(1)} %collective-permute-done.5.refs_1_.refs_0_, bf16[128,1024]{1,0:T(8,128)(2,1)S(1)} %broadcast_select_fusion.refs_1_, ...), custom_call_target="tpu_custom_call" | custom-call | flops 134217728 | bytes 1048576 | tf_op jit(solution)/shard_map/pallas_call | solution.py:212
  66.8 8.6 %collective-permute-start.11 = (bf16[544,512]{1,0:T(8,128)(2,1)S(1)}, bf16[544,512]{1,0:T(8,128)(2,1)S(1)}, u32[]{:S(2)}, u32[]{:S(2)}) collective-permute-start(bf16[544,512]{1,0:T(8,128)(2,1)S(1)} %shard_map.58), channel_id=1, source_target_pairs={{0,1},{1,0},{4,5},{5,4},{8,9},{9,8},{12,13},{13,12},{16,17},{17,16... | collective-permute-start | bytes 1671176 | tf_op jit(solution)/shard_map/ppermute | solution.py:58
  75.4 1.4 %shard_map.57 = (f32[4,128,512]{2,1,0:T(8,128)S(1)}, f32[8,512]{1,0:T(8,128)S(1)}) custom-call(s32[2]{0:T(128)S(1)} %pad_add_fusion.where_ref, s32[512]{0:T(512)S(1)} %copy-done.2, s32[512]{0:T(512)S(1)} %copy-done.3, bf16[128,2048]{1,0:T(8,128)(2,1)S(1)} %copy-done, bf16[128,1024]{1,0:T(8,128)(2,1)S(1)} %broadcast_select_fusion.refs_1_, ...), custom_call_target="tpu_custom_call" | custom-call | flops 134217728 | bytes 1048576 | tf_op jit(solution)/shard_map/pallas_call | solution.py:212
  76.8 0.2 collective-permute-done.11.got_ref
  77.0 1.1 %shard_map.59 = bf16[128,2048]{1,0:T(8,128)(2,1)} custom-call(f32[4,128,512]{2,1,0:T(8,128)S(1)} %get-tuple-element.27.acc_ref, f32[8,512]{1,0:T(8,128)S(1)} %get-tuple-element.28.stat_ref, bf16[544,512]{1,0:T(8,128)(2,1)S(1)} %collective-permute-done.11.got_ref), custom_call_target="tpu_custom_call" | custom-call | flops 1048576 | bytes 3145728 | tf_op jit(solution)/shard_map/pallas_call | solution.py:225
  (4 shorter events, 0.1 us)
Async XLA Ops:
  0.0 1.0 %copy-start.4 = (bf16[128,512]{1,0:T(8,128)(2,1)S(1)}, bf16[128,512]{1,0:T(8,128)(2,1)}, u32[]{:S(2)}) copy-start(bf16[128,512]{1,0:T(8,128)(2,1)} %param.7) | copy-start | bytes 393220
  1.0 22.6 %collective-permute-start.1 = (bf16[128,1024]{1,0:T(8,128)(2,1)S(1)}, bf16[128,1024]{1,0:T(8,128)(2,1)S(1)}, u32[]{:S(2)}, u32[]{:S(2)}) collective-permute-start(bf16[128,1024]{1,0:T(8,128)(2,1)S(1)} %constant_dynamic-update-slice_fusion.refs_2_), channel_id=1, source_target_pairs={{0,4},{1,5},{4,8},{5,9},{8,12},{9,13},{12,16},{13,17},{16,20},{17,... | collective-permute-start | bytes 786440 | tf_op jit(solution)/shard_map/ppermute | solution.py:58
  5.8 22.3 %collective-permute-start = (bf16[128,1024]{1,0:T(8,128)(2,1)S(1)}, bf16[128,1024]{1,0:T(8,128)(2,1)S(1)}, u32[]{:S(2)}, u32[]{:S(2)}) collective-permute-start(bf16[128,1024]{1,0:T(8,128)(2,1)S(1)} %constant_dynamic-update-slice_fusion.refs_2_), channel_id=1, source_target_pairs={{0,2},{1,3},{4,6},{5,7},{8,10},{9,11},{12,14},{13,15},{16,18},{17,... | collective-permute-start | bytes 786440 | tf_op jit(solution)/shard_map/ppermute | solution.py:58
  23.6 5.9 %collective-permute-start.3 = (bf16[128,1024]{1,0:T(8,128)(2,1)S(1)}, bf16[128,1024]{1,0:T(8,128)(2,1)S(1)}, u32[]{:S(2)}, u32[]{:S(2)}) collective-permute-start(bf16[128,1024]{1,0:T(8,128)(2,1)S(1)} %collective-permute-done.1.refs_4_), channel_id=1, source_target_pairs={{0,4},{1,5},{4,8},{5,9},{8,12},{9,13},{12,16},{13,17},{16,20},{17,... | collective-permute-start | bytes 786440 | tf_op jit(solution)/shard_map/ppermute | solution.py:58
  24.9 13.7 %collective-permute-start.5 = (bf16[128,2048]{1,0:T(8,128)(2,1)}, bf16[128,2048]{1,0:T(8,128)(2,1)S(1)}, u32[]{:S(2)}, u32[]{:S(2)}) collective-permute-start(bf16[128,2048]{1,0:T(8,128)(2,1)} %refs_0_.5), channel_id=1, source_target_pairs={{0,1},{1,0},{4,5},{5,4},{8,9},{9,8},{12,13},{13,12},{16,17},{17,16... | collective-permute-start | bytes 1572872 | tf_op jit(solution)/shard_map/ppermute | solution.py:58
  28.1 19.5 %collective-permute-start.2 = (bf16[256,1024]{1,0:T(8,128)(2,1)S(1)}, bf16[256,1024]{1,0:T(8,128)(2,1)S(1)}, u32[]{:S(2)}, u32[]{:S(2)}) collective-permute-start(bf16[256,1024]{1,0:T(8,128)(2,1)S(1)} %pad_maximum_fusion), channel_id=1, source_target_pairs={{28,32},{29,33},{60,64},{61,65},{92,96},{93,97},{124,130},{125,131... | collective-permute-start | bytes 1572872 | tf_op jit(solution)/shard_map/ppermute | solution.py:58
  29.5 7.8 %collective-permute-start.4 = (bf16[128,1024]{1,0:T(8,128)(2,1)S(1)}, bf16[128,1024]{1,0:T(8,128)(2,1)S(1)}, u32[]{:S(2)}, u32[]{:S(2)}) collective-permute-start(bf16[128,1024]{1,0:T(8,128)(2,1)S(1)} %collective-permute-done.refs_3_), channel_id=1, source_target_pairs={{0,4},{1,5},{4,8},{5,9},{8,12},{9,13},{12,16},{13,17},{16,20},{17,... | collective-permute-start | bytes 786440 | tf_op jit(solution)/shard_map/ppermute | solution.py:58
  33.7 4.9 %copy-start = (bf16[128,2048]{1,0:T(8,128)(2,1)S(1)}, bf16[128,2048]{1,0:T(8,128)(2,1)}, u32[]{:S(2)}) copy-start(bf16[128,2048]{1,0:T(8,128)(2,1)} %refs_0_.5) | copy-start | bytes 1572868
  33.7 4.9 %copy-start.2 = (s32[512]{0:T(512)S(1)}, s32[512]{0:T(512)}, u32[]{:S(2)}) copy-start(s32[512]{0:T(512)} %frame_ref.7) | copy-start | bytes 6148
  33.7 4.9 %copy-start.3 = (s32[512]{0:T(512)S(1)}, s32[512]{0:T(512)}, u32[]{:S(2)}) copy-start(s32[512]{0:T(512)} %count_ref.7) | copy-start | bytes 6148
  37.3 21.7 %collective-permute-start.8 = (bf16[256,1024]{1,0:T(8,128)(2,1)S(1)}, bf16[256,1024]{1,0:T(8,128)(2,1)S(1)}, u32[]{:S(2)}, u32[]{:S(2)}) collective-permute-start(bf16[256,1024]{1,0:T(8,128)(2,1)S(1)} %pad_maximum_fusion.1), channel_id=1, source_target_pairs={{28,32},{29,33},{60,64},{61,65},{92,96},{93,97},{124,130},{125,131... | collective-permute-start | bytes 1572872 | tf_op jit(solution)/shard_map/ppermute | solution.py:58
  42.0 17.1 %copy-start.1 = (f32[4,128,512]{2,1,0:T(8,128)}, f32[4,128,512]{2,1,0:T(8,128)S(1)}, u32[]{:S(2)}) copy-start(f32[4,128,512]{2,1,0:T(8,128)S(1)} %get-tuple-element.23.refs_8_) | copy-start | bytes 3145732
  47.7 4.6 %collective-permute-start.6 = (bf16[128,1024]{1,0:T(8,128)(2,1)S(1)}, bf16[128,1024]{1,0:T(8,128)(2,1)S(1)}, u32[]{:S(2)}, u32[]{:S(2)}) collective-permute-start(bf16[128,1024]{1,0:T(8,128)(2,1)S(1)} %get-tuple-element.21.refs_3_), channel_id=1, source_target_pairs={{0,4},{1,5},{4,8},{5,9},{8,12},{9,13},{12,16},{13,17},{16,20},{17,... | collective-permute-start | bytes 786440 | tf_op jit(solution)/shard_map/ppermute | solution.py:58
  49.0 7.0 %collective-permute-start.10 = (bf16[128,1024]{1,0:T(8,128)(2,1)S(1)}, bf16[128,1024]{1,0:T(8,128)(2,1)S(1)}, u32[]{:S(2)}, u32[]{:S(2)}) collective-permute-start(bf16[128,1024]{1,0:T(8,128)(2,1)S(1)} %get-tuple-element.33.refs_2_), channel_id=1, source_target_pairs={{0,4},{1,5},{4,8},{5,9},{8,12},{9,13},{12,16},{13,17},{16,20},{17,... | collective-permute-start | bytes 786440 | tf_op jit(solution)/shard_map/ppermute | solution.py:58
  52.3 13.0 %collective-permute-start.7 = (bf16[128,1024]{1,0:T(8,128)(2,1)S(1)}, bf16[128,1024]{1,0:T(8,128)(2,1)S(1)}, u32[]{:S(2)}, u32[]{:S(2)}) collective-permute-start(bf16[128,1024]{1,0:T(8,128)(2,1)S(1)} %collective-permute-done.6), channel_id=1, source_target_pairs={{28,32},{29,33},{60,64},{61,65},{92,96},{93,97},{124,130},{125,131... | collective-permute-start | bytes 786440 | tf_op jit(solution)/shard_map/ppermute | solution.py:58
  59.1 6.2 %collective-permute-start.9 = (bf16[128,1024]{1,0:T(8,128)(2,1)S(1)}, bf16[128,1024]{1,0:T(8,128)(2,1)S(1)}, u32[]{:S(2)}, u32[]{:S(2)}) collective-permute-start(bf16[128,1024]{1,0:T(8,128)(2,1)S(1)} %get-tuple-element.32.refs_5_), channel_id=1, source_target_pairs={{0,4},{1,5},{4,8},{5,9},{8,12},{9,13},{12,16},{13,17},{16,20},{17,... | collective-permute-start | bytes 786440 | tf_op jit(solution)/shard_map/ppermute | solution.py:58
  66.8 10.2 %collective-permute-start.11 = (bf16[544,512]{1,0:T(8,128)(2,1)S(1)}, bf16[544,512]{1,0:T(8,128)(2,1)S(1)}, u32[]{:S(2)}, u32[]{:S(2)}) collective-permute-start(bf16[544,512]{1,0:T(8,128)(2,1)S(1)} %shard_map.58), channel_id=1, source_target_pairs={{0,1},{1,0},{4,5},{5,4},{8,9},{9,8},{12,13},{13,12},{16,17},{17,16... | collective-permute-start | bytes 1671176 | tf_op jit(solution)/shard_map/ppermute | solution.py:58

commit v4 on v3

--- a/solution.py
+++ b/solution.py
@@ -196,7 +196,7 @@
 
 IN_SMEM = pl.BlockSpec(memory_space=pltpu.SMEM)
 IN_VMEM = pl.BlockSpec(memory_space=pltpu.VMEM)
-PARAMS = pltpu.CompilerParams(vmem_limit_bytes=48 * 1024 * 1024)
+PARAMS = pltpu.CompilerParams(vmem_limit_bytes=20 * 1024 * 1024)
 
 
 def attend(tags, sets, state, tables, queries, pieces, sent=False):
@@ -255,8 +255,9 @@
     in_cross2 = inside(after(cross1, state[1]))
     in_near3 = inside(near2)
     on_cross3 = onward(in_cross2)
-    cross2, near3 = either(on_second[:rows], in_cross2), either(on_second[rows:], in_near3)
+    cross2 = either(on_second[:rows], in_cross2)
     in_cross3 = inside(cross2)
+    near3 = either(after(on_second, cross2)[rows:], in_near3)
     state = attend(((2, 0), (1, 1), (3, 0), (2, 1)), (0, 1), state, tables, both, (near2, cross1, near3, cross2))
     cross3 = either(on_cross3, in_cross3)
     got = moved(attend(((3, 1),), (1,), state[2:], tables, both[1:], (cross3,), True), other_core)

time: 78.5 us -> 78.4 us (level)
  transfers between devices with their start and end apart: 12 -> 12, of which waited for: 7 -> 7; matrix products, arithmetic and copies ran while one was open for 0% -> 0% of each run, Pallas kernels for 12% -> 11%
where the time goes in v4:
time: 78.4 us; the launch traced here: 78.1 us
  starting transfers between devices  37.7 us (48%)
  waiting for transfers between devices  27.4 us (35%)
  Pallas kernels  11.5 us (15%)
  local copies, waits for them, and re-layouts  0.98 us (1%)
    ppermute x12, starting transfers between devices, moved(): lax.ppermute(value, AXES, [(flat(p), flat(target(p))) for p in places() i...  37.7 us
    ppermute x12, waiting for transfers between devices, moved(): lax.ppermute(value, AXES, [(flat(p), flat(target(p))) for p in places() i...  27.4 us
    pallas_call x4, Pallas kernels, attend(): pl.pallas_call(functools.partial(attend_kernel, tags, sets, state is None...  10.3 us
  transfers between devices with their start and end apart: 12, of which 7 were waited for; matrix products, arithmetic and copies ran while one was open for 0% of the time, Pallas kernels for 11%

profile of v4, /device:TPU:1, one launch (start us, length us, event | category | flops | bytes accessed | tf_op | source)
XLA Modules:
  0.0 78.1 jit_solution(16538198562716935992)
XLA Ops:
  0.0 0.0 copy-start.3
  0.0 0.9 %constant_dynamic-update-slice_fusion.1 = bf16[128,1024]{1,0:T(8,128)(2,1)S(1)} fusion(bf16[128,512]{1,0:T(8,128)(2,1)} %param.6), kind=kLoop, calls=%fused_computation.8 | loop fusion | bytes 262144
  1.0 0.0 copy-done.3
  1.0 4.8 %collective-permute-start.1 = (bf16[128,1024]{1,0:T(8,128)(2,1)S(1)}, bf16[128,1024]{1,0:T(8,128)(2,1)S(1)}, u32[]{:S(2)}, u32[]{:S(2)}) collective-permute-start(bf16[128,1024]{1,0:T(8,128)(2,1)S(1)} %constant_dynamic-update-slice_fusion.refs_2_), channel_id=1, source_target_pairs={{0,4},{1,5},{4,8},{5,9},{8,12},{9,13},{12,16},{13,17},{16,20},{17,... | collective-permute-start | bytes 786440 | tf_op jit(solution)/shard_map/ppermute | solution.py:58
  5.8 7.5 %collective-permute-start = (bf16[128,1024]{1,0:T(8,128)(2,1)S(1)}, bf16[128,1024]{1,0:T(8,128)(2,1)S(1)}, u32[]{:S(2)}, u32[]{:S(2)}) collective-permute-start(bf16[128,1024]{1,0:T(8,128)(2,1)S(1)} %constant_dynamic-update-slice_fusion.refs_2_), channel_id=1, source_target_pairs={{0,2},{1,3},{4,6},{5,7},{8,10},{9,11},{12,14},{13,15},{16,18},{17,... | collective-permute-start | bytes 786440 | tf_op jit(solution)/shard_map/ppermute | solution.py:58
  13.3 10.3 %collective-permute-done.1.refs_4_ = bf16[128,1024]{1,0:T(8,128)(2,1)S(1)} collective-permute-done((bf16[128,1024]{1,0:T(8,128)(2,1)S(1)}, bf16[128,1024]{1,0:T(8,128)(2,1)S(1)}, u32[]{:S(2)}, u32[]{:S(2)}) %collective-permute-start.1) | collective-permute-done | bytes 262176 | tf_op jit(solution)/shard_map/ppermute | solution.py:58
  23.6 1.3 %collective-permute-start.3 = (bf16[128,1024]{1,0:T(8,128)(2,1)S(1)}, bf16[128,1024]{1,0:T(8,128)(2,1)S(1)}, u32[]{:S(2)}, u32[]{:S(2)}) collective-permute-start(bf16[128,1024]{1,0:T(8,128)(2,1)S(1)} %collective-permute-done.1.refs_4_), channel_id=1, source_target_pairs={{0,4},{1,5},{4,8},{5,9},{8,12},{9,13},{12,16},{13,17},{16,20},{17,... | collective-permute-start | bytes 786440 | tf_op jit(solution)/shard_map/ppermute | solution.py:58
  24.9 3.2 %collective-permute-start.5 = (bf16[128,2048]{1,0:T(8,128)(2,1)}, bf16[128,2048]{1,0:T(8,128)(2,1)S(1)}, u32[]{:S(2)}, u32[]{:S(2)}) collective-permute-start(bf16[128,2048]{1,0:T(8,128)(2,1)} %refs_0_.5), channel_id=1, source_target_pairs={{0,1},{1,0},{4,5},{5,4},{8,9},{9,8},{12,13},{13,12},{16,17},{17,16... | collective-permute-start | bytes 1572872 | tf_op jit(solution)/shard_map/ppermute | solution.py:58
  28.1 0.0 collective-permute-done.refs_3_
  28.1 1.3 %collective-permute-start.2 = (bf16[256,1024]{1,0:T(8,128)(2,1)S(1)}, bf16[256,1024]{1,0:T(8,128)(2,1)S(1)}, u32[]{:S(2)}, u32[]{:S(2)}) collective-permute-start(bf16[256,1024]{1,0:T(8,128)(2,1)S(1)} %pad_maximum_fusion), channel_id=1, source_target_pairs={{28,32},{29,33},{60,64},{61,65},{92,96},{93,97},{124,130},{125,131... | collective-permute-start | bytes 1572872 | tf_op jit(solution)/shard_map/ppermute | solution.py:58
  29.4 0.0 collective-permute-done.3
  29.5 4.1 %collective-permute-start.4 = (bf16[128,1024]{1,0:T(8,128)(2,1)S(1)}, bf16[128,1024]{1,0:T(8,128)(2,1)S(1)}, u32[]{:S(2)}, u32[]{:S(2)}) collective-permute-start(bf16[128,1024]{1,0:T(8,128)(2,1)S(1)} %collective-permute-done.refs_3_), channel_id=1, source_target_pairs={{0,4},{1,5},{4,8},{5,9},{8,12},{9,13},{12,16},{13,17},{16,20},{17,... | collective-permute-start | bytes 786440 | tf_op jit(solution)/shard_map/ppermute | solution.py:58
  33.6 0.1 pad_add_fusion.where_ref
  33.7 0.0 copy-start
  33.7 0.0 copy-start.1
  33.7 0.0 copy-start.2
  33.7 3.6 %collective-permute-done.4 = bf16[128,1024]{1,0:T(8,128)(2,1)S(1)} collective-permute-done((bf16[128,1024]{1,0:T(8,128)(2,1)S(1)}, bf16[128,1024]{1,0:T(8,128)(2,1)S(1)}, u32[]{:S(2)}, u32[]{:S(2)}) %collective-permute-start.4) | collective-permute-done | bytes 262176 | tf_op jit(solution)/shard_map/ppermute | solution.py:58
  37.3 1.3 %collective-permute-start.8 = (bf16[256,1024]{1,0:T(8,128)(2,1)S(1)}, bf16[256,1024]{1,0:T(8,128)(2,1)S(1)}, u32[]{:S(2)}, u32[]{:S(2)}) collective-permute-start(bf16[256,1024]{1,0:T(8,128)(2,1)S(1)} %pad_maximum_fusion.1), channel_id=1, source_target_pairs={{28,32},{29,33},{60,64},{61,65},{92,96},{93,97},{124,130},{125,131... | collective-permute-start | bytes 1572872 | tf_op jit(solution)/shard_map/ppermute | solution.py:58
  38.6 0.0 collective-permute-done.5.refs_1_.refs_0_
  38.6 0.0 copy-done
  38.6 0.0 copy-done.1
  38.6 0.0 copy-done.2
  38.6 3.3 %shard_map.55 = (f32[4,128,512]{2,1,0:T(8,128)S(1)}, f32[8,512]{1,0:T(8,128)S(1)}, f32[4,128,512]{2,1,0:T(8,128)S(1)}, f32[8,512]{1,0:T(8,128)S(1)}) custom-call(s32[2]{0:T(128)S(1)} %pad_add_fusion.where_ref, s32[512]{0:T(512)S(1)} %copy-done.1, s32[512]{0:T(512)S(1)} %copy-done.2, bf16[128,2048]{1,0:T(8,128)(2,1)S(1)} %copy-done, ...), custom_call_target="tpu_custom_call" | custom-call | flops 805306368 | bytes 1048576 | tf_op jit(solution)/shard_map/pallas_call | solution.py:212
  42.0 5.7 %collective-permute-done.2 = bf16[256,1024]{1,0:T(8,128)(2,1)S(1)} collective-permute-done((bf16[256,1024]{1,0:T(8,128)(2,1)S(1)}, bf16[256,1024]{1,0:T(8,128)(2,1)S(1)}, u32[]{:S(2)}, u32[]{:S(2)}) %collective-permute-start.2) | collective-permute-done | bytes 524320 | tf_op jit(solution)/shard_map/ppermute | solution.py:58
  47.6 0.1 slice_select_fusion
  47.7 1.3 %collective-permute-start.6 = (bf16[128,1024]{1,0:T(8,128)(2,1)S(1)}, bf16[128,1024]{1,0:T(8,128)(2,1)S(1)}, u32[]{:S(2)}, u32[]{:S(2)}) collective-permute-start(bf16[128,1024]{1,0:T(8,128)(2,1)S(1)} %get-tuple-element.22.refs_3_), channel_id=1, source_target_pairs={{0,4},{1,5},{4,8},{5,9},{8,12},{9,13},{12,16},{13,17},{16,20},{17,... | collective-permute-start | bytes 786440 | tf_op jit(solution)/shard_map/ppermute | solution.py:58
  49.0 1.3 %collective-permute-start.10 = (bf16[128,1024]{1,0:T(8,128)(2,1)S(1)}, bf16[128,1024]{1,0:T(8,128)(2,1)S(1)}, u32[]{:S(2)}, u32[]{:S(2)}) collective-permute-start(bf16[128,1024]{1,0:T(8,128)(2,1)S(1)} %get-tuple-element.33.refs_2_), channel_id=1, source_target_pairs={{0,4},{1,5},{4,8},{5,9},{8,12},{9,13},{12,16},{13,17},{16,20},{17,... | collective-permute-start | bytes 786440 | tf_op jit(solution)/shard_map/ppermute | solution.py:58
  50.3 2.0 %collective-permute-done.6 = bf16[128,1024]{1,0:T(8,128)(2,1)S(1)} collective-permute-done((bf16[128,1024]{1,0:T(8,128)(2,1)S(1)}, bf16[128,1024]{1,0:T(8,128)(2,1)S(1)}, u32[]{:S(2)}, u32[]{:S(2)}) %collective-permute-start.6) | collective-permute-done | bytes 262176 | tf_op jit(solution)/shard_map/ppermute | solution.py:58
  52.3 1.3 %collective-permute-start.7 = (bf16[128,1024]{1,0:T(8,128)(2,1)S(1)}, bf16[128,1024]{1,0:T(8,128)(2,1)S(1)}, u32[]{:S(2)}, u32[]{:S(2)}) collective-permute-start(bf16[128,1024]{1,0:T(8,128)(2,1)S(1)} %collective-permute-done.6), channel_id=1, source_target_pairs={{28,32},{29,33},{60,64},{61,65},{92,96},{93,97},{124,130},{125,131... | collective-permute-start | bytes 786440 | tf_op jit(solution)/shard_map/ppermute | solution.py:58
  53.6 5.4 %collective-permute-done.8 = bf16[256,1024]{1,0:T(8,128)(2,1)S(1)} collective-permute-done((bf16[256,1024]{1,0:T(8,128)(2,1)S(1)}, bf16[256,1024]{1,0:T(8,128)(2,1)S(1)}, u32[]{:S(2)}, u32[]{:S(2)}) %collective-permute-start.8) | collective-permute-done | bytes 524320 | tf_op jit(solution)/shard_map/ppermute | solution.py:58
  59.1 1.3 %collective-permute-start.9 = (bf16[128,1024]{1,0:T(8,128)(2,1)S(1)}, bf16[128,1024]{1,0:T(8,128)(2,1)S(1)}, u32[]{:S(2)}, u32[]{:S(2)}) collective-permute-start(bf16[128,1024]{1,0:T(8,128)(2,1)S(1)} %slice_select_fusion.1.refs_5_), channel_id=1, source_target_pairs={{0,4},{1,5},{4,8},{5,9},{8,12},{9,13},{12,16},{13,17},{16,20},{17,... | collective-permute-start | bytes 786440 | tf_op jit(solution)/shard_map/ppermute | solution.py:58
  60.4 0.0 collective-permute-done.10
  60.4 4.2 %shard_map.56 = (f32[4,128,512]{2,1,0:T(8,128)S(1)}, f32[8,512]{1,0:T(8,128)S(1)}, f32[4,128,512]{2,1,0:T(8,128)S(1)}, f32[8,512]{1,0:T(8,128)S(1)}) custom-call(s32[2]{0:T(128)S(1)} %pad_add_fusion.where_ref, s32[512]{0:T(512)S(1)} %copy-done.1, s32[512]{0:T(512)S(1)} %copy-done.2, bf16[128,2048]{1,0:T(8,128)(2,1)S(1)} %copy-done, ...), custom_call_target="tpu_custom_call" | custom-call | flops 1073741824 | bytes 1048576 | tf_op jit(solution)/shard_map/pallas_call | solution.py:212
  64.7 0.2 collective-permute-done.7
  64.8 0.0 collective-permute-done.9
  64.9 1.4 %shard_map.58 = bf16[544,512]{1,0:T(8,128)(2,1)S(1)} custom-call(s32[2]{0:T(128)S(1)} %pad_add_fusion.where_ref, s32[512]{0:T(512)S(1)} %copy-done.1, s32[512]{0:T(512)S(1)} %copy-done.2, bf16[128,2048]{1,0:T(8,128)(2,1)S(1)} %collective-permute-done.5.refs_1_.refs_0_, bf16[128,1024]{1,0:T(8,128)(2,1)S(1)} %broadcast_select_fusion.refs_1_, ...), custom_call_target="tpu_custom_call" | custom-call | flops 134217728 | bytes 1048576 | tf_op jit(solution)/shard_map/pallas_call | solution.py:212
  66.3 9.1 %collective-permute-start.11 = (bf16[544,512]{1,0:T(8,128)(2,1)S(1)}, bf16[544,512]{1,0:T(8,128)(2,1)S(1)}, u32[]{:S(2)}, u32[]{:S(2)}) collective-permute-start(bf16[544,512]{1,0:T(8,128)(2,1)S(1)} %shard_map.58), channel_id=1, source_target_pairs={{0,1},{1,0},{4,5},{5,4},{8,9},{9,8},{12,13},{13,12},{16,17},{17,16... | collective-permute-start | bytes 1671176 | tf_op jit(solution)/shard_map/ppermute | solution.py:58
  75.4 1.4 %shard_map.57 = (f32[4,128,512]{2,1,0:T(8,128)S(1)}, f32[8,512]{1,0:T(8,128)S(1)}) custom-call(s32[2]{0:T(128)S(1)} %pad_add_fusion.where_ref, s32[512]{0:T(512)S(1)} %copy-done.1, s32[512]{0:T(512)S(1)} %copy-done.2, bf16[128,2048]{1,0:T(8,128)(2,1)S(1)} %copy-done, bf16[128,1024]{1,0:T(8,128)(2,1)S(1)} %broadcast_select_fusion.refs_1_, ...), custom_call_target="tpu_custom_call" | custom-call | flops 134217728 | bytes 1048576 | tf_op jit(solution)/shard_map/pallas_call | solution.py:212
  76.8 0.2 collective-permute-done.11.got_ref
  77.0 1.1 %shard_map.59 = bf16[128,2048]{1,0:T(8,128)(2,1)} custom-call(f32[4,128,512]{2,1,0:T(8,128)S(1)} %get-tuple-element.29.acc_ref, f32[8,512]{1,0:T(8,128)S(1)} %get-tuple-element.30.stat_ref, bf16[544,512]{1,0:T(8,128)(2,1)S(1)} %collective-permute-done.11.got_ref), custom_call_target="tpu_custom_call" | custom-call | flops 1048576 | bytes 3145728 | tf_op jit(solution)/shard_map/pallas_call | solution.py:225
  (6 shorter events, 0.2 us)
Async XLA Ops:
  0.0 1.0 %copy-start.3 = (bf16[128,512]{1,0:T(8,128)(2,1)S(1)}, bf16[128,512]{1,0:T(8,128)(2,1)}, u32[]{:S(2)}) copy-start(bf16[128,512]{1,0:T(8,128)(2,1)} %param.7) | copy-start | bytes 393220
  1.0 22.6 %collective-permute-start.1 = (bf16[128,1024]{1,0:T(8,128)(2,1)S(1)}, bf16[128,1024]{1,0:T(8,128)(2,1)S(1)}, u32[]{:S(2)}, u32[]{:S(2)}) collective-permute-start(bf16[128,1024]{1,0:T(8,128)(2,1)S(1)} %constant_dynamic-update-slice_fusion.refs_2_), channel_id=1, source_target_pairs={{0,4},{1,5},{4,8},{5,9},{8,12},{9,13},{12,16},{13,17},{16,20},{17,... | collective-permute-start | bytes 786440 | tf_op jit(solution)/shard_map/ppermute | solution.py:58
  5.8 22.3 %collective-permute-start = (bf16[128,1024]{1,0:T(8,128)(2,1)S(1)}, bf16[128,1024]{1,0:T(8,128)(2,1)S(1)}, u32[]{:S(2)}, u32[]{:S(2)}) collective-permute-start(bf16[128,1024]{1,0:T(8,128)(2,1)S(1)} %constant_dynamic-update-slice_fusion.refs_2_), channel_id=1, source_target_pairs={{0,2},{1,3},{4,6},{5,7},{8,10},{9,11},{12,14},{13,15},{16,18},{17,... | collective-permute-start | bytes 786440 | tf_op jit(solution)/shard_map/ppermute | solution.py:58
  23.6 5.9 %collective-permute-start.3 = (bf16[128,1024]{1,0:T(8,128)(2,1)S(1)}, bf16[128,1024]{1,0:T(8,128)(2,1)S(1)}, u32[]{:S(2)}, u32[]{:S(2)}) collective-permute-start(bf16[128,1024]{1,0:T(8,128)(2,1)S(1)} %collective-permute-done.1.refs_4_), channel_id=1, source_target_pairs={{0,4},{1,5},{4,8},{5,9},{8,12},{9,13},{12,16},{13,17},{16,20},{17,... | collective-permute-start | bytes 786440 | tf_op jit(solution)/shard_map/ppermute | solution.py:58
  24.9 13.7 %collective-permute-start.5 = (bf16[128,2048]{1,0:T(8,128)(2,1)}, bf16[128,2048]{1,0:T(8,128)(2,1)S(1)}, u32[]{:S(2)}, u32[]{:S(2)}) collective-permute-start(bf16[128,2048]{1,0:T(8,128)(2,1)} %refs_0_.5), channel_id=1, source_target_pairs={{0,1},{1,0},{4,5},{5,4},{8,9},{9,8},{12,13},{13,12},{16,17},{17,16... | collective-permute-start | bytes 1572872 | tf_op jit(solution)/shard_map/ppermute | solution.py:58
  28.1 19.5 %collective-permute-start.2 = (bf16[256,1024]{1,0:T(8,128)(2,1)S(1)}, bf16[256,1024]{1,0:T(8,128)(2,1)S(1)}, u32[]{:S(2)}, u32[]{:S(2)}) collective-permute-start(bf16[256,1024]{1,0:T(8,128)(2,1)S(1)} %pad_maximum_fusion), channel_id=1, source_target_pairs={{28,32},{29,33},{60,64},{61,65},{92,96},{93,97},{124,130},{125,131... | collective-permute-start | bytes 1572872 | tf_op jit(solution)/shard_map/ppermute | solution.py:58
  29.5 7.8 %collective-permute-start.4 = (bf16[128,1024]{1,0:T(8,128)(2,1)S(1)}, bf16[128,1024]{1,0:T(8,128)(2,1)S(1)}, u32[]{:S(2)}, u32[]{:S(2)}) collective-permute-start(bf16[128,1024]{1,0:T(8,128)(2,1)S(1)} %collective-permute-done.refs_3_), channel_id=1, source_target_pairs={{0,4},{1,5},{4,8},{5,9},{8,12},{9,13},{12,16},{13,17},{16,20},{17,... | collective-permute-start | bytes 786440 | tf_op jit(solution)/shard_map/ppermute | solution.py:58
  33.7 4.9 %copy-start = (bf16[128,2048]{1,0:T(8,128)(2,1)S(1)}, bf16[128,2048]{1,0:T(8,128)(2,1)}, u32[]{:S(2)}) copy-start(bf16[128,2048]{1,0:T(8,128)(2,1)} %refs_0_.5) | copy-start | bytes 1572868
  33.7 4.9 %copy-start.1 = (s32[512]{0:T(512)S(1)}, s32[512]{0:T(512)}, u32[]{:S(2)}) copy-start(s32[512]{0:T(512)} %frame_ref.7) | copy-start | bytes 6148
  33.7 4.9 %copy-start.2 = (s32[512]{0:T(512)S(1)}, s32[512]{0:T(512)}, u32[]{:S(2)}) copy-start(s32[512]{0:T(512)} %count_ref.7) | copy-start | bytes 6148
  37.3 21.7 %collective-permute-start.8 = (bf16[256,1024]{1,0:T(8,128)(2,1)S(1)}, bf16[256,1024]{1,0:T(8,128)(2,1)S(1)}, u32[]{:S(2)}, u32[]{:S(2)}) collective-permute-start(bf16[256,1024]{1,0:T(8,128)(2,1)S(1)} %pad_maximum_fusion.1), channel_id=1, source_target_pairs={{28,32},{29,33},{60,64},{61,65},{92,96},{93,97},{124,130},{125,131... | collective-permute-start | bytes 1572872 | tf_op jit(solution)/shard_map/ppermute | solution.py:58
  47.7 4.6 %collective-permute-start.6 = (bf16[128,1024]{1,0:T(8,128)(2,1)S(1)}, bf16[128,1024]{1,0:T(8,128)(2,1)S(1)}, u32[]{:S(2)}, u32[]{:S(2)}) collective-permute-start(bf16[128,1024]{1,0:T(8,128)(2,1)S(1)} %get-tuple-element.22.refs_3_), channel_id=1, source_target_pairs={{0,4},{1,5},{4,8},{5,9},{8,12},{9,13},{12,16},{13,17},{16,20},{17,... | collective-permute-start | bytes 786440 | tf_op jit(solution)/shard_map/ppermute | solution.py:58
  49.0 11.4 %collective-permute-start.10 = (bf16[128,1024]{1,0:T(8,128)(2,1)S(1)}, bf16[128,1024]{1,0:T(8,128)(2,1)S(1)}, u32[]{:S(2)}, u32[]{:S(2)}) collective-permute-start(bf16[128,1024]{1,0:T(8,128)(2,1)S(1)} %get-tuple-element.33.refs_2_), channel_id=1, source_target_pairs={{0,4},{1,5},{4,8},{5,9},{8,12},{9,13},{12,16},{13,17},{16,20},{17,... | collective-permute-start | bytes 786440 | tf_op jit(solution)/shard_map/ppermute | solution.py:58
  52.3 12.5 %collective-permute-start.7 = (bf16[128,1024]{1,0:T(8,128)(2,1)S(1)}, bf16[128,1024]{1,0:T(8,128)(2,1)S(1)}, u32[]{:S(2)}, u32[]{:S(2)}) collective-permute-start(bf16[128,1024]{1,0:T(8,128)(2,1)S(1)} %collective-permute-done.6), channel_id=1, source_target_pairs={{28,32},{29,33},{60,64},{61,65},{92,96},{93,97},{124,130},{125,131... | collective-permute-start | bytes 786440 | tf_op jit(solution)/shard_map/ppermute | solution.py:58
  59.1 5.8 %collective-permute-start.9 = (bf16[128,1024]{1,0:T(8,128)(2,1)S(1)}, bf16[128,1024]{1,0:T(8,128)(2,1)S(1)}, u32[]{:S(2)}, u32[]{:S(2)}) collective-permute-start(bf16[128,1024]{1,0:T(8,128)(2,1)S(1)} %slice_select_fusion.1.refs_5_), channel_id=1, source_target_pairs={{0,4},{1,5},{4,8},{5,9},{8,12},{9,13},{12,16},{13,17},{16,20},{17,... | collective-permute-start | bytes 786440 | tf_op jit(solution)/shard_map/ppermute | solution.py:58
  66.3 10.6 %collective-permute-start.11 = (bf16[544,512]{1,0:T(8,128)(2,1)S(1)}, bf16[544,512]{1,0:T(8,128)(2,1)S(1)}, u32[]{:S(2)}, u32[]{:S(2)}) collective-permute-start(bf16[544,512]{1,0:T(8,128)(2,1)S(1)} %shard_map.58), channel_id=1, source_target_pairs={{0,1},{1,0},{4,5},{5,4},{8,9},{9,8},{12,13},{13,12},{16,17},{17,16... | collective-permute-start | bytes 1671176 | tf_op jit(solution)/shard_map/ppermute | solution.py:58

commit v5 on v4

--- a/solution.py
+++ b/solution.py
@@ -157,15 +157,20 @@
             states_out[2 * i + 1][c:c + 1, :] = top
             states_out[2 * i + 1][kv_heads + c:kv_heads + c + 1, :] = total
 
-    scores = score(*todo[0])
-    before = None
-    for n, item in enumerate(todo):
-        following = score(*todo[n + 1]) if n + 1 < len(todo) else None
-        done = weigh(*item, scores)
-        if before is not None:
-            gather(*todo[n - 1], *before)
-        scores, before = following, done
-    gather(*todo[-1], *before)
+    if len(todo) <= kv_heads:
+        weighed = [weigh(*item, scores) for item, scores in [(item, score(*item)) for item in todo]]
+        for item, done in zip(todo, weighed):
+            gather(*item, *done)
+    else:
+        scores = score(*todo[0])
+        before = None
+        for n, item in enumerate(todo):
+            following = score(*todo[n + 1]) if n + 1 < len(todo) else None
+            done = weigh(*item, scores)
+            if before is not None:
+                gather(*todo[n - 1], *before)
+            scores, before = following, done
+        gather(*todo[-1], *before)
     if sent:
         rest = jnp.concatenate([top for top, _ in stats] + [total for _, total in stats], axis=0)
         parts = []
@@ -188,9 +193,10 @@
         mine, theirs = jnp.exp2((top - most) * SCALE), jnp.exp2((got_top - most) * SCALE)
         share = 1.0 / (total * mine + got_total * theirs)
         result = acc_ref[c] * (mine * share) + got_ref[c * HEAD_DIM:(c + 1) * HEAD_DIM, :].astype(jnp.float32) * (theirs * share)
+        result = result.astype(jnp.bfloat16)
         for r in range(GROUP):
             out_ref[:, (GROUP * c + r) * HEAD_DIM:(GROUP * c + r + 1) * HEAD_DIM] = (
-                result[:, r * FRAME_TOK:(r + 1) * FRAME_TOK].T.astype(jnp.bfloat16)
+                result[:, r * FRAME_TOK:(r + 1) * FRAME_TOK].T
             )
 
 

time: 78.4 us -> 78.3 us (level)
  no operation moved by 1% of the time
where the time goes in v5:
time: 78.3 us; the launch traced here: 77.9 us
  starting transfers between devices  37.7 us (48%)
  waiting for transfers between devices  27.4 us (35%)
  Pallas kernels  11.3 us (14%)
  local copies, waits for them, and re-layouts  0.98 us (1%)
    ppermute x12, starting transfers between devices, moved(): lax.ppermute(value, AXES, [(flat(p), flat(target(p))) for p in places() i...  37.7 us
    ppermute x12, waiting for transfers between devices, moved(): lax.ppermute(value, AXES, [(flat(p), flat(target(p))) for p in places() i...  27.4 us
    pallas_call x4, Pallas kernels, attend(): pl.pallas_call(functools.partial(attend_kernel, tags, sets, state is None...  10.2 us
  transfers between devices with their start and end apart: 12, of which 7 were waited for; matrix products, arithmetic and copies ran while one was open for 0% of the time, Pallas kernels for 11%

profile of v5, /device:TPU:1, one launch (start us, length us, event | category | flops | bytes accessed | tf_op | source)
XLA Modules:
  0.0 77.9 jit_solution(16657622586329873538)
XLA Ops:
  0.0 0.0 copy-start.3
  0.0 0.9 %constant_dynamic-update-slice_fusion.1 = bf16[128,1024]{1,0:T(8,128)(2,1)S(1)} fusion(bf16[128,512]{1,0:T(8,128)(2,1)} %param.6), kind=kLoop, calls=%fused_computation.8 | loop fusion | bytes 262144
  1.0 0.0 copy-done.3
  1.0 4.8 %collective-permute-start.1 = (bf16[128,1024]{1,0:T(8,128)(2,1)S(1)}, bf16[128,1024]{1,0:T(8,128)(2,1)S(1)}, u32[]{:S(2)}, u32[]{:S(2)}) collective-permute-start(bf16[128,1024]{1,0:T(8,128)(2,1)S(1)} %constant_dynamic-update-slice_fusion.refs_2_), channel_id=1, source_target_pairs={{0,4},{1,5},{4,8},{5,9},{8,12},{9,13},{12,16},{13,17},{16,20},{17,... | collective-permute-start | bytes 786440 | tf_op jit(solution)/shard_map/ppermute | solution.py:58
  5.8 7.5 %collective-permute-start = (bf16[128,1024]{1,0:T(8,128)(2,1)S(1)}, bf16[128,1024]{1,0:T(8,128)(2,1)S(1)}, u32[]{:S(2)}, u32[]{:S(2)}) collective-permute-start(bf16[128,1024]{1,0:T(8,128)(2,1)S(1)} %constant_dynamic-update-slice_fusion.refs_2_), channel_id=1, source_target_pairs={{0,2},{1,3},{4,6},{5,7},{8,10},{9,11},{12,14},{13,15},{16,18},{17,... | collective-permute-start | bytes 786440 | tf_op jit(solution)/shard_map/ppermute | solution.py:58
  13.3 10.3 %collective-permute-done.1.refs_4_ = bf16[128,1024]{1,0:T(8,128)(2,1)S(1)} collective-permute-done((bf16[128,1024]{1,0:T(8,128)(2,1)S(1)}, bf16[128,1024]{1,0:T(8,128)(2,1)S(1)}, u32[]{:S(2)}, u32[]{:S(2)}) %collective-permute-start.1) | collective-permute-done | bytes 262176 | tf_op jit(solution)/shard_map/ppermute | solution.py:58
  23.6 1.3 %collective-permute-start.3 = (bf16[128,1024]{1,0:T(8,128)(2,1)S(1)}, bf16[128,1024]{1,0:T(8,128)(2,1)S(1)}, u32[]{:S(2)}, u32[]{:S(2)}) collective-permute-start(bf16[128,1024]{1,0:T(8,128)(2,1)S(1)} %collective-permute-done.1.refs_4_), channel_id=1, source_target_pairs={{0,4},{1,5},{4,8},{5,9},{8,12},{9,13},{12,16},{13,17},{16,20},{17,... | collective-permute-start | bytes 786440 | tf_op jit(solution)/shard_map/ppermute | solution.py:58
  24.9 3.2 %collective-permute-start.5 = (bf16[128,2048]{1,0:T(8,128)(2,1)}, bf16[128,2048]{1,0:T(8,128)(2,1)S(1)}, u32[]{:S(2)}, u32[]{:S(2)}) collective-permute-start(bf16[128,2048]{1,0:T(8,128)(2,1)} %refs_0_.5), channel_id=1, source_target_pairs={{0,1},{1,0},{4,5},{5,4},{8,9},{9,8},{12,13},{13,12},{16,17},{17,16... | collective-permute-start | bytes 1572872 | tf_op jit(solution)/shard_map/ppermute | solution.py:58
  28.1 0.0 collective-permute-done.refs_3_
  28.1 1.3 %collective-permute-start.2 = (bf16[256,1024]{1,0:T(8,128)(2,1)S(1)}, bf16[256,1024]{1,0:T(8,128)(2,1)S(1)}, u32[]{:S(2)}, u32[]{:S(2)}) collective-permute-start(bf16[256,1024]{1,0:T(8,128)(2,1)S(1)} %pad_maximum_fusion), channel_id=1, source_target_pairs={{28,32},{29,33},{60,64},{61,65},{92,96},{93,97},{124,130},{125,131... | collective-permute-start | bytes 1572872 | tf_op jit(solution)/shard_map/ppermute | solution.py:58
  29.4 0.0 collective-permute-done.3
  29.5 4.1 %collective-permute-start.4 = (bf16[128,1024]{1,0:T(8,128)(2,1)S(1)}, bf16[128,1024]{1,0:T(8,128)(2,1)S(1)}, u32[]{:S(2)}, u32[]{:S(2)}) collective-permute-start(bf16[128,1024]{1,0:T(8,128)(2,1)S(1)} %collective-permute-done.refs_3_), channel_id=1, source_target_pairs={{0,4},{1,5},{4,8},{5,9},{8,12},{9,13},{12,16},{13,17},{16,20},{17,... | collective-permute-start | bytes 786440 | tf_op jit(solution)/shard_map/ppermute | solution.py:58
  33.6 0.1 pad_add_fusion.where_ref
  33.7 0.0 copy-start
  33.7 0.0 copy-start.1
  33.7 0.0 copy-start.2
  33.7 3.6 %collective-permute-done.4 = bf16[128,1024]{1,0:T(8,128)(2,1)S(1)} collective-permute-done((bf16[128,1024]{1,0:T(8,128)(2,1)S(1)}, bf16[128,1024]{1,0:T(8,128)(2,1)S(1)}, u32[]{:S(2)}, u32[]{:S(2)}) %collective-permute-start.4) | collective-permute-done | bytes 262176 | tf_op jit(solution)/shard_map/ppermute | solution.py:58
  37.3 1.3 %collective-permute-start.8 = (bf16[256,1024]{1,0:T(8,128)(2,1)S(1)}, bf16[256,1024]{1,0:T(8,128)(2,1)S(1)}, u32[]{:S(2)}, u32[]{:S(2)}) collective-permute-start(bf16[256,1024]{1,0:T(8,128)(2,1)S(1)} %pad_maximum_fusion.1), channel_id=1, source_target_pairs={{28,32},{29,33},{60,64},{61,65},{92,96},{93,97},{124,130},{125,131... | collective-permute-start | bytes 1572872 | tf_op jit(solution)/shard_map/ppermute | solution.py:58
  38.6 0.0 collective-permute-done.5.refs_1_.refs_0_
  38.6 0.0 copy-done
  38.6 0.0 copy-done.1
  38.6 0.0 copy-done.2
  38.6 3.3 %shard_map.55 = (f32[4,128,512]{2,1,0:T(8,128)S(1)}, f32[8,512]{1,0:T(8,128)S(1)}, f32[4,128,512]{2,1,0:T(8,128)S(1)}, f32[8,512]{1,0:T(8,128)S(1)}) custom-call(s32[2]{0:T(128)S(1)} %pad_add_fusion.where_ref, s32[512]{0:T(512)S(1)} %copy-done.1, s32[512]{0:T(512)S(1)} %copy-done.2, bf16[128,2048]{1,0:T(8,128)(2,1)S(1)} %copy-done, ...), custom_call_target="tpu_custom_call" | custom-call | flops 805306368 | bytes 1048576 | tf_op jit(solution)/shard_map/pallas_call | solution.py:218
  42.0 5.7 %collective-permute-done.2 = bf16[256,1024]{1,0:T(8,128)(2,1)S(1)} collective-permute-done((bf16[256,1024]{1,0:T(8,128)(2,1)S(1)}, bf16[256,1024]{1,0:T(8,128)(2,1)S(1)}, u32[]{:S(2)}, u32[]{:S(2)}) %collective-permute-start.2) | collective-permute-done | bytes 524320 | tf_op jit(solution)/shard_map/ppermute | solution.py:58
  47.6 0.1 slice_select_fusion
  47.7 1.3 %collective-permute-start.6 = (bf16[128,1024]{1,0:T(8,128)(2,1)S(1)}, bf16[128,1024]{1,0:T(8,128)(2,1)S(1)}, u32[]{:S(2)}, u32[]{:S(2)}) collective-permute-start(bf16[128,1024]{1,0:T(8,128)(2,1)S(1)} %get-tuple-element.22.refs_3_), channel_id=1, source_target_pairs={{0,4},{1,5},{4,8},{5,9},{8,12},{9,13},{12,16},{13,17},{16,20},{17,... | collective-permute-start | bytes 786440 | tf_op jit(solution)/shard_map/ppermute | solution.py:58
  49.0 1.3 %collective-permute-start.10 = (bf16[128,1024]{1,0:T(8,128)(2,1)S(1)}, bf16[128,1024]{1,0:T(8,128)(2,1)S(1)}, u32[]{:S(2)}, u32[]{:S(2)}) collective-permute-start(bf16[128,1024]{1,0:T(8,128)(2,1)S(1)} %get-tuple-element.33.refs_2_), channel_id=1, source_target_pairs={{0,4},{1,5},{4,8},{5,9},{8,12},{9,13},{12,16},{13,17},{16,20},{17,... | collective-permute-start | bytes 786440 | tf_op jit(solution)/shard_map/ppermute | solution.py:58
  50.3 2.0 %collective-permute-done.6 = bf16[128,1024]{1,0:T(8,128)(2,1)S(1)} collective-permute-done((bf16[128,1024]{1,0:T(8,128)(2,1)S(1)}, bf16[128,1024]{1,0:T(8,128)(2,1)S(1)}, u32[]{:S(2)}, u32[]{:S(2)}) %collective-permute-start.6) | collective-permute-done | bytes 262176 | tf_op jit(solution)/shard_map/ppermute | solution.py:58
  52.3 1.3 %collective-permute-start.7 = (bf16[128,1024]{1,0:T(8,128)(2,1)S(1)}, bf16[128,1024]{1,0:T(8,128)(2,1)S(1)}, u32[]{:S(2)}, u32[]{:S(2)}) collective-permute-start(bf16[128,1024]{1,0:T(8,128)(2,1)S(1)} %collective-permute-done.6), channel_id=1, source_target_pairs={{28,32},{29,33},{60,64},{61,65},{92,96},{93,97},{124,130},{125,131... | collective-permute-start | bytes 786440 | tf_op jit(solution)/shard_map/ppermute | solution.py:58
  53.6 5.4 %collective-permute-done.8 = bf16[256,1024]{1,0:T(8,128)(2,1)S(1)} collective-permute-done((bf16[256,1024]{1,0:T(8,128)(2,1)S(1)}, bf16[256,1024]{1,0:T(8,128)(2,1)S(1)}, u32[]{:S(2)}, u32[]{:S(2)}) %collective-permute-start.8) | collective-permute-done | bytes 524320 | tf_op jit(solution)/shard_map/ppermute | solution.py:58
  59.1 1.3 %collective-permute-start.9 = (bf16[128,1024]{1,0:T(8,128)(2,1)S(1)}, bf16[128,1024]{1,0:T(8,128)(2,1)S(1)}, u32[]{:S(2)}, u32[]{:S(2)}) collective-permute-start(bf16[128,1024]{1,0:T(8,128)(2,1)S(1)} %slice_select_fusion.1.refs_5_), channel_id=1, source_target_pairs={{0,4},{1,5},{4,8},{5,9},{8,12},{9,13},{12,16},{13,17},{16,20},{17,... | collective-permute-start | bytes 786440 | tf_op jit(solution)/shard_map/ppermute | solution.py:58
  60.4 0.0 collective-permute-done.10
  60.4 4.2 %shard_map.56 = (f32[4,128,512]{2,1,0:T(8,128)S(1)}, f32[8,512]{1,0:T(8,128)S(1)}, f32[4,128,512]{2,1,0:T(8,128)S(1)}, f32[8,512]{1,0:T(8,128)S(1)}) custom-call(s32[2]{0:T(128)S(1)} %pad_add_fusion.where_ref, s32[512]{0:T(512)S(1)} %copy-done.1, s32[512]{0:T(512)S(1)} %copy-done.2, bf16[128,2048]{1,0:T(8,128)(2,1)S(1)} %copy-done, ...), custom_call_target="tpu_custom_call" | custom-call | flops 1073741824 | bytes 1048576 | tf_op jit(solution)/shard_map/pallas_call | solution.py:218
  64.7 0.2 collective-permute-done.7
  64.8 0.0 collective-permute-done.9
  64.9 1.3 %shard_map.58 = bf16[544,512]{1,0:T(8,128)(2,1)S(1)} custom-call(s32[2]{0:T(128)S(1)} %pad_add_fusion.where_ref, s32[512]{0:T(512)S(1)} %copy-done.1, s32[512]{0:T(512)S(1)} %copy-done.2, bf16[128,2048]{1,0:T(8,128)(2,1)S(1)} %collective-permute-done.5.refs_1_.refs_0_, bf16[128,1024]{1,0:T(8,128)(2,1)S(1)} %broadcast_select_fusion.refs_1_, ...), custom_call_target="tpu_custom_call" | custom-call | flops 134217728 | bytes 1048576 | tf_op jit(solution)/shard_map/pallas_call | solution.py:218
  66.2 9.1 %collective-permute-start.11 = (bf16[544,512]{1,0:T(8,128)(2,1)S(1)}, bf16[544,512]{1,0:T(8,128)(2,1)S(1)}, u32[]{:S(2)}, u32[]{:S(2)}) collective-permute-start(bf16[544,512]{1,0:T(8,128)(2,1)S(1)} %shard_map.58), channel_id=1, source_target_pairs={{0,1},{1,0},{4,5},{5,4},{8,9},{9,8},{12,13},{13,12},{16,17},{17,16... | collective-permute-start | bytes 1671176 | tf_op jit(solution)/shard_map/ppermute | solution.py:58
  75.3 1.3 %shard_map.57 = (f32[4,128,512]{2,1,0:T(8,128)S(1)}, f32[8,512]{1,0:T(8,128)S(1)}) custom-call(s32[2]{0:T(128)S(1)} %pad_add_fusion.where_ref, s32[512]{0:T(512)S(1)} %copy-done.1, s32[512]{0:T(512)S(1)} %copy-done.2, bf16[128,2048]{1,0:T(8,128)(2,1)S(1)} %copy-done, bf16[128,1024]{1,0:T(8,128)(2,1)S(1)} %broadcast_select_fusion.refs_1_, ...), custom_call_target="tpu_custom_call" | custom-call | flops 134217728 | bytes 1048576 | tf_op jit(solution)/shard_map/pallas_call | solution.py:218
  76.6 0.2 collective-permute-done.11.got_ref
  76.8 1.1 %shard_map.59 = bf16[128,2048]{1,0:T(8,128)(2,1)} custom-call(f32[4,128,512]{2,1,0:T(8,128)S(1)} %get-tuple-element.29.acc_ref, f32[8,512]{1,0:T(8,128)S(1)} %get-tuple-element.30.stat_ref, bf16[544,512]{1,0:T(8,128)(2,1)S(1)} %collective-permute-done.11.got_ref), custom_call_target="tpu_custom_call" | custom-call | flops 1048576 | bytes 3145728 | tf_op jit(solution)/shard_map/pallas_call | solution.py:231
  (6 shorter events, 0.2 us)
Async XLA Ops:
  0.0 1.0 %copy-start.3 = (bf16[128,512]{1,0:T(8,128)(2,1)S(1)}, bf16[128,512]{1,0:T(8,128)(2,1)}, u32[]{:S(2)}) copy-start(bf16[128,512]{1,0:T(8,128)(2,1)} %param.7) | copy-start | bytes 393220
  1.0 22.6 %collective-permute-start.1 = (bf16[128,1024]{1,0:T(8,128)(2,1)S(1)}, bf16[128,1024]{1,0:T(8,128)(2,1)S(1)}, u32[]{:S(2)}, u32[]{:S(2)}) collective-permute-start(bf16[128,1024]{1,0:T(8,128)(2,1)S(1)} %constant_dynamic-update-slice_fusion.refs_2_), channel_id=1, source_target_pairs={{0,4},{1,5},{4,8},{5,9},{8,12},{9,13},{12,16},{13,17},{16,20},{17,... | collective-permute-start | bytes 786440 | tf_op jit(solution)/shard_map/ppermute | solution.py:58
  5.8 22.3 %collective-permute-start = (bf16[128,1024]{1,0:T(8,128)(2,1)S(1)}, bf16[128,1024]{1,0:T(8,128)(2,1)S(1)}, u32[]{:S(2)}, u32[]{:S(2)}) collective-permute-start(bf16[128,1024]{1,0:T(8,128)(2,1)S(1)} %constant_dynamic-update-slice_fusion.refs_2_), channel_id=1, source_target_pairs={{0,2},{1,3},{4,6},{5,7},{8,10},{9,11},{12,14},{13,15},{16,18},{17,... | collective-permute-start | bytes 786440 | tf_op jit(solution)/shard_map/ppermute | solution.py:58
  23.6 5.9 %collective-permute-start.3 = (bf16[128,1024]{1,0:T(8,128)(2,1)S(1)}, bf16[128,1024]{1,0:T(8,128)(2,1)S(1)}, u32[]{:S(2)}, u32[]{:S(2)}) collective-permute-start(bf16[128,1024]{1,0:T(8,128)(2,1)S(1)} %collective-permute-done.1.refs_4_), channel_id=1, source_target_pairs={{0,4},{1,5},{4,8},{5,9},{8,12},{9,13},{12,16},{13,17},{16,20},{17,... | collective-permute-start | bytes 786440 | tf_op jit(solution)/shard_map/ppermute | solution.py:58
  24.9 13.7 %collective-permute-start.5 = (bf16[128,2048]{1,0:T(8,128)(2,1)}, bf16[128,2048]{1,0:T(8,128)(2,1)S(1)}, u32[]{:S(2)}, u32[]{:S(2)}) collective-permute-start(bf16[128,2048]{1,0:T(8,128)(2,1)} %refs_0_.5), channel_id=1, source_target_pairs={{0,1},{1,0},{4,5},{5,4},{8,9},{9,8},{12,13},{13,12},{16,17},{17,16... | collective-permute-start | bytes 1572872 | tf_op jit(solution)/shard_map/ppermute | solution.py:58
  28.1 19.5 %collective-permute-start.2 = (bf16[256,1024]{1,0:T(8,128)(2,1)S(1)}, bf16[256,1024]{1,0:T(8,128)(2,1)S(1)}, u32[]{:S(2)}, u32[]{:S(2)}) collective-permute-start(bf16[256,1024]{1,0:T(8,128)(2,1)S(1)} %pad_maximum_fusion), channel_id=1, source_target_pairs={{28,32},{29,33},{60,64},{61,65},{92,96},{93,97},{124,130},{125,131... | collective-permute-start | bytes 1572872 | tf_op jit(solution)/shard_map/ppermute | solution.py:58
  29.5 7.8 %collective-permute-start.4 = (bf16[128,1024]{1,0:T(8,128)(2,1)S(1)}, bf16[128,1024]{1,0:T(8,128)(2,1)S(1)}, u32[]{:S(2)}, u32[]{:S(2)}) collective-permute-start(bf16[128,1024]{1,0:T(8,128)(2,1)S(1)} %collective-permute-done.refs_3_), channel_id=1, source_target_pairs={{0,4},{1,5},{4,8},{5,9},{8,12},{9,13},{12,16},{13,17},{16,20},{17,... | collective-permute-start | bytes 786440 | tf_op jit(solution)/shard_map/ppermute | solution.py:58
  33.7 4.9 %copy-start = (bf16[128,2048]{1,0:T(8,128)(2,1)S(1)}, bf16[128,2048]{1,0:T(8,128)(2,1)}, u32[]{:S(2)}) copy-start(bf16[128,2048]{1,0:T(8,128)(2,1)} %refs_0_.5) | copy-start | bytes 1572868
  33.7 4.9 %copy-start.1 = (s32[512]{0:T(512)S(1)}, s32[512]{0:T(512)}, u32[]{:S(2)}) copy-start(s32[512]{0:T(512)} %frame_ref.7) | copy-start | bytes 6148
  33.7 4.9 %copy-start.2 = (s32[512]{0:T(512)S(1)}, s32[512]{0:T(512)}, u32[]{:S(2)}) copy-start(s32[512]{0:T(512)} %count_ref.7) | copy-start | bytes 6148
  37.3 21.7 %collective-permute-start.8 = (bf16[256,1024]{1,0:T(8,128)(2,1)S(1)}, bf16[256,1024]{1,0:T(8,128)(2,1)S(1)}, u32[]{:S(2)}, u32[]{:S(2)}) collective-permute-start(bf16[256,1024]{1,0:T(8,128)(2,1)S(1)} %pad_maximum_fusion.1), channel_id=1, source_target_pairs={{28,32},{29,33},{60,64},{61,65},{92,96},{93,97},{124,130},{125,131... | collective-permute-start | bytes 1572872 | tf_op jit(solution)/shard_map/ppermute | solution.py:58
  47.7 4.6 %collective-permute-start.6 = (bf16[128,1024]{1,0:T(8,128)(2,1)S(1)}, bf16[128,1024]{1,0:T(8,128)(2,1)S(1)}, u32[]{:S(2)}, u32[]{:S(2)}) collective-permute-start(bf16[128,1024]{1,0:T(8,128)(2,1)S(1)} %get-tuple-element.22.refs_3_), channel_id=1, source_target_pairs={{0,4},{1,5},{4,8},{5,9},{8,12},{9,13},{12,16},{13,17},{16,20},{17,... | collective-permute-start | bytes 786440 | tf_op jit(solution)/shard_map/ppermute | solution.py:58
  49.0 11.4 %collective-permute-start.10 = (bf16[128,1024]{1,0:T(8,128)(2,1)S(1)}, bf16[128,1024]{1,0:T(8,128)(2,1)S(1)}, u32[]{:S(2)}, u32[]{:S(2)}) collective-permute-start(bf16[128,1024]{1,0:T(8,128)(2,1)S(1)} %get-tuple-element.33.refs_2_), channel_id=1, source_target_pairs={{0,4},{1,5},{4,8},{5,9},{8,12},{9,13},{12,16},{13,17},{16,20},{17,... | collective-permute-start | bytes 786440 | tf_op jit(solution)/shard_map/ppermute | solution.py:58
  52.3 12.5 %collective-permute-start.7 = (bf16[128,1024]{1,0:T(8,128)(2,1)S(1)}, bf16[128,1024]{1,0:T(8,128)(2,1)S(1)}, u32[]{:S(2)}, u32[]{:S(2)}) collective-permute-start(bf16[128,1024]{1,0:T(8,128)(2,1)S(1)} %collective-permute-done.6), channel_id=1, source_target_pairs={{28,32},{29,33},{60,64},{61,65},{92,96},{93,97},{124,130},{125,131... | collective-permute-start | bytes 786440 | tf_op jit(solution)/shard_map/ppermute | solution.py:58
  59.1 5.8 %collective-permute-start.9 = (bf16[128,1024]{1,0:T(8,128)(2,1)S(1)}, bf16[128,1024]{1,0:T(8,128)(2,1)S(1)}, u32[]{:S(2)}, u32[]{:S(2)}) collective-permute-start(bf16[128,1024]{1,0:T(8,128)(2,1)S(1)} %slice_select_fusion.1.refs_5_), channel_id=1, source_target_pairs={{0,4},{1,5},{4,8},{5,9},{8,12},{9,13},{12,16},{13,17},{16,20},{17,... | collective-permute-start | bytes 786440 | tf_op jit(solution)/shard_map/ppermute | solution.py:58
  66.2 10.6 %collective-permute-start.11 = (bf16[544,512]{1,0:T(8,128)(2,1)S(1)}, bf16[544,512]{1,0:T(8,128)(2,1)S(1)}, u32[]{:S(2)}, u32[]{:S(2)}) collective-permute-start(bf16[544,512]{1,0:T(8,128)(2,1)S(1)} %shard_map.58), channel_id=1, source_target_pairs={{0,1},{1,0},{4,5},{5,4},{8,9},{9,8},{12,13},{13,12},{16,17},{17,16... | collective-permute-start | bytes 1671176 | tf_op jit(solution)/shard_map/ppermute | solution.py:58

commit v6 on v5

--- a/solution.py
+++ b/solution.py
@@ -257,14 +257,16 @@
     in_cross1 = inside(after(cross0, in_near2))
     on_second = onward(jnp.concatenate([in_cross1, in_near2], axis=0))
     cross1, near2 = either(on_first[:rows], in_cross1), either(on_first[rows:], in_near2)
-    state = attend(((0, 0), (0, 1), (1, 0)), (0, 1), None, tables, both, (own, cross0, near1))
+    state = attend(((0, 0), (1, 0)), (0, 1), None, tables, both, (own, near1))
     in_cross2 = inside(after(cross1, state[1]))
     in_near3 = inside(near2)
     on_cross3 = onward(in_cross2)
     cross2 = either(on_second[:rows], in_cross2)
     in_cross3 = inside(cross2)
     near3 = either(after(on_second, cross2)[rows:], in_near3)
-    state = attend(((2, 0), (1, 1), (3, 0), (2, 1)), (0, 1), state, tables, both, (near2, cross1, near3, cross2))
+    state = attend(
+        ((0, 1), (2, 0), (1, 1), (3, 0), (2, 1)), (0, 1), state, tables, both, (cross0, near2, cross1, near3, cross2)
+    )
     cross3 = either(on_cross3, in_cross3)
     got = moved(attend(((3, 1),), (1,), state[2:], tables, both[1:], (cross3,), True), other_core)
     own_state = attend(((3, 1),), (0,), state[:2], tables, both[:1], (cross3,))

time: 78.3 us -> 78.3 us (level)
  transfers between devices with their start and end apart: 12 -> 12, of which waited for: 7 -> 6; matrix products, arithmetic and copies ran while one was open for 0% -> 0% of each run, Pallas kernels for 11% -> 11%
where the time goes in v6:
time: 78.3 us; the launch traced here: 77.9 us
  starting transfers between devices  37 us (47%)
  waiting for transfers between devices  28 us (36%)
  Pallas kernels  11.4 us (15%)
  local copies, waits for them, and re-layouts  0.98 us (1%)
    ppermute x12, starting transfers between devices, moved(): lax.ppermute(value, AXES, [(flat(p), flat(target(p))) for p in places() i...  37 us
    ppermute x12, waiting for transfers between devices, moved(): lax.ppermute(value, AXES, [(flat(p), flat(target(p))) for p in places() i...  28 us
    pallas_call x4, Pallas kernels, attend(): pl.pallas_call(functools.partial(attend_kernel, tags, sets, state is None...  10.3 us
  transfers between devices with their start and end apart: 12, of which 6 were waited for; matrix products, arithmetic and copies ran while one was open for 0% of the time, Pallas kernels for 11%

profile of v6, /device:TPU:1, one launch (start us, length us, event | category | flops | bytes accessed | tf_op | source)
XLA Modules:
  0.0 77.9 jit_solution(10591085347119641740)
XLA Ops:
  0.0 0.0 copy-start.3
  0.0 0.9 %constant_dynamic-update-slice_fusion.1 = bf16[128,1024]{1,0:T(8,128)(2,1)S(1)} fusion(bf16[128,512]{1,0:T(8,128)(2,1)} %param.6), kind=kLoop, calls=%fused_computation.8 | loop fusion | bytes 262144
  1.0 0.0 copy-done.3
  1.0 4.8 %collective-permute-start.1 = (bf16[128,1024]{1,0:T(8,128)(2,1)S(1)}, bf16[128,1024]{1,0:T(8,128)(2,1)S(1)}, u32[]{:S(2)}, u32[]{:S(2)}) collective-permute-start(bf16[128,1024]{1,0:T(8,128)(2,1)S(1)} %constant_dynamic-update-slice_fusion.refs_2_), channel_id=1, source_target_pairs={{0,4},{1,5},{4,8},{5,9},{8,12},{9,13},{12,16},{13,17},{16,20},{17,... | collective-permute-start | bytes 786440 | tf_op jit(solution)/shard_map/ppermute | solution.py:58
  5.8 7.5 %collective-permute-start = (bf16[128,1024]{1,0:T(8,128)(2,1)S(1)}, bf16[128,1024]{1,0:T(8,128)(2,1)S(1)}, u32[]{:S(2)}, u32[]{:S(2)}) collective-permute-start(bf16[128,1024]{1,0:T(8,128)(2,1)S(1)} %constant_dynamic-update-slice_fusion.refs_2_), channel_id=1, source_target_pairs={{0,2},{1,3},{4,6},{5,7},{8,10},{9,11},{12,14},{13,15},{16,18},{17,... | collective-permute-start | bytes 786440 | tf_op jit(solution)/shard_map/ppermute | solution.py:58
  13.3 10.3 %collective-permute-done.1.refs_3_ = bf16[128,1024]{1,0:T(8,128)(2,1)S(1)} collective-permute-done((bf16[128,1024]{1,0:T(8,128)(2,1)S(1)}, bf16[128,1024]{1,0:T(8,128)(2,1)S(1)}, u32[]{:S(2)}, u32[]{:S(2)}) %collective-permute-start.1) | collective-permute-done | bytes 262176 | tf_op jit(solution)/shard_map/ppermute | solution.py:58
  23.6 1.3 %collective-permute-start.3 = (bf16[128,1024]{1,0:T(8,128)(2,1)S(1)}, bf16[128,1024]{1,0:T(8,128)(2,1)S(1)}, u32[]{:S(2)}, u32[]{:S(2)}) collective-permute-start(bf16[128,1024]{1,0:T(8,128)(2,1)S(1)} %collective-permute-done.1.refs_3_), channel_id=1, source_target_pairs={{0,4},{1,5},{4,8},{5,9},{8,12},{9,13},{12,16},{13,17},{16,20},{17,... | collective-permute-start | bytes 786440 | tf_op jit(solution)/shard_map/ppermute | solution.py:58
  24.9 3.2 %collective-permute-start.5 = (bf16[128,2048]{1,0:T(8,128)(2,1)}, bf16[128,2048]{1,0:T(8,128)(2,1)S(1)}, u32[]{:S(2)}, u32[]{:S(2)}) collective-permute-start(bf16[128,2048]{1,0:T(8,128)(2,1)} %refs_0_.5), channel_id=1, source_target_pairs={{0,1},{1,0},{4,5},{5,4},{8,9},{9,8},{12,13},{13,12},{16,17},{17,16... | collective-permute-start | bytes 1572872 | tf_op jit(solution)/shard_map/ppermute | solution.py:58
  28.1 0.0 collective-permute-done.refs_2_
  28.1 1.3 %collective-permute-start.2 = (bf16[256,1024]{1,0:T(8,128)(2,1)S(1)}, bf16[256,1024]{1,0:T(8,128)(2,1)S(1)}, u32[]{:S(2)}, u32[]{:S(2)}) collective-permute-start(bf16[256,1024]{1,0:T(8,128)(2,1)S(1)} %pad_maximum_fusion), channel_id=1, source_target_pairs={{28,32},{29,33},{60,64},{61,65},{92,96},{93,97},{124,130},{125,131... | collective-permute-start | bytes 1572872 | tf_op jit(solution)/shard_map/ppermute | solution.py:58
  29.4 0.0 collective-permute-done.3
  29.5 4.1 %collective-permute-start.4 = (bf16[128,1024]{1,0:T(8,128)(2,1)S(1)}, bf16[128,1024]{1,0:T(8,128)(2,1)S(1)}, u32[]{:S(2)}, u32[]{:S(2)}) collective-permute-start(bf16[128,1024]{1,0:T(8,128)(2,1)S(1)} %collective-permute-done.refs_2_), channel_id=1, source_target_pairs={{0,4},{1,5},{4,8},{5,9},{8,12},{9,13},{12,16},{13,17},{16,20},{17,... | collective-permute-start | bytes 786440 | tf_op jit(solution)/shard_map/ppermute | solution.py:58
  33.6 0.1 pad_add_fusion.where_ref
  33.7 0.0 copy-start
  33.7 0.0 copy-start.1
  33.7 0.0 copy-start.2
  33.7 3.6 %collective-permute-done.4 = bf16[128,1024]{1,0:T(8,128)(2,1)S(1)} collective-permute-done((bf16[128,1024]{1,0:T(8,128)(2,1)S(1)}, bf16[128,1024]{1,0:T(8,128)(2,1)S(1)}, u32[]{:S(2)}, u32[]{:S(2)}) %collective-permute-start.4) | collective-permute-done | bytes 262176 | tf_op jit(solution)/shard_map/ppermute | solution.py:58
  37.3 1.3 %collective-permute-start.8 = (bf16[256,1024]{1,0:T(8,128)(2,1)S(1)}, bf16[256,1024]{1,0:T(8,128)(2,1)S(1)}, u32[]{:S(2)}, u32[]{:S(2)}) collective-permute-start(bf16[256,1024]{1,0:T(8,128)(2,1)S(1)} %pad_maximum_fusion.1), channel_id=1, source_target_pairs={{28,32},{29,33},{60,64},{61,65},{92,96},{93,97},{124,130},{125,131... | collective-permute-start | bytes 1572872 | tf_op jit(solution)/shard_map/ppermute | solution.py:58
  38.6 0.0 collective-permute-done.5.refs_1_.refs_0_
  38.6 0.0 copy-done
  38.6 0.0 copy-done.1
  38.6 0.0 copy-done.2
  38.6 2.6 %shard_map.55 = (f32[4,128,512]{2,1,0:T(8,128)S(1)}, f32[8,512]{1,0:T(8,128)S(1)}, f32[4,128,512]{2,1,0:T(8,128)S(1)}, f32[8,512]{1,0:T(8,128)S(1)}) custom-call(s32[2]{0:T(128)S(1)} %pad_add_fusion.where_ref, s32[512]{0:T(512)S(1)} %copy-done.1, s32[512]{0:T(512)S(1)} %copy-done.2, bf16[128,2048]{1,0:T(8,128)(2,1)S(1)} %copy-done, ...), custom_call_target="tpu_custom_call" | custom-call | flops 536870912 | bytes 1048576 | tf_op jit(solution)/shard_map/pallas_call | solution.py:218
  41.2 6.4 %collective-permute-done.2 = bf16[256,1024]{1,0:T(8,128)(2,1)S(1)} collective-permute-done((bf16[256,1024]{1,0:T(8,128)(2,1)S(1)}, bf16[256,1024]{1,0:T(8,128)(2,1)S(1)}, u32[]{:S(2)}, u32[]{:S(2)}) %collective-permute-start.2) | collective-permute-done | bytes 524320 | tf_op jit(solution)/shard_map/ppermute | solution.py:58
  47.6 0.1 slice_select_fusion
  47.7 1.3 %collective-permute-start.6 = (bf16[128,1024]{1,0:T(8,128)(2,1)S(1)}, bf16[128,1024]{1,0:T(8,128)(2,1)S(1)}, u32[]{:S(2)}, u32[]{:S(2)}) collective-permute-start(bf16[128,1024]{1,0:T(8,128)(2,1)S(1)} %get-tuple-element.22.refs_4_), channel_id=1, source_target_pairs={{0,4},{1,5},{4,8},{5,9},{8,12},{9,13},{12,16},{13,17},{16,20},{17,... | collective-permute-start | bytes 786440 | tf_op jit(solution)/shard_map/ppermute | solution.py:58
  49.0 1.3 %collective-permute-start.10 = (bf16[128,1024]{1,0:T(8,128)(2,1)S(1)}, bf16[128,1024]{1,0:T(8,128)(2,1)S(1)}, u32[]{:S(2)}, u32[]{:S(2)}) collective-permute-start(bf16[128,1024]{1,0:T(8,128)(2,1)S(1)} %get-tuple-element.33.refs_3_), channel_id=1, source_target_pairs={{0,4},{1,5},{4,8},{5,9},{8,12},{9,13},{12,16},{13,17},{16,20},{17,... | collective-permute-start | bytes 786440 | tf_op jit(solution)/shard_map/ppermute | solution.py:58
  50.3 2.0 %collective-permute-done.6 = bf16[128,1024]{1,0:T(8,128)(2,1)S(1)} collective-permute-done((bf16[128,1024]{1,0:T(8,128)(2,1)S(1)}, bf16[128,1024]{1,0:T(8,128)(2,1)S(1)}, u32[]{:S(2)}, u32[]{:S(2)}) %collective-permute-start.6) | collective-permute-done | bytes 262176 | tf_op jit(solution)/shard_map/ppermute | solution.py:58
  52.3 1.3 %collective-permute-start.7 = (bf16[128,1024]{1,0:T(8,128)(2,1)S(1)}, bf16[128,1024]{1,0:T(8,128)(2,1)S(1)}, u32[]{:S(2)}, u32[]{:S(2)}) collective-permute-start(bf16[128,1024]{1,0:T(8,128)(2,1)S(1)} %collective-permute-done.6), channel_id=1, source_target_pairs={{28,32},{29,33},{60,64},{61,65},{92,96},{93,97},{124,130},{125,131... | collective-permute-start | bytes 786440 | tf_op jit(solution)/shard_map/ppermute | solution.py:58
  53.6 5.4 %collective-permute-done.8 = bf16[256,1024]{1,0:T(8,128)(2,1)S(1)} collective-permute-done((bf16[256,1024]{1,0:T(8,128)(2,1)S(1)}, bf16[256,1024]{1,0:T(8,128)(2,1)S(1)}, u32[]{:S(2)}, u32[]{:S(2)}) %collective-permute-start.8) | collective-permute-done | bytes 524320 | tf_op jit(solution)/shard_map/ppermute | solution.py:58
  59.1 1.3 %collective-permute-start.9 = (bf16[128,1024]{1,0:T(8,128)(2,1)S(1)}, bf16[128,1024]{1,0:T(8,128)(2,1)S(1)}, u32[]{:S(2)}, u32[]{:S(2)}) collective-permute-start(bf16[128,1024]{1,0:T(8,128)(2,1)S(1)} %slice_select_fusion.1.refs_6_), channel_id=1, source_target_pairs={{0,4},{1,5},{4,8},{5,9},{8,12},{9,13},{12,16},{13,17},{16,20},{17,... | collective-permute-start | bytes 786440 | tf_op jit(solution)/shard_map/ppermute | solution.py:58
  60.4 0.0 collective-permute-done.10
  60.4 5.1 %shard_map.56 = (f32[4,128,512]{2,1,0:T(8,128)S(1)}, f32[8,512]{1,0:T(8,128)S(1)}, f32[4,128,512]{2,1,0:T(8,128)S(1)}, f32[8,512]{1,0:T(8,128)S(1)}) custom-call(s32[2]{0:T(128)S(1)} %pad_add_fusion.where_ref, s32[512]{0:T(512)S(1)} %copy-done.1, s32[512]{0:T(512)S(1)} %copy-done.2, bf16[128,2048]{1,0:T(8,128)(2,1)S(1)} %copy-done, ...), custom_call_target="tpu_custom_call" | custom-call | flops 1342177280 | bytes 1048576 | tf_op jit(solution)/shard_map/pallas_call | solution.py:218
  65.5 0.0 collective-permute-done.7
  65.5 0.0 collective-permute-done.9
  65.5 1.3 %shard_map.58 = bf16[544,512]{1,0:T(8,128)(2,1)S(1)} custom-call(s32[2]{0:T(128)S(1)} %pad_add_fusion.where_ref, s32[512]{0:T(512)S(1)} %copy-done.1, s32[512]{0:T(512)S(1)} %copy-done.2, bf16[128,2048]{1,0:T(8,128)(2,1)S(1)} %collective-permute-done.5.refs_1_.refs_0_, bf16[128,1024]{1,0:T(8,128)(2,1)S(1)} %broadcast_select_fusion.refs_1_, ...), custom_call_target="tpu_custom_call" | custom-call | flops 134217728 | bytes 1048576 | tf_op jit(solution)/shard_map/pallas_call | solution.py:218
  66.9 8.4 %collective-permute-start.11 = (bf16[544,512]{1,0:T(8,128)(2,1)S(1)}, bf16[544,512]{1,0:T(8,128)(2,1)S(1)}, u32[]{:S(2)}, u32[]{:S(2)}) collective-permute-start(bf16[544,512]{1,0:T(8,128)(2,1)S(1)} %shard_map.58), channel_id=1, source_target_pairs={{0,1},{1,0},{4,5},{5,4},{8,9},{9,8},{12,13},{13,12},{16,17},{17,16... | collective-permute-start | bytes 1671176 | tf_op jit(solution)/shard_map/ppermute | solution.py:58
  75.3 1.3 %shard_map.57 = (f32[4,128,512]{2,1,0:T(8,128)S(1)}, f32[8,512]{1,0:T(8,128)S(1)}) custom-call(s32[2]{0:T(128)S(1)} %pad_add_fusion.where_ref, s32[512]{0:T(512)S(1)} %copy-done.1, s32[512]{0:T(512)S(1)} %copy-done.2, bf16[128,2048]{1,0:T(8,128)(2,1)S(1)} %copy-done, bf16[128,1024]{1,0:T(8,128)(2,1)S(1)} %broadcast_select_fusion.refs_1_, ...), custom_call_target="tpu_custom_call" | custom-call | flops 134217728 | bytes 1048576 | tf_op jit(solution)/shard_map/pallas_call | solution.py:218
  76.6 0.2 collective-permute-done.11.got_ref
  76.8 1.1 %shard_map.59 = bf16[128,2048]{1,0:T(8,128)(2,1)} custom-call(f32[4,128,512]{2,1,0:T(8,128)S(1)} %get-tuple-element.29.acc_ref, f32[8,512]{1,0:T(8,128)S(1)} %get-tuple-element.30.stat_ref, bf16[544,512]{1,0:T(8,128)(2,1)S(1)} %collective-permute-done.11.got_ref), custom_call_target="tpu_custom_call" | custom-call | flops 1048576 | bytes 3145728 | tf_op jit(solution)/shard_map/pallas_call | solution.py:231
  (6 shorter events, 0.2 us)
Async XLA Ops:
  0.0 1.0 %copy-start.3 = (bf16[128,512]{1,0:T(8,128)(2,1)S(1)}, bf16[128,512]{1,0:T(8,128)(2,1)}, u32[]{:S(2)}) copy-start(bf16[128,512]{1,0:T(8,128)(2,1)} %param.7) | copy-start | bytes 393220
  1.0 22.6 %collective-permute-start.1 = (bf16[128,1024]{1,0:T(8,128)(2,1)S(1)}, bf16[128,1024]{1,0:T(8,128)(2,1)S(1)}, u32[]{:S(2)}, u32[]{:S(2)}) collective-permute-start(bf16[128,1024]{1,0:T(8,128)(2,1)S(1)} %constant_dynamic-update-slice_fusion.refs_2_), channel_id=1, source_target_pairs={{0,4},{1,5},{4,8},{5,9},{8,12},{9,13},{12,16},{13,17},{16,20},{17,... | collective-permute-start | bytes 786440 | tf_op jit(solution)/shard_map/ppermute | solution.py:58
  5.8 22.3 %collective-permute-start = (bf16[128,1024]{1,0:T(8,128)(2,1)S(1)}, bf16[128,1024]{1,0:T(8,128)(2,1)S(1)}, u32[]{:S(2)}, u32[]{:S(2)}) collective-permute-start(bf16[128,1024]{1,0:T(8,128)(2,1)S(1)} %constant_dynamic-update-slice_fusion.refs_2_), channel_id=1, source_target_pairs={{0,2},{1,3},{4,6},{5,7},{8,10},{9,11},{12,14},{13,15},{16,18},{17,... | collective-permute-start | bytes 786440 | tf_op jit(solution)/shard_map/ppermute | solution.py:58
  23.6 5.9 %collective-permute-start.3 = (bf16[128,1024]{1,0:T(8,128)(2,1)S(1)}, bf16[128,1024]{1,0:T(8,128)(2,1)S(1)}, u32[]{:S(2)}, u32[]{:S(2)}) collective-permute-start(bf16[128,1024]{1,0:T(8,128)(2,1)S(1)} %collective-permute-done.1.refs_3_), channel_id=1, source_target_pairs={{0,4},{1,5},{4,8},{5,9},{8,12},{9,13},{12,16},{13,17},{16,20},{17,... | collective-permute-start | bytes 786440 | tf_op jit(solution)/shard_map/ppermute | solution.py:58
  24.9 13.7 %collective-permute-start.5 = (bf16[128,2048]{1,0:T(8,128)(2,1)}, bf16[128,2048]{1,0:T(8,128)(2,1)S(1)}, u32[]{:S(2)}, u32[]{:S(2)}) collective-permute-start(bf16[128,2048]{1,0:T(8,128)(2,1)} %refs_0_.5), channel_id=1, source_target_pairs={{0,1},{1,0},{4,5},{5,4},{8,9},{9,8},{12,13},{13,12},{16,17},{17,16... | collective-permute-start | bytes 1572872 | tf_op jit(solution)/shard_map/ppermute | solution.py:58
  28.1 19.5 %collective-permute-start.2 = (bf16[256,1024]{1,0:T(8,128)(2,1)S(1)}, bf16[256,1024]{1,0:T(8,128)(2,1)S(1)}, u32[]{:S(2)}, u32[]{:S(2)}) collective-permute-start(bf16[256,1024]{1,0:T(8,128)(2,1)S(1)} %pad_maximum_fusion), channel_id=1, source_target_pairs={{28,32},{29,33},{60,64},{61,65},{92,96},{93,97},{124,130},{125,131... | collective-permute-start | bytes 1572872 | tf_op jit(solution)/shard_map/ppermute | solution.py:58
  29.5 7.8 %collective-permute-start.4 = (bf16[128,1024]{1,0:T(8,128)(2,1)S(1)}, bf16[128,1024]{1,0:T(8,128)(2,1)S(1)}, u32[]{:S(2)}, u32[]{:S(2)}) collective-permute-start(bf16[128,1024]{1,0:T(8,128)(2,1)S(1)} %collective-permute-done.refs_2_), channel_id=1, source_target_pairs={{0,4},{1,5},{4,8},{5,9},{8,12},{9,13},{12,16},{13,17},{16,20},{17,... | collective-permute-start | bytes 786440 | tf_op jit(solution)/shard_map/ppermute | solution.py:58
  33.7 4.9 %copy-start = (bf16[128,2048]{1,0:T(8,128)(2,1)S(1)}, bf16[128,2048]{1,0:T(8,128)(2,1)}, u32[]{:S(2)}) copy-start(bf16[128,2048]{1,0:T(8,128)(2,1)} %refs_0_.5) | copy-start | bytes 1572868
  33.7 4.9 %copy-start.1 = (s32[512]{0:T(512)S(1)}, s32[512]{0:T(512)}, u32[]{:S(2)}) copy-start(s32[512]{0:T(512)} %frame_ref.7) | copy-start | bytes 6148
  33.7 4.9 %copy-start.2 = (s32[512]{0:T(512)S(1)}, s32[512]{0:T(512)}, u32[]{:S(2)}) copy-start(s32[512]{0:T(512)} %count_ref.7) | copy-start | bytes 6148
  37.3 21.7 %collective-permute-start.8 = (bf16[256,1024]{1,0:T(8,128)(2,1)S(1)}, bf16[256,1024]{1,0:T(8,128)(2,1)S(1)}, u32[]{:S(2)}, u32[]{:S(2)}) collective-permute-start(bf16[256,1024]{1,0:T(8,128)(2,1)S(1)} %pad_maximum_fusion.1), channel_id=1, source_target_pairs={{28,32},{29,33},{60,64},{61,65},{92,96},{93,97},{124,130},{125,131... | collective-permute-start | bytes 1572872 | tf_op jit(solution)/shard_map/ppermute | solution.py:58
  47.7 4.6 %collective-permute-start.6 = (bf16[128,1024]{1,0:T(8,128)(2,1)S(1)}, bf16[128,1024]{1,0:T(8,128)(2,1)S(1)}, u32[]{:S(2)}, u32[]{:S(2)}) collective-permute-start(bf16[128,1024]{1,0:T(8,128)(2,1)S(1)} %get-tuple-element.22.refs_4_), channel_id=1, source_target_pairs={{0,4},{1,5},{4,8},{5,9},{8,12},{9,13},{12,16},{13,17},{16,20},{17,... | collective-permute-start | bytes 786440 | tf_op jit(solution)/shard_map/ppermute | solution.py:58
  49.0 11.4 %collective-permute-start.10 = (bf16[128,1024]{1,0:T(8,128)(2,1)S(1)}, bf16[128,1024]{1,0:T(8,128)(2,1)S(1)}, u32[]{:S(2)}, u32[]{:S(2)}) collective-permute-start(bf16[128,1024]{1,0:T(8,128)(2,1)S(1)} %get-tuple-element.33.refs_3_), channel_id=1, source_target_pairs={{0,4},{1,5},{4,8},{5,9},{8,12},{9,13},{12,16},{13,17},{16,20},{17,... | collective-permute-start | bytes 786440 | tf_op jit(solution)/shard_map/ppermute | solution.py:58
  52.3 13.2 %collective-permute-start.7 = (bf16[128,1024]{1,0:T(8,128)(2,1)S(1)}, bf16[128,1024]{1,0:T(8,128)(2,1)S(1)}, u32[]{:S(2)}, u32[]{:S(2)}) collective-permute-start(bf16[128,1024]{1,0:T(8,128)(2,1)S(1)} %collective-permute-done.6), channel_id=1, source_target_pairs={{28,32},{29,33},{60,64},{61,65},{92,96},{93,97},{124,130},{125,131... | collective-permute-start | bytes 786440 | tf_op jit(solution)/shard_map/ppermute | solution.py:58
  59.1 6.4 %collective-permute-start.9 = (bf16[128,1024]{1,0:T(8,128)(2,1)S(1)}, bf16[128,1024]{1,0:T(8,128)(2,1)S(1)}, u32[]{:S(2)}, u32[]{:S(2)}) collective-permute-start(bf16[128,1024]{1,0:T(8,128)(2,1)S(1)} %slice_select_fusion.1.refs_6_), channel_id=1, source_target_pairs={{0,4},{1,5},{4,8},{5,9},{8,12},{9,13},{12,16},{13,17},{16,20},{17,... | collective-permute-start | bytes 786440 | tf_op jit(solution)/shard_map/ppermute | solution.py:58
  66.9 10.0 %collective-permute-start.11 = (bf16[544,512]{1,0:T(8,128)(2,1)S(1)}, bf16[544,512]{1,0:T(8,128)(2,1)S(1)}, u32[]{:S(2)}, u32[]{:S(2)}) collective-permute-start(bf16[544,512]{1,0:T(8,128)(2,1)S(1)} %shard_map.58), channel_id=1, source_target_pairs={{0,1},{1,0},{4,5},{5,4},{8,9},{9,8},{12,13},{13,12},{16,17},{17,16... | collective-permute-start | bytes 1671176 | tf_op jit(solution)/shard_map/ppermute | solution.py:58
